TPU v7x, 32 devices: a whole 2x2x4 slice. The times are simulated.
32 devices in a mesh: grp: 4 (over y, x), dev: 8 (over z, core).
Axes of the slice: x: 2, y: 2, z: 4, core: 2. Of those that a mesh axis runs over, the one named last changes fastest.
Arguments:
- embedded: bfloat16 [32, 320, 768], P(('grp', 'dev')), may hold values from -6 to 6
- mask_order: int32 [32, 256], P(('grp', 'dev')), may hold values from 0 to 255, each once within a row
- counts: int32 [32], P(('grp', 'dev')), may hold values from 180 to 256, as said below
- targets: float32 [32, 256, 16], P(('grp', 'dev')), may hold values from -6 to 6
- noise_copies: bfloat16 [32, 256, 4, 16], P(('grp', 'dev')), may hold values from -6 to 6
- timesteps: int32 [32, 256, 4], P(('grp', 'dev')), may hold values from 0 to 999
- enc_gain_one: bfloat16 [768], P('dev'), may hold values from 0.5 to 1.5
- enc_qkv: bfloat16 [768, 2304], P('dev'), may hold values from -0.21875 to 0.21875
- enc_proj: bfloat16 [768, 768], P('dev'), may hold values from -0.875 to 0.875
- enc_gain_two: bfloat16 [768], P('dev'), may hold values from 0.5 to 1.5
- enc_up: bfloat16 [768, 3072], P('dev'), may hold values from -0.21875 to 0.21875
- enc_down: bfloat16 [3072, 768], P('dev'), may hold values from -0.109375 to 0.109375
- dec_gain_one: bfloat16 [768], P('dev'), may hold values from 0.5 to 1.5
- dec_qkv: bfloat16 [768, 2304], P('dev'), may hold values from -0.21875 to 0.21875
- dec_proj: bfloat16 [768, 768], P('dev'), may hold values from -0.875 to 0.875
- dec_gain_two: bfloat16 [768], P('dev'), may hold values from 0.5 to 1.5
- dec_up: bfloat16 [768, 3072], P('dev'), may hold values from -0.21875 to 0.21875
- dec_down: bfloat16 [3072, 768], P('dev'), may hold values from -0.109375 to 0.109375
- mask_token: bfloat16 [768], P('dev'), may hold values from -6 to 6
- head_in: bfloat16 [16, 1024], P(None, 'dev'), may hold values from -1.5 to 1.5
- head_cond: bfloat16 [768, 1024], P('dev'), may hold values from -0.21875 to 0.21875
- head_ada: bfloat16 [1024, 3072], P('dev'), may hold values from -0.1875 to 0.1875
- head_inner: bfloat16 [1024, 1024], P('dev'), may hold values from -0.1875 to 0.1875
- head_outer: bfloat16 [1024, 1024], P('dev'), may hold values from -0.1875 to 0.1875
- head_out: bfloat16 [1024, 16], P('dev'), may hold values from -0.1875 to 0.1875
Outputs:
- image_loss: float32 [32], P(('grp', 'dev'))
- activations: bfloat16 [32, 320, 768], P(('grp', 'dev'))
- embed_grad: float32 [32, 320, 768], P(('grp', 'dev'))
- enc_gain_one_grad: float32 [768], P('dev')
- enc_qkv_grad: float32 [768, 2304], P('dev')
- enc_proj_grad: float32 [768, 768], P('dev')
- enc_gain_two_grad: float32 [768], P('dev')
- enc_up_grad: float32 [768, 3072], P('dev')
- enc_down_grad: float32 [3072, 768], P('dev')
- dec_gain_one_grad: float32 [768], P('dev')
- dec_qkv_grad: float32 [768, 2304], P('dev')
- dec_proj_grad: float32 [768, 768], P('dev')
- dec_gain_two_grad: float32 [768], P('dev')
- dec_up_grad: float32 [768, 3072], P('dev')
- dec_down_grad: float32 [3072, 768], P('dev')
- mask_token_grad: float32 [768], P('dev')
- head_in_grad: float32 [16, 1024], P(None, 'dev')
- head_cond_grad: float32 [768, 1024], P('dev')
- head_ada_grad: float32 [1024, 3072], P('dev')
- head_inner_grad: float32 [1024, 1024], P('dev')
- head_outer_grad: float32 [1024, 1024], P('dev')
- head_out_grad: float32 [1024, 16], P('dev')
Inputs may be any that keep to these rules, and one draw needn't show every extreme that they name: `mask_order`: each row is a permutation of the token positions; the first counts entries of a row are that image's masked tokens. The masked counts of each aligned group of 8 images (the images of one index of grp) sum to exactly 1664; in every group one image has all 256 tokens masked and one has exactly 180.
All inputs are finite; a program needn't handle non-finite values.
Results may differ from a plain program's by a relative error of at most 0.02.
Values may be sent and summed in bfloat16 or wider, within the bound.
A program may use at most 320 MiB of HBM per device.

v0:
```python
import math

import jax
import jax.numpy as jnp
from jax import lax
from jax.sharding import PartitionSpec as P

HEADS = 12
HW = 1024
CH = 16
COPIES = 4
STEPS_T = 1000
ENC = 140
SPAN = 208


EPSILON = 1e-06
NEG_FILL = -1e30


def entering(value, axis, join, neutral):
    count, mine = (lax.axis_size(axis), lax.axis_index(axis))
    pieces = lax.all_gather(value, axis)
    so_far = jnp.full_like(value, 0) + jnp.asarray(neutral, value.dtype)

    def turn(position, so_far):
        longer = join(so_far, pieces[position])
        return jnp.where(position < mine, longer, so_far)

    return lax.fori_loop(0, count - 1, turn, so_far)


def matmul(left, right):
    return jnp.dot(left, right, preferred_element_type=jnp.float32)


def left_trans(left, right):
    return lax.dot_general(
        left, right, (((0,), (0,)), ((), ())), preferred_element_type=jnp.float32
    )


def right_trans(left, right):
    return lax.dot_general(
        left, right, (((1,), (1,)), ((), ())), preferred_element_type=jnp.float32
    )


def norm_rows(values):
    centre = values - jnp.mean(values, axis=-1, keepdims=True)
    inv_std = lax.rsqrt(jnp.mean(centre * centre, axis=-1, keepdims=True) + EPSILON)
    return (centre * inv_std, inv_std)


def norm_back(grad, normed, inv_std):
    mean_grad = jnp.mean(grad, axis=-1, keepdims=True)
    mean_cross = jnp.mean(grad * normed, axis=-1, keepdims=True)
    return inv_std * (grad - mean_grad - normed * mean_cross)


def silu_slope(values):
    sigma = jax.nn.sigmoid(values)
    return sigma * (1.0 + values * (1.0 - sigma))


def gelu_slope(values):
    cumul = 0.5 * (1.0 + lax.erf(values * (1.0 / math.sqrt(2.0))))
    density = jnp.exp(-0.5 * values * values) * (1.0 / math.sqrt(2.0 * math.pi))
    return cumul + values * density


def time_embed(steps):
    half_width = HW // 2
    freqs = jnp.exp(-math.log(10000.0) * jnp.arange(half_width, dtype=jnp.float32) / half_width)
    phase = steps.astype(jnp.float32)[..., None] * freqs
    return jnp.concatenate([jnp.cos(phase), jnp.sin(phase)], axis=-1)


def noise_angle(steps):
    return (steps.astype(jnp.float32) / STEPS_T + 0.008) / 1.008 * (math.pi / 2)


def pick_rows(table, index):
    return table[index]


def place_rows(base, index, values):
    return base.at[index].set(values, mode="drop")


def inverse_order(order_row):
    return (
        jnp.zeros(order_row.shape, jnp.int32)
        .at[order_row]
        .set(jnp.arange(order_row.shape[0], dtype=jnp.int32))
    )


def add_counts(earlier, later):
    return earlier + later


def attention_scores(qkv_proj, key_valid, head_size):
    raw_scores = jnp.einsum(
        "iqhd,ikhd->ihqk", qkv_proj[:, :, 0], qkv_proj[:, :, 1], preferred_element_type=jnp.float32
    )
    return jnp.where(key_valid[:, None, None, :], raw_scores * head_size ** (-0.5), NEG_FILL)


def block_forward(stream, key_valid, weights):
    gain_one, w_qkv, w_proj, gain_two, w_up, w_down = weights
    images, row_count, width = stream.shape
    head_size = width // HEADS
    flat = stream.reshape(images * row_count, width)
    normed_one, inv_one = norm_rows(flat)
    ln_one = (normed_one * gain_one.astype(jnp.float32)).astype(jnp.bfloat16)
    qkv_proj = (
        matmul(ln_one, w_qkv).astype(jnp.bfloat16).reshape(images, row_count, 3, HEADS, head_size)
    )
    scores = attention_scores(qkv_proj, key_valid, head_size)
    top_score = jnp.max(scores, axis=-1, keepdims=True)
    exp_scores = jnp.exp(scores - top_score)
    exp_total = jnp.sum(exp_scores, axis=-1, keepdims=True)
    log_total = top_score + jnp.log(exp_total)
    attn_probs = (exp_scores / exp_total).astype(jnp.bfloat16)
    mixed = jnp.einsum(
        "ihqk,ikhd->iqhd", attn_probs, qkv_proj[:, :, 2], preferred_element_type=jnp.float32
    )
    mixed = mixed.astype(jnp.bfloat16).reshape(images * row_count, width)
    middle = flat + matmul(mixed, w_proj)
    normed_two, inv_two = norm_rows(middle)
    ln_two = (normed_two * gain_two.astype(jnp.float32)).astype(jnp.bfloat16)
    up_proj = matmul(ln_two, w_up)
    up_act = jax.nn.gelu(up_proj, approximate=False).astype(jnp.bfloat16)
    result = middle + matmul(up_act, w_down)
    kept = (
        normed_one,
        inv_one,
        ln_one,
        qkv_proj,
        log_total,
        mixed,
        normed_two,
        inv_two,
        ln_two,
        up_proj,
        up_act,
    )
    return (result.reshape(images, row_count, width), kept)


def block_backward(grad_out, key_valid, weights, kept):
    gain_one, w_qkv, w_proj, gain_two, w_up, w_down = weights
    (
        normed_one,
        inv_one,
        ln_one,
        qkv_proj,
        log_total,
        mixed,
        normed_two,
        inv_two,
        ln_two,
        up_proj,
        up_act,
    ) = kept
    images, row_count, width = grad_out.shape
    head_size = width // HEADS
    grad_flat = grad_out.reshape(images * row_count, width)
    grad_low = grad_flat.astype(jnp.bfloat16)
    grad_w_down = left_trans(up_act, grad_low)
    grad_act = right_trans(grad_low, w_down)
    grad_up = (grad_act * gelu_slope(up_proj)).astype(jnp.bfloat16)
    grad_w_up = left_trans(ln_two, grad_up)
    grad_ln_two = right_trans(grad_up, w_up)
    grad_gain_two = jnp.sum(grad_ln_two * normed_two, axis=0)
    grad_mid = grad_flat + norm_back(
        grad_ln_two * gain_two.astype(jnp.float32), normed_two, inv_two
    )
    grad_mid_low = grad_mid.astype(jnp.bfloat16)
    grad_w_proj = left_trans(mixed, grad_mid_low)
    grad_mixed = (
        right_trans(grad_mid_low, w_proj)
        .astype(jnp.bfloat16)
        .reshape(images, row_count, HEADS, head_size)
    )
    scores = attention_scores(qkv_proj, key_valid, head_size)
    attn_probs = jnp.exp(scores - log_total)
    grad_probs = jnp.einsum(
        "iqhd,ikhd->ihqk", grad_mixed, qkv_proj[:, :, 2], preferred_element_type=jnp.float32
    )
    row_dot = jnp.sum(grad_probs * attn_probs, axis=-1, keepdims=True)
    grad_scores = (attn_probs * (grad_probs - row_dot) * head_size ** (-0.5)).astype(jnp.bfloat16)
    grad_query = jnp.einsum(
        "ihqk,ikhd->iqhd", grad_scores, qkv_proj[:, :, 1], preferred_element_type=jnp.float32
    )
    grad_key = jnp.einsum(
        "ihqk,iqhd->ikhd", grad_scores, qkv_proj[:, :, 0], preferred_element_type=jnp.float32
    )
    grad_value = jnp.einsum(
        "ihqk,iqhd->ikhd",
        attn_probs.astype(jnp.bfloat16),
        grad_mixed,
        preferred_element_type=jnp.float32,
    )
    grad_qkv = jnp.stack([grad_query, grad_key, grad_value], axis=2)
    grad_qkv = grad_qkv.reshape(images * row_count, 3 * width).astype(jnp.bfloat16)
    grad_w_qkv = left_trans(ln_one, grad_qkv)
    grad_ln_one = right_trans(grad_qkv, w_qkv)
    grad_gain_one = jnp.sum(grad_ln_one * normed_one, axis=0)
    grad_in = grad_mid + norm_back(grad_ln_one * gain_one.astype(jnp.float32), normed_one, inv_one)
    grads = (grad_gain_one, grad_w_qkv, grad_w_proj, grad_gain_two, grad_w_up, grad_w_down)
    return (grad_in.reshape(images, row_count, width), grads)


def head_step(cond_rows, signal, steps, weights):
    w_in, w_cond, w_ada, w_inner, w_outer, w_out = weights
    row_count = cond_rows.shape[0]
    flat_count = row_count * COPIES
    noisy = signal[:, : COPIES * CH].reshape(flat_count, CH)
    noise_vals = signal[:, COPIES * CH :].astype(jnp.float32).reshape(flat_count, CH)
    cond = matmul(cond_rows, w_cond)
    cond_full = (cond[:, None, :] + time_embed(steps)).reshape(flat_count, HW)
    cond_act = jax.nn.silu(cond_full).astype(jnp.bfloat16)
    modulate = matmul(cond_act, w_ada)
    shift_part = modulate[:, :HW]
    scale_part = modulate[:, HW : 2 * HW]
    gate_part = modulate[:, 2 * HW :]
    hidden = matmul(noisy, w_in)
    normed_in, inv_in = norm_rows(hidden)
    mlp_in = (normed_in * (1.0 + scale_part) + shift_part).astype(jnp.bfloat16)
    inner = matmul(mlp_in, w_inner)
    inner_act = jax.nn.silu(inner).astype(jnp.bfloat16)
    branch = matmul(inner_act, w_outer)
    hidden_two = hidden + gate_part * branch
    normed_out, inv_out = norm_rows(hidden_two)
    final_in = normed_out.astype(jnp.bfloat16)
    error = matmul(final_in, w_out) - noise_vals
    row_loss = jnp.sum((error * error).reshape(row_count, COPIES * CH), axis=1).astype(jnp.bfloat16)
    grad_pred = (error * (2.0 / COPIES)).astype(jnp.bfloat16)
    grad_w_out = left_trans(final_in, grad_pred)
    grad_two = norm_back(right_trans(grad_pred, w_out), normed_out, inv_out)
    grad_branch = (grad_two * gate_part).astype(jnp.bfloat16)
    grad_gate = grad_two * branch
    grad_w_outer = left_trans(inner_act, grad_branch)
    grad_inner = (right_trans(grad_branch, w_outer) * silu_slope(inner)).astype(jnp.bfloat16)
    grad_w_inner = left_trans(mlp_in, grad_inner)
    grad_mlp_in = right_trans(grad_inner, w_inner)
    grad_hidden = (
        grad_two + norm_back(grad_mlp_in * (1.0 + scale_part), normed_in, inv_in)
    ).astype(jnp.bfloat16)
    grad_w_in = left_trans(noisy, grad_hidden)
    grad_mod = jnp.concatenate([grad_mlp_in, grad_mlp_in * normed_in, grad_gate], axis=1).astype(
        jnp.bfloat16
    )
    grad_w_ada = left_trans(cond_act, grad_mod)
    grad_cond_full = right_trans(grad_mod, w_ada) * silu_slope(cond_full)
    grad_cond = jnp.sum(grad_cond_full.reshape(row_count, COPIES, HW), axis=1).astype(jnp.bfloat16)
    grad_w_cond = left_trans(cond_rows, grad_cond)
    grad_rows = right_trans(grad_cond, w_cond).astype(jnp.bfloat16)
    grads = (grad_w_in, grad_w_cond, grad_w_ada, grad_w_inner, grad_w_outer, grad_w_out)
    return (grads, grad_rows, row_loss)


def per_device(
    embedded,
    mask_order,
    counts,
    targets,
    noise_copies,
    timesteps,
    enc_gain_one,
    enc_qkv,
    enc_proj,
    enc_gain_two,
    enc_up,
    enc_down,
    dec_gain_one,
    dec_qkv,
    dec_proj,
    dec_gain_two,
    dec_up,
    dec_down,
    mask_token,
    head_in,
    head_cond,
    head_ada,
    head_inner,
    head_outer,
    head_out,
):
    images, tokens, width = embedded.shape
    seq_len = mask_order.shape[1]
    buffer = tokens - seq_len
    visible_max = ENC - buffer
    lanes = lax.axis_size("dev")
    all_rows = images * seq_len
    slots = all_rows // lanes
    dev_count = jnp.sum(counts)
    start_row = entering(dev_count, "dev", add_counts, jnp.zeros((), jnp.int32))
    enc_weights = (
        lax.all_gather(enc_gain_one, "dev", axis=0, tiled=True),
        lax.all_gather(enc_qkv, "dev", axis=0, tiled=True),
        lax.all_gather(enc_proj, "dev", axis=0, tiled=True),
        lax.all_gather(enc_gain_two, "dev", axis=0, tiled=True),
        lax.all_gather(enc_up, "dev", axis=0, tiled=True),
        lax.all_gather(enc_down, "dev", axis=0, tiled=True),
    )
    spots = jnp.arange(visible_max, dtype=jnp.int32)
    spot_src = jnp.minimum(counts[:, None] + spots[None, :], seq_len - 1)
    vis_tokens = jnp.take_along_axis(mask_order, spot_src, axis=1)
    spot_live = spots[None, :] < (seq_len - counts)[:, None]
    buffer_rows = jnp.arange(buffer, dtype=jnp.int32)[None, :]
    enc_rows = jnp.concatenate([buffer_rows, buffer + vis_tokens], axis=1)
    enc_in = jax.vmap(pick_rows)(embedded, enc_rows).astype(jnp.float32)
    enc_valid = jnp.concatenate([jnp.ones((images, buffer), bool), spot_live], axis=1)
    enc_out, enc_kept = block_forward(enc_in, enc_valid, enc_weights)
    dec_all = (
        lax.all_gather(dec_gain_one, "dev", axis=0, tiled=True),
        lax.all_gather(dec_qkv, "dev", axis=0, tiled=True),
        lax.all_gather(dec_proj, "dev", axis=0, tiled=True),
        lax.all_gather(dec_gain_two, "dev", axis=0, tiled=True),
        lax.all_gather(dec_up, "dev", axis=0, tiled=True),
        lax.all_gather(dec_down, "dev", axis=0, tiled=True),
        lax.all_gather(mask_token, "dev", axis=0, tiled=True),
    )
    dec_weights = dec_all[:6]
    token_fill = dec_all[6].astype(jnp.float32)
    rank = jax.vmap(inverse_order)(mask_order)
    visible = rank >= counts[:, None]
    enc_source = buffer + jnp.clip(rank - counts[:, None], 0, visible_max - 1)
    tok_rows = jnp.where(
        visible[..., None], jax.vmap(pick_rows)(enc_out, enc_source), token_fill[None, None, :]
    )
    dec_in = jnp.concatenate([enc_out[:, :buffer], tok_rows], axis=1)
    dec_valid = jnp.ones((images, tokens), bool)
    dec_out, dec_kept = block_forward(dec_in, dec_valid, dec_weights)
    activations = dec_out.astype(jnp.bfloat16)
    list_pos = jnp.arange(all_rows, dtype=jnp.int32)
    image_ends = jnp.cumsum(counts)
    image_of = jnp.minimum(
        jnp.sum((list_pos[:, None] >= image_ends[None, :]).astype(jnp.int32), axis=1), images - 1
    )
    within = jnp.clip(list_pos - (image_ends - counts)[image_of], 0, seq_len - 1)
    list_live = list_pos < dev_count
    token_pos = mask_order[image_of, within]
    source_row = image_of * tokens + buffer + token_pos
    cond_list = activations.reshape(images * tokens, width)[source_row]
    step_list = timesteps[image_of, token_pos]
    noise_list = noise_copies[image_of, token_pos]
    angle = noise_angle(step_list)
    noisy = jnp.cos(angle)[..., None] * targets[image_of, token_pos][:, None, :] + jnp.sin(angle)[
        ..., None
    ] * noise_list.astype(jnp.float32)
    signal = jnp.concatenate(
        [
            noisy.astype(jnp.bfloat16).reshape(all_rows, COPIES * CH),
            noise_list.reshape(all_rows, COPIES * CH),
        ],
        axis=1,
    )
    target_slot = jnp.where(list_live, (start_row + list_pos) // lanes, SPAN).astype(jnp.int32)
    turn = start_row % lanes

    def spread(values):
        return jnp.roll(values.reshape((slots, lanes) + values.shape[1:]), turn, axis=1)

    def gather_back(values):
        return jnp.roll(values, -turn, axis=1).reshape((all_rows,) + values.shape[2:])

    got_cond, got_signal = (
        lax.all_to_all(spread(cond_list), "dev", split_axis=1, concat_axis=1, tiled=True),
        lax.all_to_all(spread(signal), "dev", split_axis=1, concat_axis=1, tiled=True),
    )
    got_steps, got_slot = (
        lax.all_to_all(spread(step_list), "dev", split_axis=1, concat_axis=1, tiled=True),
        lax.all_to_all(spread(target_slot), "dev", split_axis=1, concat_axis=1, tiled=True),
    )
    head_weights = (
        lax.all_gather(head_in, "dev", axis=1, tiled=True),
        lax.all_gather(head_cond, "dev", axis=0, tiled=True),
        lax.all_gather(head_ada, "dev", axis=0, tiled=True),
        lax.all_gather(head_inner, "dev", axis=0, tiled=True),
        lax.all_gather(head_outer, "dev", axis=0, tiled=True),
        lax.all_gather(head_out, "dev", axis=0, tiled=True),
    )
    flat_slot = got_slot.reshape(slots * lanes)

    def compact(values):
        rest = values.shape[2:]
        return (
            jnp.zeros((SPAN,) + rest, values.dtype)
            .at[flat_slot]
            .set(values.reshape((slots * lanes,) + rest), mode="drop")
        )

    head_grads, grad_rows, row_loss = head_step(
        compact(got_cond), compact(got_signal), compact(got_steps), head_weights
    )
    safe_slot = jnp.minimum(got_slot, SPAN - 1)
    slot_live = got_slot < SPAN
    back_rows = jnp.where(slot_live[..., None], grad_rows[safe_slot], jnp.zeros((), jnp.bfloat16))
    back_loss = jnp.where(slot_live, row_loss[safe_slot], jnp.zeros((), jnp.bfloat16))
    ret_rows, ret_loss = (
        lax.all_to_all(back_rows, "dev", split_axis=1, concat_axis=1, tiled=True),
        lax.all_to_all(back_loss, "dev", split_axis=1, concat_axis=1, tiled=True),
    )
    ret_rows = gather_back(ret_rows)
    ret_loss = gather_back(ret_loss)
    member = (image_of[:, None] == jnp.arange(images, dtype=jnp.int32)[None, :]) & list_live[
        :, None
    ]
    image_loss = jnp.sum(jnp.where(member, ret_loss.astype(jnp.float32)[:, None], 0.0), axis=0)
    image_loss = image_loss / (counts.astype(jnp.float32) * (COPIES * CH))
    grad_dec = jnp.zeros((images * tokens, width), jnp.float32)
    grad_dec = grad_dec.at[jnp.where(list_live, source_row, images * tokens)].set(
        ret_rows.astype(jnp.float32), mode="drop"
    )
    grad_dec_in, dec_grads = block_backward(
        grad_dec.reshape(images, tokens, width), dec_valid, dec_weights, dec_kept
    )
    grad_tok = grad_dec_in[:, buffer:]
    fill_grad = jnp.sum(jnp.where(visible[..., None], 0.0, grad_tok), axis=(0, 1))
    grad_vis = jnp.where(spot_live[..., None], jax.vmap(pick_rows)(grad_tok, vis_tokens), 0.0)
    grad_enc_out = jnp.concatenate([grad_dec_in[:, :buffer], grad_vis], axis=1)
    grad_enc_in, enc_grads = block_backward(grad_enc_out, enc_valid, enc_weights, enc_kept)
    token_grad = jax.vmap(place_rows)(
        jnp.zeros((images, seq_len, width), jnp.float32),
        jnp.where(spot_live, vis_tokens, seq_len),
        grad_enc_in[:, buffer:],
    )
    embed_grad = jnp.concatenate([grad_enc_in[:, :buffer], token_grad], axis=1)
    enc_gain_one_g, enc_qkv_g, enc_proj_g, enc_gain_two_g, enc_up_g, enc_down_g = enc_grads
    dec_gain_one_g, dec_qkv_g, dec_proj_g, dec_gain_two_g, dec_up_g, dec_down_g = dec_grads
    head_in_g, head_cond_g, head_ada_g, head_inner_g, head_outer_g, head_out_g = head_grads
    shard_grads = (
        lax.psum_scatter(enc_gain_one_g, "dev", scatter_dimension=0, tiled=True),
        lax.psum_scatter(enc_qkv_g, "dev", scatter_dimension=0, tiled=True),
        lax.psum_scatter(enc_proj_g, "dev", scatter_dimension=0, tiled=True),
        lax.psum_scatter(enc_gain_two_g, "dev", scatter_dimension=0, tiled=True),
        lax.psum_scatter(enc_up_g, "dev", scatter_dimension=0, tiled=True),
        lax.psum_scatter(enc_down_g, "dev", scatter_dimension=0, tiled=True),
        lax.psum_scatter(dec_gain_one_g, "dev", scatter_dimension=0, tiled=True),
        lax.psum_scatter(dec_qkv_g, "dev", scatter_dimension=0, tiled=True),
        lax.psum_scatter(dec_proj_g, "dev", scatter_dimension=0, tiled=True),
        lax.psum_scatter(dec_gain_two_g, "dev", scatter_dimension=0, tiled=True),
        lax.psum_scatter(dec_up_g, "dev", scatter_dimension=0, tiled=True),
        lax.psum_scatter(dec_down_g, "dev", scatter_dimension=0, tiled=True),
        lax.psum_scatter(fill_grad, "dev", scatter_dimension=0, tiled=True),
        lax.psum_scatter(head_in_g, "dev", scatter_dimension=1, tiled=True),
        lax.psum_scatter(head_cond_g, "dev", scatter_dimension=0, tiled=True),
        lax.psum_scatter(head_ada_g, "dev", scatter_dimension=0, tiled=True),
        lax.psum_scatter(head_inner_g, "dev", scatter_dimension=0, tiled=True),
        lax.psum_scatter(head_outer_g, "dev", scatter_dimension=0, tiled=True),
        lax.psum_scatter(head_out_g, "dev", scatter_dimension=0, tiled=True),
    )
    (
        sum_e_one,
        sum_e_qkv,
        sum_e_proj,
        sum_e_two,
        sum_e_up,
        sum_e_down,
        sum_d_one,
        sum_d_qkv,
        sum_d_proj,
        sum_d_two,
        sum_d_up,
        sum_d_down,
        sum_fill,
        sum_h_in,
        sum_h_cond,
        sum_h_ada,
        sum_h_inner,
        sum_h_outer,
        sum_h_out,
    ) = shard_grads
    final_grads = (
        lax.psum(sum_e_one.astype(jnp.bfloat16), "grp").astype(jnp.float32),
        lax.psum(sum_e_qkv.astype(jnp.bfloat16), "grp").astype(jnp.float32),
        lax.psum(sum_e_proj.astype(jnp.bfloat16), "grp").astype(jnp.float32),
        lax.psum(sum_e_two.astype(jnp.bfloat16), "grp").astype(jnp.float32),
        lax.psum(sum_e_up.astype(jnp.bfloat16), "grp").astype(jnp.float32),
        lax.psum(sum_e_down.astype(jnp.bfloat16), "grp").astype(jnp.float32),
        lax.psum(sum_d_one.astype(jnp.bfloat16), "grp").astype(jnp.float32),
        lax.psum(sum_d_qkv.astype(jnp.bfloat16), "grp").astype(jnp.float32),
        lax.psum(sum_d_proj.astype(jnp.bfloat16), "grp").astype(jnp.float32),
        lax.psum(sum_d_two.astype(jnp.bfloat16), "grp").astype(jnp.float32),
        lax.psum(sum_d_up.astype(jnp.bfloat16), "grp").astype(jnp.float32),
        lax.psum(sum_d_down.astype(jnp.bfloat16), "grp").astype(jnp.float32),
        lax.psum(sum_fill.astype(jnp.bfloat16), "grp").astype(jnp.float32),
        lax.psum(sum_h_in.astype(jnp.bfloat16), "grp").astype(jnp.float32),
        lax.psum(sum_h_cond.astype(jnp.bfloat16), "grp").astype(jnp.float32),
        lax.psum(sum_h_ada.astype(jnp.bfloat16), "grp").astype(jnp.float32),
        lax.psum(sum_h_inner.astype(jnp.bfloat16), "grp").astype(jnp.float32),
        lax.psum(sum_h_outer.astype(jnp.bfloat16), "grp").astype(jnp.float32),
        lax.psum(sum_h_out.astype(jnp.bfloat16), "grp").astype(jnp.float32),
    )
    return (
        image_loss,
        activations,
        embed_grad,
        final_grads[0],
        final_grads[1],
        final_grads[2],
        final_grads[3],
        final_grads[4],
        final_grads[5],
        final_grads[6],
        final_grads[7],
        final_grads[8],
        final_grads[9],
        final_grads[10],
        final_grads[11],
        final_grads[12],
        final_grads[13],
        final_grads[14],
        final_grads[15],
        final_grads[16],
        final_grads[17],
        final_grads[18],
    )


def solution(mesh):
    return jax.shard_map(
        per_device,
        mesh=mesh,
        in_specs=(
            P(("grp", "dev"), None, None),
            P(("grp", "dev"), None),
            P(("grp", "dev")),
            P(("grp", "dev"), None, None),
            P(("grp", "dev"), None, None, None),
            P(("grp", "dev"), None, None),
            P("dev"),
            P("dev", None),
            P("dev", None),
            P("dev"),
            P("dev", None),
            P("dev", None),
            P("dev"),
            P("dev", None),
            P("dev", None),
            P("dev"),
            P("dev", None),
            P("dev", None),
            P("dev"),
            P(None, "dev"),
            P("dev", None),
            P("dev", None),
            P("dev", None),
            P("dev", None),
            P("dev", None),
        ),
        out_specs=(
            P(("grp", "dev")),
            P(("grp", "dev"), None, None),
            P(("grp", "dev"), None, None),
            P("dev"),
            P("dev", None),
            P("dev", None),
            P("dev"),
            P("dev", None),
            P("dev", None),
            P("dev"),
            P("dev", None),
            P("dev", None),
            P("dev"),
            P("dev", None),
            P("dev", None),
            P("dev"),
            P(None, "dev"),
            P("dev", None),
            P("dev", None),
            P("dev", None),
            P("dev", None),
            P("dev", None),
        ),
        check_vma=False,
    )
```

profile of v0, /device:TPU:24, one launch (start us, length us, event | category | flops | bytes accessed | tf_op | source)
XLA Modules:
  0.0 1756.2 jit_solution(4959851368242692641)
XLA Ops:
  47.2 11.5 all_gather.80
  58.6 11.5 all_gather.62
  80.6 35.3 %all-reduce.13 = (bf16[768]{0:T(1024)(128)(2,1)S(1)}, bf16[768]{0:T(1024)(128)(2,1)S(1)}, bf16[768]{0:T(1024)(128)(2,1)S(1)}, bf16[768]{0:T(1024)(128)(2,1)S(1)}, bf16[768]{0:T(1024)(128)(2,1)S(1)}) all-reduce(bf16[768]{0:T(1024)(128)(2,1)S(1)} %dynamic-update-slice.4, ...), channel_id=1, replica_groups=mesh['grp'=4,'dev'=8] {'dev'}, use_global_device_ids=true, to_apply=%add.5 | all-reduce | flops 3840 | bytes 15360
  166.4 12.5 all-gather.19.cloned.1.call-done
  185.3 36.1 %all-gather.21.cloned.1.call-done = bf16[768,2304]{1,0:T(8,128)(2,1)} async-done(((bf16[96,2304]{1,0:T(8,128)(2,1)}), bf16[768,2304]{1,0:T(8,128)(2,1)}) %all-gather.21.cloned.1.call-update) | async-done | bytes 3538960 | tf_op jit(solution)/shard_map/all_gather | solution.py:320
  233.8 11.3 all-gather.23.cloned.1.call-done
  247.4 49.6 %all-gather.25.cloned.1.call-done = bf16[768,3072]{1,0:T(8,128)(2,1)} async-done(((bf16[96,3072]{1,0:T(8,128)(2,1)}), bf16[768,3072]{1,0:T(8,128)(2,1)}) %all-gather.25.cloned.1.call-update) | async-done | bytes 4718608 | tf_op jit(solution)/shard_map/all_gather | solution.py:323
  297.0 12.8 fusion.9
  309.8 39.3 %all-gather.27.cloned.1.call-done = bf16[3072,768]{1,0:T(8,128)(2,1)} async-done(((bf16[384,768]{1,0:T(8,128)(2,1)}), bf16[3072,768]{1,0:T(8,128)(2,1)}) %all-gather.27.cloned.1.call-update) | async-done | bytes 4718608 | tf_op jit(solution)/shard_map/all_gather | solution.py:324
  367.4 14.9 all-to-all-done.2
  400.5 46.9 %all-gather.31.cloned.1.call-done = bf16[1024,3072]{1,0:T(8,128)(2,1)} async-done(((bf16[128,3072]{1,0:T(8,128)(2,1)}), bf16[1024,3072]{1,0:T(8,128)(2,1)}) %all-gather.31.cloned.1.call-update) | async-done | bytes 6291472 | tf_op jit(solution)/shard_map/all_gather | solution.py:382
  461.2 16.8 all-gather.33.cloned.1.call-done
  483.8 24.2 %all-gather.35.cloned.1.call-done = bf16[1024,1024]{1,0:T(8,128)(2,1)} async-done(((bf16[128,1024]{1,0:T(8,128)(2,1)}), bf16[1024,1024]{1,0:T(8,128)(2,1)}) %all-gather.35.cloned.1.call-update) | async-done | bytes 2097168 | tf_op jit(solution)/shard_map/all_gather | solution.py:384
  548.6 11.0 multiply_multiply_fusion.6
  584.3 9.4 all-to-all-done.5
  623.1 12.0 fusion.89
  635.1 11.9 fusion.92
  757.1 12.4 fusion.45
  784.1 18.6 %reduce-scatter.39.cloned.1.call-done = f32[128,1024]{1,0:T(8,128)} async-done(((f32[1024,1024]{1,0:T(8,128)}), f32[128,1024]{1,0:T(8,128)}) %reduce-scatter.39.cloned.1.call-update) | async-done | bytes 524304 | tf_op jit(solution)/shard_map/reduce_scatter | solution.py:454
  804.5 48.6 %reduce-scatter.37.cloned.1.call-done = f32[128,1024]{1,0:T(8,128)} async-done(((f32[1024,1024]{1,0:T(8,128)}), f32[128,1024]{1,0:T(8,128)}) %reduce-scatter.37.cloned.1.call-update) | async-done | bytes 524304 | tf_op jit(solution)/shard_map/reduce_scatter | solution.py:453
  854.9 75.9 %reduce-scatter.23.cloned.1.call-done = f32[96,2304]{1,0:T(8,128)} async-done(((f32[768,2304]{1,0:T(8,128)}), f32[96,2304]{1,0:T(8,128)}) %reduce-scatter.23.cloned.1.call-update) | async-done | bytes 884752 | tf_op jit(solution)/shard_map/reduce_scatter | solution.py:444
  932.7 76.0 %reduce-scatter.15.cloned.1.call-done = f32[96,2304]{1,0:T(8,128)} async-done(((f32[768,2304]{1,0:T(8,128)}), f32[96,2304]{1,0:T(8,128)}) %reduce-scatter.15.cloned.1.call-update) | async-done | bytes 884752 | tf_op jit(solution)/shard_map/reduce_scatter | solution.py:438
  1010.7 98.1 %reduce-scatter.27.cloned.1.call-done = f32[96,3072]{1,0:T(8,128)} async-done(((f32[768,3072]{1,0:T(8,128)}), f32[96,3072]{1,0:T(8,128)}) %reduce-scatter.27.cloned.1.call-update) | async-done | bytes 1179664 | tf_op jit(solution)/shard_map/reduce_scatter | solution.py:447
  1110.9 98.1 %reduce-scatter.29.cloned.1.call-done = f32[384,768]{1,0:T(8,128)} async-done(((f32[3072,768]{1,0:T(8,128)}), f32[384,768]{1,0:T(8,128)}) %reduce-scatter.29.cloned.1.call-update) | async-done | bytes 1179664 | tf_op jit(solution)/shard_map/reduce_scatter | solution.py:448
  1211.1 98.1 %reduce-scatter.19.cloned.1.call-done = f32[96,3072]{1,0:T(8,128)} async-done(((f32[768,3072]{1,0:T(8,128)}), f32[96,3072]{1,0:T(8,128)}) %reduce-scatter.19.cloned.1.call-update) | async-done | bytes 1179664 | tf_op jit(solution)/shard_map/reduce_scatter | solution.py:441
  1311.3 98.1 %reduce-scatter.21.cloned.1.call-done = f32[384,768]{1,0:T(8,128)} async-done(((f32[3072,768]{1,0:T(8,128)}), f32[384,768]{1,0:T(8,128)}) %reduce-scatter.21.cloned.1.call-update) | async-done | bytes 1179664 | tf_op jit(solution)/shard_map/reduce_scatter | solution.py:442
  1411.5 127.6 %reduce-scatter.35.cloned.1.call-done = f32[128,3072]{1,0:T(8,128)} async-done(((f32[1024,3072]{1,0:T(8,128)}), f32[128,3072]{1,0:T(8,128)}) %reduce-scatter.35.cloned.1.call-update) | async-done | bytes 1572880 | tf_op jit(solution)/shard_map/reduce_scatter | solution.py:452
  1552.0 16.7 reduce-scatter.41.cloned.1.call-done
  1569.5 30.3 %reduce-scatter.31.cloned.1.call-done = f32[16,128]{1,0:T(8,128)} async-done(((f32[16,1024]{1,0:T(8,128)}), f32[16,128]{1,0:T(8,128)}) %reduce-scatter.31.cloned.1.call-update) | async-done | bytes 8208 | tf_op jit(solution)/shard_map/reduce_scatter | solution.py:450
  1603.9 24.6 %all-reduce.12 = (bf16[768]{0:T(1024)(128)(2,1)S(1)}, bf16[768]{0:T(1024)(128)(2,1)S(1)}, bf16[768]{0:T(1024)(128)(2,1)S(1)}, bf16[768]{0:T(1024)(128)(2,1)S(1)}, bf16[768]{0:T(1024)(128)(2,1)S(1)}) all-reduce(f32[768]{0:T(1024)S(1)} %get-tuple-element.115, ...), channel_id=2, replica_groups=mesh['grp'=4,'dev'=8] {'dev'}, use_global_device_ids=true, to_apply=%region_41.43.clone | all-reduce | flops 3840 | bytes 23040
  1628.9 16.6 all-reduce.14
  1651.7 79.7 %all-reduce.18.cloned.1.call-done = (bf16[96,2304]{1,0:T(8,128)(2,1)}, bf16[96,768]{1,0:T(8,128)(2,1)}, bf16[96,3072]{1,0:T(8,128)(2,1)}, bf16[384,768]{1,0:T(8,...) async-done(((bf16[96,2304]{1,0:T(8,128)(2,1)}, ...) | async-done | bytes 5046288 | tf_op jit(solution)/shard_map/psum | solution.py:480
  (583 shorter events, 453.6 us)
Async XLA Ops:
  7.2 143.1 %all-gather.13.cloned.1.call-start = ((), (), s32[]{:S(2)}) async-start(), calls=%async_computation.20 | async-start | bytes 3981312 | tf_op jit(solution)/shard_map/all_gather | solution.py:303
  8.0 148.1 %all-gather.15.cloned.1.call-start = ((), (), s32[]{:S(2)}) async-start(), calls=%async_computation.21 | async-start | bytes 1327104 | tf_op jit(solution)/shard_map/all_gather | solution.py:304
  8.8 149.6 %all-gather.17.cloned.1.call-start = ((), (), s32[]{:S(2)}) async-start(), calls=%async_computation.22 | async-start | bytes 5308416 | tf_op jit(solution)/shard_map/all_gather | solution.py:306
  9.5 169.4 %all-gather.19.cloned.1.call-start = ((), (), s32[]{:S(2)}) async-start(), calls=%async_computation.23 | async-start | bytes 5308416 | tf_op jit(solution)/shard_map/all_gather | solution.py:307
  10.1 211.2 %all-gather.21.cloned.1.call-start = ((), (), s32[]{:S(2)}) async-start(), calls=%async_computation.24 | async-start | bytes 3981312 | tf_op jit(solution)/shard_map/all_gather | solution.py:320
  10.7 234.5 %all-gather.23.cloned.1.call-start = ((), (), s32[]{:S(2)}) async-start(), calls=%async_computation.25 | async-start | bytes 1327104 | tf_op jit(solution)/shard_map/all_gather | solution.py:321
  11.2 285.7 %all-gather.25.cloned.1.call-start = ((), (), s32[]{:S(2)}) async-start(), calls=%async_computation.26 | async-start | bytes 5308416 | tf_op jit(solution)/shard_map/all_gather | solution.py:323
  12.0 337.2 %all-gather.27.cloned.1.call-start = ((), (), s32[]{:S(2)}) async-start(), calls=%async_computation.27 | async-start | bytes 5308416 | tf_op jit(solution)/shard_map/all_gather | solution.py:324
  12.7 372.5 %all-gather.29.cloned.1.call-start = ((), (), s32[]{:S(2)}) async-start(), calls=%async_computation.28 | async-start | bytes 1769472 | tf_op jit(solution)/shard_map/all_gather | solution.py:381
  13.5 433.9 %all-gather.31.cloned.1.call-start = ((), (), s32[]{:S(2)}) async-start(), calls=%async_computation.29 | async-start | bytes 7077888 | tf_op jit(solution)/shard_map/all_gather | solution.py:382
  14.1 463.9 %all-gather.33.cloned.1.call-start = ((), (), s32[]{:S(2)}) async-start(), calls=%async_computation.30 | async-start | bytes 2359296 | tf_op jit(solution)/shard_map/all_gather | solution.py:383
  33.2 84.2 %all-to-all-start = ((s32[32,8,1]{0,2,1:T(1,128)}), s32[32,8,1]{0,2,1:T(1,128)S(1)}, u32[]{:S(2)}, u32[]{:S(2)}) async-start(s32[32,8,1]{0,2,1:T(1,128)} %bitcast.3), calls=%async_computation | async-start | bytes 8192 | tf_op jit(solution)/shard_map/all_to_all | solution.py:377
  39.9 468.1 %all-gather.35.cloned.1.call-start = ((), (), s32[]{:S(2)}) async-start(), calls=%async_computation.31 | async-start | bytes 2359296 | tf_op jit(solution)/shard_map/all_gather | solution.py:384
  117.4 11.6 all-to-all-start.3
  129.0 16.7 all-to-all-start.1
  359.9 22.3 %all-to-all-start.2 = ((bf16[32,8,768]{2,0,1:T(8,128)(2,1)}), bf16[32,8,768]{2,0,1:T(8,128)(2,1)}, u32[]{:S(2)}, u32[]{:S(2)}) async-start(bf16[32,8,768]{2,0,1:T(8,128)(2,1)} %fusion.142), calls=%async_computation.2 | async-start | bytes 786432 | tf_op jit(solution)/shard_map/all_to_all | solution.py:372
  577.8 16.0 all-to-all-start.5
  583.7 195.4 %reduce-scatter.25.cloned.1.call-start = ((), (), s32[]{:S(2)}) async-start(), calls=%async_computation.37 | async-start | bytes 2654208 | tf_op jit(solution)/shard_map/reduce_scatter | solution.py:445
  618.1 162.7 %reduce-scatter.17.cloned.1.call-start = ((), (), s32[]{:S(2)}) async-start(), calls=%async_computation.33 | async-start | bytes 2654208 | tf_op jit(solution)/shard_map/reduce_scatter | solution.py:439
  675.0 107.4 %reduce-scatter.33.cloned.1.call-start = ((), (), s32[]{:S(2)}) async-start(), calls=%async_computation.41 | async-start | bytes 3538944 | tf_op jit(solution)/shard_map/reduce_scatter | solution.py:451
  678.6 124.2 %reduce-scatter.39.cloned.1.call-start = ((), (), s32[]{:S(2)}) async-start(), calls=%async_computation.44 | async-start | bytes 4718592 | tf_op jit(solution)/shard_map/reduce_scatter | solution.py:454
  685.5 167.5 %reduce-scatter.37.cloned.1.call-start = ((), (), s32[]{:S(2)}) async-start(), calls=%async_computation.43 | async-start | bytes 4718592 | tf_op jit(solution)/shard_map/reduce_scatter | solution.py:453
  692.0 238.8 %reduce-scatter.23.cloned.1.call-start = ((), (), s32[]{:S(2)}) async-start(), calls=%async_computation.36 | async-start | bytes 7962624 | tf_op jit(solution)/shard_map/reduce_scatter | solution.py:444
  700.7 308.0 %reduce-scatter.15.cloned.1.call-start = ((), (), s32[]{:S(2)}) async-start(), calls=%async_computation.32 | async-start | bytes 7962624 | tf_op jit(solution)/shard_map/reduce_scatter | solution.py:438
  727.4 381.3 %reduce-scatter.27.cloned.1.call-start = ((), (), s32[]{:S(2)}) async-start(), calls=%async_computation.38 | async-start | bytes 10616832 | tf_op jit(solution)/shard_map/reduce_scatter | solution.py:447
  735.7 473.2 %reduce-scatter.29.cloned.1.call-start = ((), (), s32[]{:S(2)}) async-start(), calls=%async_computation.39 | async-start | bytes 10616832 | tf_op jit(solution)/shard_map/reduce_scatter | solution.py:448
  743.8 565.3 %reduce-scatter.19.cloned.1.call-start = ((), (), s32[]{:S(2)}) async-start(), calls=%async_computation.34 | async-start | bytes 10616832 | tf_op jit(solution)/shard_map/reduce_scatter | solution.py:441
  750.4 659.0 %reduce-scatter.21.cloned.1.call-start = ((), (), s32[]{:S(2)}) async-start(), calls=%async_computation.35 | async-start | bytes 10616832 | tf_op jit(solution)/shard_map/reduce_scatter | solution.py:442
  757.0 782.1 %reduce-scatter.35.cloned.1.call-start = ((), (), s32[]{:S(2)}) async-start(), calls=%async_computation.42 | async-start | bytes 14155776 | tf_op jit(solution)/shard_map/reduce_scatter | solution.py:452
  769.5 799.3 %reduce-scatter.41.cloned.1.call-start = ((), (), s32[]{:S(2)}) async-start(), calls=%async_computation.45 | async-start | bytes 73728 | tf_op jit(solution)/shard_map/reduce_scatter | solution.py:455
  772.8 826.9 %reduce-scatter.31.cloned.1.call-start = ((), (), s32[]{:S(2)}) async-start(), calls=%async_computation.40 | async-start | bytes 73728 | tf_op jit(solution)/shard_map/reduce_scatter | solution.py:450
  779.1 952.4 %all-reduce.18.cloned.1.call-start = ((), (), s32[]{:S(2)}) async-start(), calls=%async_computation.46 | async-start | bytes 10092544 | tf_op jit(solution)/shard_map/psum | solution.py:480
  (122 other events, 2735.9 us)
Sparse Core Ops, SparseCore 0:
  9.7 40.7 all-gather.12
  52.2 22.3 all-gather.14
  76.2 50.5 all-gather.16
  128.3 50.5 all-gather.18
  180.4 40.8 all-gather.20
  222.8 22.2 all-gather.22
  246.8 50.1 all-gather.24
  298.6 50.5 all-gather.26
  350.8 31.8 all-gather.28
  384.2 63.1 all-gather.30
  449.0 28.9 all-gather.32
  479.4 28.5 all-gather.34
  618.2 33.1 reduce-scatter.24
  675.1 33.3 reduce-scatter.16
  710.6 40.2 reduce-scatter.32
  753.1 49.6 reduce-scatter.38
  804.9 48.1 reduce-scatter.36
  855.2 75.4 reduce-scatter.22
  933.1 75.5 reduce-scatter.14
  1010.8 97.8 reduce-scatter.26
  1111.1 97.8 reduce-scatter.28
  1211.3 97.8 reduce-scatter.18
  1311.5 97.8 reduce-scatter.20
  1411.5 127.5 reduce-scatter.34
  1541.3 27.3 reduce-scatter.40
  1571.5 28.1 reduce-scatter.30
  1607.1 124.3 all-reduce.17
where the time goes:
time: 1770 us; the launch traced here: 1760 us
  waiting for transfers between devices  1140 us (64%)
  matrix products  259 us (15%)
  blocking collectives  106 us (6%)
  local copies, waits for them, and re-layouts  92.3 us (5%)
  other arithmetic  92.3 us (5%)
  starting transfers between devices  43.5 us (2%)
  between operations  20.3 us (1%)
    reduce_scatter x1, waiting for transfers between devices, per_device(): lax.psum_scatter(head_ada_g, 'dev', scatter_dimension=0, tiled=True)  128 us
    reduce_scatter x1, waiting for transfers between devices, per_device(): lax.psum_scatter(dec_up_g, 'dev', scatter_dimension=0, tiled=True)  98.1 us
    reduce_scatter x1, waiting for transfers between devices, per_device(): lax.psum_scatter(dec_down_g, 'dev', scatter_dimension=0, tiled=True)  98.1 us
    reduce_scatter x1, waiting for transfers between devices, per_device(): lax.psum_scatter(enc_up_g, 'dev', scatter_dimension=0, tiled=True)  98.1 us
    reduce_scatter x1, waiting for transfers between devices, per_device(): lax.psum_scatter(enc_down_g, 'dev', scatter_dimension=0, tiled=True)  98.1 us
    dot_general x14, matrix products, left_trans(): lax.dot_general(left, right, (((0,), (0,)), ((), ())), preferred_element_...  81.8 us
    psum x1, waiting for transfers between devices, per_device(): lax.psum(sum_e_qkv.astype(jnp.bfloat16), 'grp').astype(jnp.float32)  79.7 us
    reduce_scatter x1, waiting for transfers between devices, per_device(): lax.psum_scatter(enc_qkv_g, 'dev', scatter_dimension=0, tiled=True)  76 us
  transfers between devices with their start and end apart: 33, of which 24 were waited for; matrix products, arithmetic and copies ran while one was open for 18% of the time, Pallas kernels for 0%

commit v1 on v0

v1 whole, which is shorter than its diff:
```python
import functools
import math

import jax
import jax.numpy as jnp
from jax import lax
from jax.experimental import pallas as pl
from jax.experimental.pallas import tpu as pltpu
from jax.sharding import PartitionSpec as P

MESH = pl.DeviceIdType.MESH
SUM_VMEM = 60 * 1024 * 1024
HEADS = 12
HW = 1024
CH = 16
COPIES = 4
STEPS_T = 1000
ENC = 140

EPSILON = 1e-06
NEG_FILL = -1e30


def matmul(left, right):
    return jnp.dot(left, right, preferred_element_type=jnp.float32)


def left_trans(left, right):
    return lax.dot_general(
        left, right, (((0,), (0,)), ((), ())), preferred_element_type=jnp.float32
    )


def right_trans(left, right):
    return lax.dot_general(
        left, right, (((1,), (1,)), ((), ())), preferred_element_type=jnp.float32
    )


def norm_rows(values):
    centre = values - jnp.mean(values, axis=-1, keepdims=True)
    inv_std = lax.rsqrt(jnp.mean(centre * centre, axis=-1, keepdims=True) + EPSILON)
    return (centre * inv_std, inv_std)


def norm_back(grad, normed, inv_std):
    mean_grad = jnp.mean(grad, axis=-1, keepdims=True)
    mean_cross = jnp.mean(grad * normed, axis=-1, keepdims=True)
    return inv_std * (grad - mean_grad - normed * mean_cross)


def silu_slope(values):
    sigma = jax.nn.sigmoid(values)
    return sigma * (1.0 + values * (1.0 - sigma))


def gelu_slope(values):
    cumul = 0.5 * (1.0 + lax.erf(values * (1.0 / math.sqrt(2.0))))
    density = jnp.exp(-0.5 * values * values) * (1.0 / math.sqrt(2.0 * math.pi))
    return cumul + values * density


def time_embed(steps):
    half_width = HW // 2
    freqs = jnp.exp(-math.log(10000.0) * jnp.arange(half_width, dtype=jnp.float32) / half_width)
    phase = steps.astype(jnp.float32)[..., None] * freqs
    return jnp.concatenate([jnp.cos(phase), jnp.sin(phase)], axis=-1)


def noise_angle(steps):
    return (steps.astype(jnp.float32) / STEPS_T + 0.008) / 1.008 * (math.pi / 2)


def pick_rows(table, index):
    return table[index]


def place_rows(base, index, values):
    return base.at[index].set(values, mode="drop")


def inverse_order(order_row):
    return (
        jnp.zeros(order_row.shape, jnp.int32)
        .at[order_row]
        .set(jnp.arange(order_row.shape[0], dtype=jnp.int32))
    )


def attention_scores(qkv_proj, key_valid, head_size):
    raw_scores = jnp.einsum(
        "iqhd,ikhd->ihqk", qkv_proj[:, :, 0], qkv_proj[:, :, 1], preferred_element_type=jnp.float32
    )
    return jnp.where(key_valid[:, None, None, :], raw_scores * head_size ** (-0.5), NEG_FILL)


def block_forward(stream, key_valid, weights):
    gain_one, w_qkv, w_proj, gain_two, w_up, w_down = weights
    images, row_count, width = stream.shape
    head_size = width // HEADS
    flat = stream.reshape(images * row_count, width)
    normed_one, inv_one = norm_rows(flat)
    ln_one = (normed_one * gain_one.astype(jnp.float32)).astype(jnp.bfloat16)
    qkv_proj = (
        matmul(ln_one, w_qkv).astype(jnp.bfloat16).reshape(images, row_count, 3, HEADS, head_size)
    )
    scores = attention_scores(qkv_proj, key_valid, head_size)
    top_score = jnp.max(scores, axis=-1, keepdims=True)
    exp_scores = jnp.exp(scores - top_score)
    exp_total = jnp.sum(exp_scores, axis=-1, keepdims=True)
    log_total = top_score + jnp.log(exp_total)
    attn_probs = (exp_scores / exp_total).astype(jnp.bfloat16)
    mixed = jnp.einsum(
        "ihqk,ikhd->iqhd", attn_probs, qkv_proj[:, :, 2], preferred_element_type=jnp.float32
    )
    mixed = mixed.astype(jnp.bfloat16).reshape(images * row_count, width)
    middle = flat + matmul(mixed, w_proj)
    normed_two, inv_two = norm_rows(middle)
    ln_two = (normed_two * gain_two.astype(jnp.float32)).astype(jnp.bfloat16)
    up_proj = matmul(ln_two, w_up)
    up_act = jax.nn.gelu(up_proj, approximate=False).astype(jnp.bfloat16)
    result = middle + matmul(up_act, w_down)
    kept = (
        normed_one,
        inv_one,
        ln_one,
        qkv_proj,
        log_total,
        mixed,
        normed_two,
        inv_two,
        ln_two,
        up_proj,
        up_act,
    )
    return (result.reshape(images, row_count, width), kept)


def block_backward(grad_out, key_valid, weights, kept):
    gain_one, w_qkv, w_proj, gain_two, w_up, w_down = weights
    (
        normed_one,
        inv_one,
        ln_one,
        qkv_proj,
        log_total,
        mixed,
        normed_two,
        inv_two,
        ln_two,
        up_proj,
        up_act,
    ) = kept
    images, row_count, width = grad_out.shape
    head_size = width // HEADS
    grad_flat = grad_out.reshape(images * row_count, width)
    grad_low = grad_flat.astype(jnp.bfloat16)
    grad_w_down = left_trans(up_act, grad_low)
    grad_act = right_trans(grad_low, w_down)
    grad_up = (grad_act * gelu_slope(up_proj)).astype(jnp.bfloat16)
    grad_w_up = left_trans(ln_two, grad_up)
    grad_ln_two = right_trans(grad_up, w_up)
    grad_gain_two = jnp.sum(grad_ln_two * normed_two, axis=0)
    grad_mid = grad_flat + norm_back(
        grad_ln_two * gain_two.astype(jnp.float32), normed_two, inv_two
    )
    grad_mid_low = grad_mid.astype(jnp.bfloat16)
    grad_w_proj = left_trans(mixed, grad_mid_low)
    grad_mixed = (
        right_trans(grad_mid_low, w_proj)
        .astype(jnp.bfloat16)
        .reshape(images, row_count, HEADS, head_size)
    )
    scores = attention_scores(qkv_proj, key_valid, head_size)
    attn_probs = jnp.exp(scores - log_total)
    grad_probs = jnp.einsum(
        "iqhd,ikhd->ihqk", grad_mixed, qkv_proj[:, :, 2], preferred_element_type=jnp.float32
    )
    row_dot = jnp.sum(grad_probs * attn_probs, axis=-1, keepdims=True)
    grad_scores = (attn_probs * (grad_probs - row_dot) * head_size ** (-0.5)).astype(jnp.bfloat16)
    grad_query = jnp.einsum(
        "ihqk,ikhd->iqhd", grad_scores, qkv_proj[:, :, 1], preferred_element_type=jnp.float32
    )
    grad_key = jnp.einsum(
        "ihqk,iqhd->ikhd", grad_scores, qkv_proj[:, :, 0], preferred_element_type=jnp.float32
    )
    grad_value = jnp.einsum(
        "ihqk,iqhd->ikhd",
        attn_probs.astype(jnp.bfloat16),
        grad_mixed,
        preferred_element_type=jnp.float32,
    )
    grad_qkv = jnp.stack([grad_query, grad_key, grad_value], axis=2)
    grad_qkv = grad_qkv.reshape(images * row_count, 3 * width).astype(jnp.bfloat16)
    grad_w_qkv = left_trans(ln_one, grad_qkv)
    grad_ln_one = right_trans(grad_qkv, w_qkv)
    grad_gain_one = jnp.sum(grad_ln_one * normed_one, axis=0)
    grad_in = grad_mid + norm_back(grad_ln_one * gain_one.astype(jnp.float32), normed_one, inv_one)
    grads = (grad_gain_one, grad_w_qkv, grad_w_proj, grad_gain_two, grad_w_up, grad_w_down)
    return (grad_in.reshape(images, row_count, width), grads)


def head_step(cond_rows, live, noisy, noise_vals, steps, weights):
    w_in, w_cond, w_ada, w_inner, w_outer, w_out = weights
    row_count = cond_rows.shape[0]
    flat_count = row_count * COPIES
    cond = matmul(cond_rows, w_cond)
    cond_full = (cond[:, None, :] + time_embed(steps)).reshape(flat_count, HW)
    cond_act = jax.nn.silu(cond_full).astype(jnp.bfloat16)
    modulate = matmul(cond_act, w_ada)
    shift_part = modulate[:, :HW]
    scale_part = modulate[:, HW : 2 * HW]
    gate_part = modulate[:, 2 * HW :]
    hidden = matmul(noisy, w_in)
    normed_in, inv_in = norm_rows(hidden)
    mlp_in = (normed_in * (1.0 + scale_part) + shift_part).astype(jnp.bfloat16)
    inner = matmul(mlp_in, w_inner)
    inner_act = jax.nn.silu(inner).astype(jnp.bfloat16)
    branch = matmul(inner_act, w_outer)
    hidden_two = hidden + gate_part * branch
    normed_out, inv_out = norm_rows(hidden_two)
    final_in = normed_out.astype(jnp.bfloat16)
    error = matmul(final_in, w_out) - noise_vals
    row_loss = jnp.sum((error * error).reshape(row_count, COPIES * CH), axis=1).astype(jnp.bfloat16)
    live_flat = jnp.broadcast_to(live[:, None], (row_count, COPIES)).reshape(flat_count, 1)
    grad_pred = jnp.where(live_flat, error * (2.0 / COPIES), 0.0).astype(jnp.bfloat16)
    grad_w_out = left_trans(final_in, grad_pred)
    grad_two = norm_back(right_trans(grad_pred, w_out), normed_out, inv_out)
    grad_branch = (grad_two * gate_part).astype(jnp.bfloat16)
    grad_gate = grad_two * branch
    grad_w_outer = left_trans(inner_act, grad_branch)
    grad_inner = (right_trans(grad_branch, w_outer) * silu_slope(inner)).astype(jnp.bfloat16)
    grad_w_inner = left_trans(mlp_in, grad_inner)
    grad_mlp_in = right_trans(grad_inner, w_inner)
    grad_hidden = (
        grad_two + norm_back(grad_mlp_in * (1.0 + scale_part), normed_in, inv_in)
    ).astype(jnp.bfloat16)
    grad_w_in = left_trans(noisy, grad_hidden)
    grad_mod = jnp.concatenate([grad_mlp_in, grad_mlp_in * normed_in, grad_gate], axis=1).astype(
        jnp.bfloat16
    )
    grad_w_ada = left_trans(cond_act, grad_mod)
    grad_cond_full = right_trans(grad_mod, w_ada) * silu_slope(cond_full)
    grad_cond = jnp.sum(grad_cond_full.reshape(row_count, COPIES, HW), axis=1).astype(jnp.bfloat16)
    grad_w_cond = left_trans(cond_rows, grad_cond)
    grad_rows = right_trans(grad_cond, w_cond).astype(jnp.bfloat16)
    grads = (grad_w_in, grad_w_cond, grad_w_ada, grad_w_inner, grad_w_outer, grad_w_out)
    return (grads, grad_rows, row_loss)


class Slab:
    def __init__(self, rows, cols, by_rows):
        self.rows, self.cols, self.by_rows = rows, cols, by_rows
        self.piece = (rows // 4, cols) if by_rows else (rows, cols // 4)

    def spot(self, shard, quarter, half=None):
        piece_rows, piece_cols = self.piece
        row = shard * self.rows
        if self.by_rows:
            row = row + quarter * piece_rows
        height = piece_rows
        if half is not None:
            height = piece_rows // 2
            row = row + half * height
        col = 0 if self.by_rows else quarter * piece_cols
        return (pl.ds(aligned(row, 16), height), pl.ds(aligned(col, 128), piece_cols))

    def shard(self, shard):
        return (pl.ds(aligned(shard * self.rows, 16), self.rows), pl.ds(0, self.cols))

    def within(self, quarter):
        return self.spot(0, quarter)


def aligned(value, multiple):
    return value if isinstance(value, int) else pl.multiple_of(value, multiple)


def place(depth):
    group, device = lax.axis_index("grp"), lax.axis_index("dev")
    level, core = device // 2, device % 2
    flip = lambda bit: group + (1 << bit) * (1 - 2 * ((group // (1 << bit)) % 2))
    return group, level, core, flip


def greet(peers):
    barrier = pltpu.get_barrier_semaphore()
    for peer in peers:
        pl.semaphore_signal(barrier, inc=1, device_id=peer, device_id_type=MESH)
    pl.semaphore_wait(barrier, len(peers))


def gather_kernel(slabs, depth, *refs):
    count = len(slabs)
    mine, whole = refs[:count], refs[count : 2 * count]
    sent, got, own_sent, own_got, own_copy = refs[2 * count :]
    group, level, core, flip = place(depth)
    x_peer, y_peer = (flip(0), 2 * level + core), (flip(1), 2 * level + core)
    partner = (group, 2 * level + 1 - core)

    def level_at(step):
        return lax.rem(level + step + depth, depth)

    z_peers = [(group, 2 * level_at(step) + core) for step in range(1, depth)]
    greet([x_peer, y_peer, partner] + z_peers)

    def move(kind, item, source, target, device):
        return pltpu.make_async_remote_copy(
            src_ref=source,
            dst_ref=target,
            send_sem=sent.at[kind, item],
            recv_sem=got.at[kind, item],
            device_id=device,
            device_id_type=MESH,
        )

    Z, X, Y, XH, YH, CORE = range(6)
    items = [(k, step) for k in range(count) for step in range(1, depth)]

    def by_z(item):
        k, step = items[item]
        slab = slabs[k]
        target = whole[k].at[slab.spot(2 * level + core, group)]
        return move(Z, item, mine[k].at[slab.within(group)], target, z_peers[step - 1])

    def shard_of(item):
        return 2 * level_at(-items[item][1]) + core

    def forward(kind, item, quarter, half, device):
        k = items[item][0]
        here = whole[k].at[slabs[k].spot(shard_of(item), quarter, half)]
        return move(kind, item, here, here, device)

    def core_copy(item, core_of):
        k, step = items[item]
        here = whole[k].at[slabs[k].shard(2 * level_at(-step) + core_of)]
        return move(CORE, item, here, here, partner)

    own = []
    for k, slab in enumerate(slabs):
        for step in range(1, depth):
            by_z(k * (depth - 1) + step - 1).start()
        target = whole[k].at[slab.shard(2 * level + core)]
        keep = pltpu.make_async_copy(mine[k], target, own_copy.at[k])
        keep.start()
        share = pltpu.make_async_remote_copy(
            src_ref=mine[k],
            dst_ref=target,
            send_sem=own_sent.at[k],
            recv_sem=own_got.at[k],
            device_id=partner,
            device_id_type=MESH,
        )
        share.start()
        own.append((keep, share))

    total = len(items)
    for turn in range(total + 2):
        if turn < total:
            k = items[turn][0]
            here = whole[k].at[slabs[k].spot(shard_of(turn), group)]
            move(Z, turn, here, here, x_peer).wait_recv()
            forward(X, turn, group, None, x_peer).start()
            forward(Y, turn, group, None, y_peer).start()
        item = turn - 1
        if 0 <= item < total:
            forward(X, item, flip(0), None, x_peer).wait_recv()
            forward(YH, item, flip(0), 0, y_peer).start()
            forward(Y, item, flip(1), None, y_peer).wait_recv()
            forward(XH, item, flip(1), 1, x_peer).start()
        item = turn - 2
        if 0 <= item < total:
            far = 3 - group
            forward(YH, item, far, 0, y_peer).wait_recv()
            forward(XH, item, far, 1, x_peer).wait_recv()
            core_copy(item, core).start()
    for item in range(total):
        by_z(item).wait_send()
        forward(X, item, group, None, x_peer).wait_send()
        forward(Y, item, group, None, y_peer).wait_send()
        forward(YH, item, flip(0), 0, y_peer).wait_send()
        forward(XH, item, flip(1), 1, x_peer).wait_send()
        core_copy(item, core).wait_send()
        core_copy(item, 1 - core).wait_recv()
    for keep, share in own:
        keep.wait()
        share.wait()


def gather_slabs(shards, slabs, depth):
    count, items = len(slabs), len(slabs) * (depth - 1)
    return pl.pallas_call(
        functools.partial(gather_kernel, slabs, depth),
        out_shape=[
            jax.ShapeDtypeStruct((2 * depth * s.rows, s.cols), jnp.bfloat16) for s in slabs
        ],
        in_specs=[pl.BlockSpec(memory_space=pl.ANY)] * count,
        out_specs=[pl.BlockSpec(memory_space=pl.ANY)] * count,
        scratch_shapes=[
            pltpu.SemaphoreType.DMA((6, items)),
            pltpu.SemaphoreType.DMA((6, items)),
            pltpu.SemaphoreType.DMA((count,)),
            pltpu.SemaphoreType.DMA((count,)),
            pltpu.SemaphoreType.DMA((count,)),
        ],
        compiler_params=pltpu.CompilerParams(collective_id=0, has_side_effects=True),
        name="gather_weights",
    )(*shards)


def sum_kernel(slabs, orders, depth, *refs):
    count = len(slabs)
    grads, outs = refs[:count], refs[count : 2 * count]
    rest = refs[2 * count :]
    take = lambda: (rest[:count], rest[count:])
    held, rest = take()
    from_first, rest = take()
    from_second, rest = take()
    from_level, rest = take()
    result, rest = take()
    stage, rest = take()
    stage_sem, out_sem, core_sent, core_got, sent, got, z_sent, z_got = rest
    group, level, core, flip = place(depth)
    me = 2 * level + core
    partner = (group, 2 * level + 1 - core)
    bit = lambda b: (group // (1 << b)) % 2

    def level_at(step):
        return lax.rem(level + step + depth, depth)

    z_peers = [(group, 2 * level_at(step) + core) for step in range(1, depth)]
    greet([(flip(0), me), (flip(1), me), partner] + z_peers)

    def move(pair, k, kind, source, target, device):
        send, receive = pair
        return pltpu.make_async_remote_copy(
            src_ref=source,
            dst_ref=target,
            send_sem=send.at[kind, k],
            recv_sem=receive.at[kind, k],
            device_id=device,
            device_id_type=MESH,
        )

    def core_move(k, lev):
        source = grads[k].at[slabs[k].shard(2 * lev + 1 - core)]
        return move((core_sent, core_got), k, lev, source, held[k].at[lev], partner)

    def rows_loop(height, body):
        step = 32 if height % 32 == 0 else 16

        def turn(i, carry):
            body(pl.ds(aligned(i * step, 16), step))
            return carry

        lax.fori_loop(0, height // step, turn, 0)

    def shifted(rows, by):
        return pl.ds(aligned(rows.start + by, 16), rows.size)

    def first_bit(k):
        return 1 if orders[k] == "yx" else 0

    def quarter(k, first, second):
        b = first_bit(k)
        return first * (1 << b) + second * (1 << (1 - b))

    def first_move(k, j):
        b = first_bit(k)
        where = slabs[k].within(quarter(k, 1 - bit(b), j))
        source = held[k].at[(level,) + where] if orders[k][0] == "z" else held[k].at[(slice(None),) + where]
        return move((sent, got), k, j, source, from_first[k].at[j], (flip(b), me))

    def second_move(k):
        b = first_bit(k)
        where = slabs[k].within(quarter(k, bit(b), 1 - bit(1 - b)))
        source = held[k].at[(level,) + where] if orders[k][0] == "z" else held[k].at[(slice(None),) + where]
        return move((sent, got), k, 2, source, from_second[k], (flip(1 - b), me))

    def level_move(k, step):
        lev = level_at(step)
        source = held[k].at[lev] if orders[k][0] == "z" else held[k].at[(lev,) + slabs[k].within(group)]
        return move((z_sent, z_got), k, step - 1, source, from_level[k].at[step - 1], z_peers[step - 1])

    def spread_second(k, whose):
        here = result[k].at[slabs[k].within(whose)]
        return move((sent, got), k, 3, here, here, (flip(1 - first_bit(k)), me))

    def spread_first(k, j, whose):
        here = result[k].at[slabs[k].within(whose)]
        return move((sent, got), k, 4 + j, here, here, (flip(first_bit(k)), me))

    def out_copy(k):
        return pltpu.make_async_copy(result[k], outs[k], out_sem.at[k])

    def stage_copy(k, lev):
        source = grads[k].at[slabs[k].shard(2 * lev + core)]
        return pltpu.make_async_copy(source, stage[k].at[lev % 2], stage_sem.at[k, lev % 2])

    def add_core(k):
        slab = slabs[k]
        stage_copy(k, 0).start()
        for lev in range(depth):
            if lev + 1 < depth:
                stage_copy(k, lev + 1).start()
            core_move(k, lev).wait_recv()
            stage_copy(k, lev).wait()

            def body(rows):
                total = held[k][lev, rows, :].astype(jnp.float32) + stage[k][lev % 2, rows, :].astype(jnp.float32)
                held[k][lev, rows, :] = total.astype(jnp.bfloat16)

            rows_loop(slab.rows, body)

    def levels_of(k):
        return [level] if orders[k][0] == "z" else list(range(depth))

    def add_first(k):
        slab = slabs[k]
        for j in range(2):
            first_move(k, j).wait_recv()
            rows_of, cols = slab.within(quarter(k, bit(first_bit(k)), j))
            for lev in levels_of(k):

                def body(rows):
                    at = (lev, shifted(rows, rows_of.start), cols)
                    extra = from_first[k][j, rows, :] if orders[k][0] == "z" else from_first[k][j, lev, rows, :]
                    held[k][at] = (held[k][at].astype(jnp.float32) + extra.astype(jnp.float32)).astype(jnp.bfloat16)

                rows_loop(slab.piece[0], body)

    def add_second(k):
        slab = slabs[k]
        second_move(k).wait_recv()
        rows_of, cols = slab.within(group)
        for lev in levels_of(k):

            def body(rows):
                at = (lev, shifted(rows, rows_of.start), cols)
                extra = from_second[k][rows, :] if orders[k][0] == "z" else from_second[k][lev, rows, :]
                total = held[k][at].astype(jnp.float32) + extra.astype(jnp.float32)
                target = result[k].at[shifted(rows, rows_of.start), cols] if orders[k][0] == "z" else held[k].at[at]
                target[...] = total.astype(jnp.bfloat16)

            rows_loop(slab.piece[0], body)

    def add_level(k):
        slab = slabs[k]
        for step in range(1, depth):
            level_move(k, step).wait_recv()
        if orders[k][0] == "z":

            def body(rows):
                total = held[k][level, rows, :].astype(jnp.float32)
                for step in range(depth - 1):
                    total = total + from_level[k][step, rows, :].astype(jnp.float32)
                held[k][level, rows, :] = total.astype(jnp.bfloat16)

            rows_loop(slab.rows, body)
            return
        rows_of, cols = slab.within(group)

        def body(rows):
            at = (shifted(rows, rows_of.start), cols)
            total = held[k][(level,) + at].astype(jnp.float32)
            for step in range(depth - 1):
                total = total + from_level[k][step, rows, :].astype(jnp.float32)
            result[k][at] = total.astype(jnp.bfloat16)

        rows_loop(slab.piece[0], body)

    def begin_core(k):
        for lev in range(depth):
            core_move(k, lev).start()

    def begin_first(k):
        first_move(k, 0).start()
        first_move(k, 1).start()

    def begin_level(k):
        for step in range(1, depth):
            level_move(k, step).start()

    def end_spread_second(k):
        spread_second(k, flip(1 - first_bit(k))).wait_recv()
        spread_first(k, 0, group).start()
        spread_first(k, 1, flip(1 - first_bit(k))).start()

    def end_spread_first(k):
        b = first_bit(k)
        spread_first(k, 0, flip(b)).wait_recv()
        spread_first(k, 1, 3 - group).wait_recv()
        out_copy(k).start()

    def steps(k):
        if orders[k][0] == "z":
            return [
                lambda: (add_core(k), begin_level(k)),
                lambda: (add_level(k), begin_first(k)),
                lambda: (add_first(k), second_move(k).start()),
                lambda: (add_second(k), spread_second(k, group).start()),
                lambda: end_spread_second(k),
                lambda: end_spread_first(k),
            ]
        return [
            lambda: (add_core(k), begin_first(k)),
            lambda: (add_first(k), second_move(k).start()),
            lambda: (add_second(k), begin_level(k)),
            lambda: (add_level(k), spread_second(k, group).start()),
            lambda: end_spread_second(k),
            lambda: end_spread_first(k),
        ]

    plans = [steps(k) for k in range(count)]
    begin_core(0)
    for turn in range(count + 5):
        if turn + 1 < count:
            begin_core(turn + 1)
        for place_in in range(6):
            k = turn - place_in
            if 0 <= k < count:
                plans[k][place_in]()
    for k in range(count):
        for lev in range(depth):
            core_move(k, lev).wait_send()
        first_move(k, 0).wait_send()
        first_move(k, 1).wait_send()
        second_move(k).wait_send()
        for step in range(1, depth):
            level_move(k, step).wait_send()
        spread_second(k, group).wait_send()
        spread_first(k, 0, group).wait_send()
        spread_first(k, 1, flip(1 - first_bit(k))).wait_send()
        out_copy(k).wait()


def sum_slabs(grads, slabs, orders, depth):
    count = len(slabs)
    half = jnp.bfloat16
    held, first, second, lev, result, stage = [], [], [], [], [], []
    for slab, order in zip(slabs, orders, strict=True):
        shard = (slab.rows, slab.cols)
        held.append(pltpu.VMEM((depth,) + shard, half))
        result.append(pltpu.VMEM(shard, half))
        stage.append(pltpu.VMEM((2,) + shard, half))
        if order[0] == "z":
            first.append(pltpu.VMEM((2,) + slab.piece, half))
            second.append(pltpu.VMEM(slab.piece, half))
            lev.append(pltpu.VMEM((depth - 1,) + shard, half))
        else:
            first.append(pltpu.VMEM((2, depth) + slab.piece, half))
            second.append(pltpu.VMEM((depth,) + slab.piece, half))
            lev.append(pltpu.VMEM((depth - 1,) + slab.piece, half))
    dma = pltpu.SemaphoreType.DMA
    return pl.pallas_call(
        functools.partial(sum_kernel, slabs, orders, depth),
        out_shape=[jax.ShapeDtypeStruct((s.rows, s.cols), half) for s in slabs],
        in_specs=[pl.BlockSpec(memory_space=pl.ANY)] * count,
        out_specs=[pl.BlockSpec(memory_space=pl.ANY)] * count,
        scratch_shapes=held
        + first
        + second
        + lev
        + result
        + stage
        + [
            dma((count, 2)),
            dma((count,)),
            dma((depth, count)),
            dma((depth, count)),
            dma((6, count)),
            dma((6, count)),
            dma((depth - 1, count)),
            dma((depth - 1, count)),
        ],
        compiler_params=pltpu.CompilerParams(
            collective_id=1, has_side_effects=True, vmem_limit_bytes=SUM_VMEM
        ),
        name="sum_gradients",
    )(*grads)


SMALL_ROWS, SMALL_COLS = 32, 512


def pack_small(vectors, first, last):
    parts = vectors[0].shape[0] // 96
    lanes = jnp.stack([v.reshape(parts, 96) for v in vectors], axis=1)
    lanes = jnp.pad(lanes, ((0, 0), (0, 16 - len(vectors)), (0, 128 - 96)))
    first = first.reshape(CH, parts, 128).transpose(1, 0, 2)
    last = last.reshape(parts, 128, CH).transpose(0, 2, 1)
    packed = jnp.concatenate([lanes, first, last], axis=2)
    packed = jnp.pad(packed, ((0, 0), (0, SMALL_ROWS - 16), (0, SMALL_COLS - 384)))
    return packed.reshape(parts * SMALL_ROWS, SMALL_COLS)


def unpack_small(packed):
    parts = packed.shape[0] // SMALL_ROWS
    packed = packed.reshape(parts, SMALL_ROWS, SMALL_COLS)
    vectors = [packed[:, i, :96].reshape(parts * 96) for i in range(5)]
    first = packed[:, :CH, 128:256].transpose(1, 0, 2).reshape(CH, parts * 128)
    last = packed[:, :CH, 256:384].transpose(0, 2, 1).reshape(parts * 128, CH)
    return vectors, first, last


SLABS = (
    Slab(96, 3072, False),
    Slab(96, 3072, False),
    Slab(384, 768, True),
    Slab(96, 3072, False),
    Slab(96, 3072, False),
    Slab(384, 768, True),
    Slab(96, 1024, False),
    Slab(128, 3072, False),
    Slab(128, 2048, False),
    Slab(32, 512, False),
)


def gather_weights(shards):
    (e_one, e_qkv, e_proj, e_two, e_up, e_down, d_one, d_qkv, d_proj, d_two, d_up, d_down, fill, h_in, h_cond, h_ada, h_inner, h_outer, h_out) = shards
    if lax.axis_size("dev") != 8 or lax.axis_size("grp") != 4:
        whole = [lax.all_gather(w, "dev", axis=0, tiled=True) for w in shards]
        whole[13] = lax.all_gather(h_in, "dev", axis=1, tiled=True)
        return whole
    depth = lax.axis_size("dev") // 2
    packed = (
        jnp.concatenate([e_qkv, e_proj], axis=1), e_up, e_down,
        jnp.concatenate([d_qkv, d_proj], axis=1), d_up, d_down,
        h_cond, h_ada, jnp.concatenate([h_inner, h_outer], axis=1),
        pack_small([e_one, e_two, d_one, d_two, fill], h_in, h_out),
    )
    ea, eu, ed, da, du, dd, hc, ha, hio, small = gather_slabs(packed, SLABS, depth)
    (e_one, e_two, d_one, d_two, fill), h_in, h_out = unpack_small(small)
    split = e_qkv.shape[1]
    return [e_one, ea[:, :split], ea[:, split:], e_two, eu, ed, d_one, da[:, :split], da[:, split:], d_two, du, dd, fill,
            h_in, hc, ha, hio[:, :HW], hio[:, HW:], h_out]


def sum_gradients(grads):
    low = [g.astype(jnp.bfloat16) for g in grads]
    (e_one, e_qkv, e_proj, e_two, e_up, e_down, d_one, d_qkv, d_proj, d_two, d_up, d_down, fill, h_in, h_cond, h_ada, h_inner, h_outer, h_out) = low
    if lax.axis_size("dev") != 8 or lax.axis_size("grp") != 4:
        sums = [lax.psum_scatter(g, "dev", scatter_dimension=int(i == 13), tiled=True) for i, g in enumerate(grads)]
        return [lax.psum(g.astype(jnp.bfloat16), "grp").astype(jnp.float32) for g in sums]
    depth = lax.axis_size("dev") // 2
    packed = (
        jnp.concatenate([e_qkv, e_proj], axis=1), e_up, e_down,
        jnp.concatenate([d_qkv, d_proj], axis=1), d_up, d_down,
        h_cond, h_ada, jnp.concatenate([h_inner, h_outer], axis=1),
        pack_small([e_one, e_two, d_one, d_two, fill], h_in, h_out),
    )
    turn = (7, 8, 6, 3, 4, 5, 0, 1, 2, 9)
    orders = ("xy", "yx", "zx", "xy", "yx", "zx", "yx", "xy", "yx", "xy")
    sums = sum_slabs([packed[t] for t in turn], [SLABS[t] for t in turn], [orders[t] for t in turn], depth)
    back = [None] * len(turn)
    for t, s in zip(turn, sums, strict=True):
        back[t] = s.astype(jnp.float32)
    ea, eu, ed, da, du, dd, hc, ha, hio, small = back
    (e_one, e_two, d_one, d_two, fill), h_in, h_out = unpack_small(small)
    split = e_qkv.shape[1]
    return [e_one, ea[:, :split], ea[:, split:], e_two, eu, ed, d_one, da[:, :split], da[:, split:], d_two, du, dd, fill,
            h_in, hc, ha, hio[:, :HW], hio[:, HW:], h_out]


def per_device(
    embedded,
    mask_order,
    counts,
    targets,
    noise_copies,
    timesteps,
    enc_gain_one,
    enc_qkv,
    enc_proj,
    enc_gain_two,
    enc_up,
    enc_down,
    dec_gain_one,
    dec_qkv,
    dec_proj,
    dec_gain_two,
    dec_up,
    dec_down,
    mask_token,
    head_in,
    head_cond,
    head_ada,
    head_inner,
    head_outer,
    head_out,
):
    images, tokens, width = embedded.shape
    seq_len = mask_order.shape[1]
    buffer = tokens - seq_len
    visible_max = ENC - buffer
    seen = gather_weights(
        (enc_gain_one, enc_qkv, enc_proj, enc_gain_two, enc_up, enc_down,
         dec_gain_one, dec_qkv, dec_proj, dec_gain_two, dec_up, dec_down, mask_token,
         head_in, head_cond, head_ada, head_inner, head_outer, head_out)
    )
    enc_weights, dec_weights, token_fill = seen[:6], seen[6:12], seen[12].astype(jnp.float32)
    head_weights = seen[13:]
    spots = jnp.arange(visible_max, dtype=jnp.int32)
    spot_src = jnp.minimum(counts[:, None] + spots[None, :], seq_len - 1)
    vis_tokens = jnp.take_along_axis(mask_order, spot_src, axis=1)
    spot_live = spots[None, :] < (seq_len - counts)[:, None]
    buffer_rows = jnp.arange(buffer, dtype=jnp.int32)[None, :]
    enc_rows = jnp.concatenate([buffer_rows, buffer + vis_tokens], axis=1)
    enc_in = jax.vmap(pick_rows)(embedded, enc_rows).astype(jnp.float32)
    enc_valid = jnp.concatenate([jnp.ones((images, buffer), bool), spot_live], axis=1)
    enc_out, enc_kept = block_forward(enc_in, enc_valid, enc_weights)
    rank = jax.vmap(inverse_order)(mask_order)
    visible = rank >= counts[:, None]
    enc_source = buffer + jnp.clip(rank - counts[:, None], 0, visible_max - 1)
    tok_rows = jnp.where(
        visible[..., None], jax.vmap(pick_rows)(enc_out, enc_source), token_fill[None, None, :]
    )
    dec_in = jnp.concatenate([enc_out[:, :buffer], tok_rows], axis=1)
    dec_valid = jnp.ones((images, tokens), bool)
    dec_out, dec_kept = block_forward(dec_in, dec_valid, dec_weights)
    activations = dec_out.astype(jnp.bfloat16)
    masked = ~visible.reshape(images * seq_len)
    angle = noise_angle(timesteps)
    noise_vals = noise_copies.astype(jnp.float32)
    noisy = jnp.cos(angle)[..., None] * targets[:, :, None, :] + jnp.sin(angle)[..., None] * noise_vals
    flat_count = images * seq_len * COPIES
    head_grads, grad_rows, row_loss = head_step(
        activations[:, buffer:].reshape(images * seq_len, width),
        masked,
        noisy.astype(jnp.bfloat16).reshape(flat_count, CH),
        noise_vals.reshape(flat_count, CH),
        timesteps.reshape(images * seq_len, COPIES),
        head_weights,
    )
    image_loss = jnp.sum(jnp.where(masked, row_loss.astype(jnp.float32), 0.0).reshape(images, seq_len), axis=1)
    image_loss = image_loss / (counts.astype(jnp.float32) * (COPIES * CH))
    grad_dec = jnp.concatenate(
        [jnp.zeros((images, buffer, width), jnp.float32), grad_rows.astype(jnp.float32).reshape(images, seq_len, width)],
        axis=1,
    )
    grad_dec_in, dec_grads = block_backward(
        grad_dec, dec_valid, dec_weights, dec_kept
    )
    grad_tok = grad_dec_in[:, buffer:]
    fill_grad = jnp.sum(jnp.where(visible[..., None], 0.0, grad_tok), axis=(0, 1))
    grad_vis = jnp.where(spot_live[..., None], jax.vmap(pick_rows)(grad_tok, vis_tokens), 0.0)
    grad_enc_out = jnp.concatenate([grad_dec_in[:, :buffer], grad_vis], axis=1)
    grad_enc_in, enc_grads = block_backward(grad_enc_out, enc_valid, enc_weights, enc_kept)
    token_grad = jax.vmap(place_rows)(
        jnp.zeros((images, seq_len, width), jnp.float32),
        jnp.where(spot_live, vis_tokens, seq_len),
        grad_enc_in[:, buffer:],
    )
    embed_grad = jnp.concatenate([grad_enc_in[:, :buffer], token_grad], axis=1)
    final_grads = sum_gradients([*enc_grads, *dec_grads, fill_grad, *head_grads])
    return (image_loss, activations, embed_grad, *final_grads)


def solution(mesh):
    return jax.shard_map(
        per_device,
        mesh=mesh,
        in_specs=(
            P(("grp", "dev"), None, None),
            P(("grp", "dev"), None),
            P(("grp", "dev")),
            P(("grp", "dev"), None, None),
            P(("grp", "dev"), None, None, None),
            P(("grp", "dev"), None, None),
            P("dev"),
            P("dev", None),
            P("dev", None),
            P("dev"),
            P("dev", None),
            P("dev", None),
            P("dev"),
            P("dev", None),
            P("dev", None),
            P("dev"),
            P("dev", None),
            P("dev", None),
            P("dev"),
            P(None, "dev"),
            P("dev", None),
            P("dev", None),
            P("dev", None),
            P("dev", None),
            P("dev", None),
        ),
        out_specs=(
            P(("grp", "dev")),
            P(("grp", "dev"), None, None),
            P(("grp", "dev"), None, None),
            P("dev"),
            P("dev", None),
            P("dev", None),
            P("dev"),
            P("dev", None),
            P("dev", None),
            P("dev"),
            P("dev", None),
            P("dev", None),
            P("dev"),
            P("dev", None),
            P("dev", None),
            P("dev"),
            P(None, "dev"),
            P("dev", None),
            P("dev", None),
            P("dev", None),
            P("dev", None),
            P("dev", None),
        ),
        check_vma=False,
    )
```

time: 1770 us -> 831 us (0.47)
  waiting for transfers between devices: 1140 us -> 0 us
  Pallas kernels: 0 us -> 444 us
  blocking collectives: 106 us -> 0 us
  starting transfers between devices: 43.5 us -> 0 us
  matrix products: 259 us -> 231 us
  local copies, waits for them, and re-layouts: 92.3 us -> 70.4 us
  other arithmetic: 92.3 us -> 74.1 us
    reduce_scatter x14 -> x0, waiting for transfers between devices: 786 us -> none  [the longest x1 128 us: per_device(): lax.psum_scatter(head_ada_g, 'dev', scatter_dimension=0, tiled=True)]
    pallas_call x0 -> x2, Pallas kernels: none -> 444 us  [the longest x1 278 us: sum_slabs(): pl.pallas_call(functools.partial(sum_kernel, slabs, orders, depth), out_s...]
    all_gather x12 -> x0, waiting for transfers between devices: 237 us -> none  [the longest x1 49.6 us: per_device(): lax.all_gather(dec_up, 'dev', axis=0, tiled=True)]
    psum x1 -> x0, waiting for transfers between devices: 79.7 us -> none  [per_device(): lax.psum(sum_e_qkv.astype(jnp.bfloat16), 'grp').astype(jnp.float32)]
    unnamed x3 -> x0, blocking collectives: 66.9 us -> none
    all_to_all x6 -> x0, starting transfers between devices: 41.8 us -> none  [the longest x1 9.35 us: per_device(): lax.all_to_all(spread(step_list), 'dev', split_axis=1, concat_axis=1, til...]
    convert_element_type x40 -> x8, other arithmetic: 47.6 us -> 7.96 us  [the longest x6 6.49 us: sum_gradients(): back[t] = s.astype(jnp.float32)]
    all_to_all x6 -> x0, waiting for transfers between devices: 27.8 us -> none  [the longest x1 14.9 us: per_device(): lax.all_to_all(spread(cond_list), 'dev', split_axis=1, concat_axis=1, til...]
  transfers between devices with their start and end apart: 33 -> 0, of which waited for: 24 -> 0; matrix products, arithmetic and copies ran while one was open for 18% -> 0% of each run, Pallas kernels for 0% -> 0%
where the time goes in v1:
time: 831 us; the launch traced here: 824 us
  Pallas kernels  444 us (53%)
  matrix products  231 us (28%)
  other arithmetic  74.1 us (9%)
  local copies, waits for them, and re-layouts  70.4 us (8%)
    pallas_call x1, Pallas kernels, sum_slabs(): pl.pallas_call(functools.partial(sum_kernel, slabs, orders, depth), out_s...  278 us
    pallas_call x1, Pallas kernels, gather_slabs(): pl.pallas_call(functools.partial(gather_kernel, slabs, depth), out_shape=...  167 us
    dot_general x14, matrix products, matmul(): return jnp.dot(left, right, preferred_element_type=jnp.float32)  62.1 us
    dot_general x13, matrix products, right_trans(): lax.dot_general(left, right, (((1,), (1,)), ((), ())), preferred_element_...  61.5 us
    dot_general x14, matrix products, left_trans(): lax.dot_general(left, right, (((0,), (0,)), ((), ())), preferred_element_...  57.8 us

profile of v1, /device:TPU:24, one launch (start us, length us, event | category | flops | bytes accessed | tf_op | source)
XLA Modules:
  0.0 824.5 jit_solution(9035395328319692616)
XLA Ops:
  17.9 8.9 %multiply_cosine_fusion = (f32[1024,512]{0,1:T(8,128)S(1)}, f32[1024,512]{0,1:T(8,128)}) fusion(f32[512]{0:T(512)S(1)} %multiply_exponential_fusion, f32[1024]{0:T(1024)S(1)} %convert_element_type.468), kind=kLoop, calls=%fused_computation.91 | loop fusion | flops 524288 | bytes 4200448 | tf_op jit(solution)/shard_map/cos | solution.py:67
  26.8 166.6 %gather_weights.1 = (bf16[768,3072]{1,0:T(8,128)(2,1)}, bf16[768,3072]{1,0:T(8,128)(2,1)}, bf16[3072,768]{1,0:T(8,128)(2,1)}, bf16[768,3072]{1,0:T(8,128)(2,1)},...) custom-call(bf16[96,3072]{1,0:T(8,128)(2,1)} %get-tuple-element.137., ...), custom_call_target="tpu_custom_call" | custom-call | tf_op jit(solution)/shard_map/gather_weights/pallas_call | solution.py:392
  208.8 6.3 fusion.62
  224.9 4.5 convolution_convert_fusion.7
  242.1 12.7 %fusion.10 = (bf16[320,3072]{1,0:T(8,128)(2,1)S(1)}, f32[320,3072]{1,0:T(8,128)}) fusion(bf16[768,3072]{1,0:T(8,128)(2,1)S(1)} %bitcast.350, f32[320,768]{1,0:T(8,128)S(1)} %get-tuple-element.123, f32[768]{0:T(1024)S(1)} %reshape.1170, f32[320]{0:T(512)S(1)} %add_rsqrt_fusion.2, f32[320]{0:T(512)S(1)} %broadcast_multiply_fusion.10), kind=kOutput, calls=%fused_computation.56 | convolution fusion | flops 1574830080 | bytes 11605504 | tf_op jit(solution)/shard_map/dot_general | solution.py:25
  260.6 5.3 add.406
  266.0 5.4 copy.90
  271.3 4.2 multiply_convert_fusion.6
  275.5 10.2 %fusion.247 = f32[1024,3072]{0,1:T(8,128)S(1)} fusion(bf16[1024,1024]{0,1:T(8,128)(2,1)S(1)} %multiply_convert_fusion.6, bf16[1024,3072]{1,0:T(8,128)(2,1)} %get-tuple-element.50), kind=kOutput, calls=%fused_computation.424 | convolution fusion | flops 6442450944 | bytes 20971520 | tf_op jit(solution)/shard_map/dot_general | solution.py:25
  289.3 7.9 fusion.58
  297.3 7.8 fusion.240
  317.3 5.1 multiply_convert_fusion.1
  328.6 4.1 convolution_convert_fusion.9
  338.8 6.9 fusion.237
  347.8 12.0 %multiply_multiply_fusion.1 = f32[1024,1024]{0,1:T(8,128)} fusion(bf16[1024,3072]{1,0:T(8,128)(2,1)} %get-tuple-element.50, bf16[1024,1024]{0,1:T(8,128)(2,1)S(1)} %multiply_convert_fusion.1, bf16[1024,1024]{0,1:T(8,128)(2,1)S(1)} %get-tuple-element.89, bf16[1024,1024]{0,1:T(8,128)(2,1)S(1)} %get-tuple-element.90, f32[1024,1024]{0,1:T(8,128)S(1)} %copy-done.10, ...), kind=kOutput, calls=%fused_computation.36 | convolution fusion | flops 6471811072 | bytes 25165824 | tf_op jit(solution)/shard_map/dot_general | solution.py:35
  359.8 5.4 copy.102
  365.1 5.3 reshape.1151
  370.5 4.9 reduce_sum.354
  376.0 6.6 fusion.7
  382.7 5.8 multiply_reduce_fusion.7
  390.2 7.3 fusion.116
  400.4 4.8 fusion.107
  408.8 4.6 convolution_convert_fusion.6.refs_4_
  413.4 13.0 %convolution_convert_fusion.refs_0_ = bf16[1024,3072]{1,0:T(8,128)(2,1)} fusion(bf16[1024,1024]{0,1:T(8,128)(2,1)S(1)} %copy-done.40, bf16[1024,1024]{0,1:T(8,128)(2,1)S(1)} %copy-done.42, bf16[1024,1024]{0,1:T(8,128)(2,1)S(1)} %copy-done.44, bf16[1024,1024]{0,1:T(8,128)(2,1)} %copy-done.45), kind=kOutput, calls=%fused_computation.17 | convolution fusion | flops 6464471040 | bytes 14680064 | tf_op jit(solution)/shard_map/dot_general | solution.py:29
  426.4 6.6 convolution_convert_fusion.5.refs_5_
  436.5 11.6 %fusion.104 = bf16[1,320,1,12,64]{1,4,3,2,0:T(8,128)(2,1)} fusion(f32[12,320,320]{1,2,0:T(8,128)} %fusion.141, f32[12,320,320]{1,2,0:T(8,128)} %copy-done.7, f32[12,320]{1,0:T(8,128)S(1)} %copy-done.82, bf16[1,320,3,12,64]{1,4,3,2,0:T(8,128)(2,1)S(1)} %bitcast.303), kind=kOutput, calls=%fused_computation.162 | convolution fusion | flops 168595520 | bytes 24723456 | tf_op jit(solution)/shard_map/ihqk,ikhd->iqhd/dot_general | solution.py:181
  448.2 11.8 %fusion.101 = bf16[1,320,1,12,64]{1,4,3,2,0:T(8,128)(2,1)} fusion(f32[12,320,320]{1,2,0:T(8,128)} %fusion.141, f32[12,320,320]{1,2,0:T(8,128)} %copy-done.7, f32[12,320]{1,0:T(8,128)S(1)} %copy-done.82, bf16[1,320,3,12,64]{1,4,3,2,0:T(8,128)(2,1)} %bitcast.299), kind=kOutput, calls=%fused_computation.161 | convolution fusion | flops 168595520 | bytes 24723456 | tf_op jit(solution)/shard_map/ihqk,iqhd->ikhd/dot_general | solution.py:184
  461.5 4.6 multiply_reduce_fusion.8
  473.4 5.0 multiply_reduce_fusion.15
  484.4 4.1 convolution_convert_fusion.1
  504.7 4.5 fusion.160
  528.6 277.5 %sum_gradients.1 = (bf16[128,3072]{1,0:T(8,128)(2,1)}, bf16[128,2048]{1,0:T(8,128)(2,1)}, bf16[96,1024]{1,0:T(8,128)(2,1)}, bf16[96,3072]{1,0:T(8,128)(2,1)}, bf...) custom-call(bf16[1024,3072]{1,0:T(8,128)(2,1)} %convolution_convert_, ...), custom_call_target="tpu_custom_call" | custom-call | tf_op jit(solution)/shard_map/sum_gradients/pallas_call | solution.py:655
  (410 shorter events, 167.7 us)
Async XLA Ops:
  0.7 11.3 %copy-start = (bf16[1,320,768]{2,1,0:T(8,128)(2,1)S(1)}, bf16[1,320,768]{2,1,0:T(8,128)(2,1)}, u32[]{:S(2)}) copy-start(bf16[1,320,768]{2,1,0:T(8,128)(2,1)} %param.25) | copy-start | bytes 1474564
  0.7 15.7 %copy-start.79 = (bf16[1,256,4,16]{1,3,2,0:T(8,128)(2,1)S(1)}, bf16[1,256,4,16]{1,3,2,0:T(8,128)(2,1)}, u32[]{:S(2)}) copy-start(bf16[1,256,4,16]{1,3,2,0:T(8,128)(2,1)} %param.29) | copy-start | bytes 98308
  0.7 14.8 %copy-start.72 = (bf16[128,1024]{1,0:T(8,128)(2,1)S(1)}, bf16[128,1024]{1,0:T(8,128)(2,1)}, u32[]{:S(2)}) copy-start(bf16[128,1024]{1,0:T(8,128)(2,1)} %param.48) | copy-start | bytes 786436
  0.7 14.8 %copy-start.73 = (bf16[128,1024]{1,0:T(8,128)(2,1)S(1)}, bf16[128,1024]{1,0:T(8,128)(2,1)}, u32[]{:S(2)}) copy-start(bf16[128,1024]{1,0:T(8,128)(2,1)} %param.47) | copy-start | bytes 786436
  0.7 16.0 %copy-start.78 = (bf16[96,768]{1,0:T(8,128)(2,1)S(1)}, bf16[96,768]{1,0:T(8,128)(2,1)}, u32[]{:S(2)}) copy-start(bf16[96,768]{1,0:T(8,128)(2,1)} %param.39) | copy-start | bytes 442372
  0.7 16.0 %copy-start.67 = (bf16[96,2304]{1,0:T(8,128)(2,1)S(1)}, bf16[96,2304]{1,0:T(8,128)(2,1)}, u32[]{:S(2)}) copy-start(bf16[96,2304]{1,0:T(8,128)(2,1)} %param.38) | copy-start | bytes 1327108
  0.7 16.0 %copy-start.77 = (bf16[96,768]{1,0:T(8,128)(2,1)S(1)}, bf16[96,768]{1,0:T(8,128)(2,1)}, u32[]{:S(2)}) copy-start(bf16[96,768]{1,0:T(8,128)(2,1)} %param.33) | copy-start | bytes 442372
  0.7 16.0 %copy-start.66 = (bf16[96,2304]{1,0:T(8,128)(2,1)S(1)}, bf16[96,2304]{1,0:T(8,128)(2,1)}, u32[]{:S(2)}) copy-start(bf16[96,2304]{1,0:T(8,128)(2,1)} %param.32) | copy-start | bytes 1327108
  14.3 192.2 %copy-start.22 = (bf16[140,768]{1,0:T(8,128)(2,1)}, bf16[140,768]{1,0:T(8,128)(2,1)S(1)}, u32[]{:S(2)}) copy-start(bf16[140,768]{1,0:T(8,128)(2,1)S(1)} %gather_fusion.1) | copy-start | bytes 645124
  14.4 181.3 %copy-start.94 = (f32[140]{0:T(256)}, f32[140]{0:T(256)S(1)}, u32[]{:S(2)}) copy-start(f32[140]{0:T(256)S(1)} %broadcast_multiply_fusion.17) | copy-start | bytes 1684
  14.6 181.1 %copy-start.96 = (f32[140]{0:T(256)}, f32[140]{0:T(256)S(1)}, u32[]{:S(2)}) copy-start(f32[140]{0:T(256)S(1)} %add_rsqrt_fusion.5) | copy-start | bytes 1684
  195.5 29.1 %copy-start.92 = (f32[768]{0:T(1024)}, f32[768]{0:T(1024)S(1)}, u32[]{:S(2)}) copy-start(f32[768]{0:T(1024)S(1)} %reshape.1169) | copy-start | bytes 9220
  195.5 13.2 %copy-start.74 = (f32[768]{0:T(1024)}, f32[768]{0:T(1024)S(1)}, u32[]{:S(2)}) copy-start(f32[768]{0:T(1024)S(1)} %reshape.1167) | copy-start | bytes 9220
  220.8 18.3 %copy-start.13 = (f32[1,256,768]{2,1,0:T(8,128)}, f32[1,256,768]{2,1,0:T(8,128)S(1)}, u32[]{:S(2)}) copy-start(f32[1,256,768]{2,1,0:T(8,128)S(1)} %bitcast_select_fusion) | copy-start | bytes 2359300
  239.1 15.7 %copy-start.64 = (bf16[12,64,320]{2,1,0:T(8,128)(2,1)}, bf16[12,64,320]{2,1,0:T(8,128)(2,1)S(1)}, u32[]{:S(2)}) copy-start(bf16[12,64,320]{2,1,0:T(8,128)(2,1)S(1)} %fusion.84) | copy-start | bytes 1474564
  239.1 15.7 %slice-start.6 = ((s8[4718592]{0:T(1024)(128)(4,1)}), s8[4194304]{0:T(1024)(128)(4,1)S(1)}, s32[]{:S(2)}) async-start(s8[4718592]{0:T(1024)(128)(4,1)} %bitcast.351), calls=%async_computation.6 | async-start | bytes 8388608
  241.7 13.0 %copy-start.29 = (f32[320,768]{1,0:T(8,128)}, f32[320,768]{1,0:T(8,128)S(1)}, u32[]{:S(2)}) copy-start(f32[320,768]{1,0:T(8,128)S(1)} %get-tuple-element.123) | copy-start | bytes 2949124
  242.1 12.7 %slice-start.7 = ((s8[4718592]{0:T(1024)(128)(4,1)}), s8[524288]{0:T(1024)(128)(4,1)S(1)}, s32[]{:S(2)}) async-start(s8[4718592]{0:T(1024)(128)(4,1)} %bitcast.351), calls=%async_computation.7 | async-start | bytes 1048576
  275.5 10.3 %copy-start.39 = (bf16[1024,1024]{0,1:T(8,128)(2,1)}, bf16[1024,1024]{0,1:T(8,128)(2,1)S(1)}, u32[]{:S(2)}) copy-start(bf16[1024,1024]{0,1:T(8,128)(2,1)S(1)} %multiply_convert_fusion.6) | copy-start | bytes 6291460
  275.5 10.3 %copy-start.3 = (f32[1024,1024]{0,1:T(8,128)S(1)}, f32[1024,1024]{0,1:T(8,128)}, u32[]{:S(2)}) copy-start(f32[1024,1024]{0,1:T(8,128)} %copy-done.2) | copy-start | bytes 12582916
  285.8 11.5 %copy-start.9 = (f32[1024,3072]{0,1:T(8,128)}, f32[1024,3072]{0,1:T(8,128)S(1)}, u32[]{:S(2)}) copy-start(f32[1024,3072]{0,1:T(8,128)S(1)} %fusion.247) | copy-start | bytes 37748740
  322.4 23.4 %copy-start.41 = (bf16[1024,1024]{0,1:T(8,128)(2,1)}, bf16[1024,1024]{0,1:T(8,128)(2,1)S(1)}, u32[]{:S(2)}) copy-start(bf16[1024,1024]{0,1:T(8,128)(2,1)S(1)} %multiply_convert_fusion.1) | copy-start | bytes 6291460
  376.0 12.6 %copy-start.68 = (bf16[1,256,768]{2,1,0:T(8,128)(2,1)}, bf16[1,256,768]{2,1,0:T(8,128)(2,1)S(1)}, u32[]{:S(2)}) copy-start(bf16[1,256,768]{2,1,0:T(8,128)(2,1)S(1)} %fusion.111) | copy-start | bytes 1179652
  413.4 13.0 %copy-start.69 = (bf16[1,256,768]{2,1,0:T(8,128)(2,1)S(1)}, bf16[1,256,768]{2,1,0:T(8,128)(2,1)}, u32[]{:S(2)}) copy-start(bf16[1,256,768]{2,1,0:T(8,128)(2,1)} %copy-done.68) | copy-start | bytes 1179652
  448.1 11.9 %copy-start.38 = (bf16[1,320,1,12,64]{1,4,3,2,0:T(8,128)(2,1)S(1)}, bf16[1,320,1,12,64]{1,4,3,2,0:T(8,128)(2,1)}, u32[]{:S(2)}) copy-start(bf16[1,320,1,12,64]{1,4,3,2,0:T(8,128)(2,1)} %fusion.107) | copy-start | bytes 1474564
  448.1 11.9 %copy-start.63 = (bf16[1,320,1,12,64]{1,4,3,2,0:T(8,128)(2,1)S(1)}, bf16[1,320,1,12,64]{1,4,3,2,0:T(8,128)(2,1)}, u32[]{:S(2)}) copy-start(bf16[1,320,1,12,64]{1,4,3,2,0:T(8,128)(2,1)} %fusion.104) | copy-start | bytes 1474564
  448.1 13.3 %copy-start.14 = (f32[1,256,768]{2,1,0:T(8,128)S(1)}, f32[1,256,768]{2,1,0:T(8,128)}, u32[]{:S(2)}) copy-start(f32[1,256,768]{2,1,0:T(8,128)} %copy-done.13) | copy-start | bytes 2359300
  448.1 13.3 %copy-start.35 = (f32[1,64,768]{2,1,0:T(8,128)S(1)}, f32[1,64,768]{2,1,0:T(8,128)}, u32[]{:S(2)}) copy-start(f32[1,64,768]{2,1,0:T(8,128)} %get-tuple-element.96) | copy-start | bytes 589828
  448.1 13.4 %copy-start.91 = (f32[320]{0:T(512)S(1)}, f32[320]{0:T(512)}, u32[]{:S(2)}) copy-start(f32[320]{0:T(512)} %copy-done.90) | copy-start | bytes 3844
  448.1 13.4 %copy-start.93 = (f32[768]{0:T(1024)S(1)}, f32[768]{0:T(1024)}, u32[]{:S(2)}) copy-start(f32[768]{0:T(1024)} %copy-done.92) | copy-start | bytes 9220
  448.2 13.3 %copy-start.99 = (f32[320]{0:T(512)S(1)}, f32[320]{0:T(512)}, u32[]{:S(2)}) copy-start(f32[320]{0:T(512)} %copy-done.98) | copy-start | bytes 3844
  806.1 11.3 %copy-start.62 = (bf16[96,3072]{1,0:T(8,128)(2,1)S(1)}, bf16[96,3072]{1,0:T(8,128)(2,1)}, u32[]{:S(2)}) copy-start(bf16[96,3072]{1,0:T(8,128)(2,1)} %get-tuple-element.54) | copy-start | bytes 1769476
  (82 other events, 439.5 us)

commit v2 on v1

--- a/solution.py
+++ b/solution.py
@@ -10,25 +10,18 @@
 
 MESH = pl.DeviceIdType.MESH
 SUM_VMEM = 60 * 1024 * 1024
-HEADS = 12
 HW = 1024
 CH = 16
 COPIES = 4
 STEPS_T = 1000
-ENC = 140
-
+BUFFER = 64
+SPOTS = 80
 EPSILON = 1e-06
 NEG_FILL = -1e30
 
 
 def matmul(left, right):
     return jnp.dot(left, right, preferred_element_type=jnp.float32)
-
-
-def left_trans(left, right):
-    return lax.dot_general(
-        left, right, (((0,), (0,)), ((), ())), preferred_element_type=jnp.float32
-    )
 
 
 def right_trans(left, right):
@@ -54,198 +47,544 @@
     return sigma * (1.0 + values * (1.0 - sigma))
 
 
-def gelu_slope(values):
-    cumul = 0.5 * (1.0 + lax.erf(values * (1.0 / math.sqrt(2.0))))
-    density = jnp.exp(-0.5 * values * values) * (1.0 / math.sqrt(2.0 * math.pi))
-    return cumul + values * density
-
-
-def time_embed(steps):
-    half_width = HW // 2
-    freqs = jnp.exp(-math.log(10000.0) * jnp.arange(half_width, dtype=jnp.float32) / half_width)
-    phase = steps.astype(jnp.float32)[..., None] * freqs
-    return jnp.concatenate([jnp.cos(phase), jnp.sin(phase)], axis=-1)
-
-
 def noise_angle(steps):
     return (steps.astype(jnp.float32) / STEPS_T + 0.008) / 1.008 * (math.pi / 2)
 
 
-def pick_rows(table, index):
-    return table[index]
-
-
-def place_rows(base, index, values):
-    return base.at[index].set(values, mode="drop")
-
-
-def inverse_order(order_row):
-    return (
-        jnp.zeros(order_row.shape, jnp.int32)
-        .at[order_row]
-        .set(jnp.arange(order_row.shape[0], dtype=jnp.int32))
-    )
-
-
-def attention_scores(qkv_proj, key_valid, head_size):
-    raw_scores = jnp.einsum(
-        "iqhd,ikhd->ihqk", qkv_proj[:, :, 0], qkv_proj[:, :, 1], preferred_element_type=jnp.float32
-    )
-    return jnp.where(key_valid[:, None, None, :], raw_scores * head_size ** (-0.5), NEG_FILL)
-
-
-def block_forward(stream, key_valid, weights):
-    gain_one, w_qkv, w_proj, gain_two, w_up, w_down = weights
-    images, row_count, width = stream.shape
-    head_size = width // HEADS
-    flat = stream.reshape(images * row_count, width)
-    normed_one, inv_one = norm_rows(flat)
-    ln_one = (normed_one * gain_one.astype(jnp.float32)).astype(jnp.bfloat16)
-    qkv_proj = (
-        matmul(ln_one, w_qkv).astype(jnp.bfloat16).reshape(images, row_count, 3, HEADS, head_size)
-    )
-    scores = attention_scores(qkv_proj, key_valid, head_size)
-    top_score = jnp.max(scores, axis=-1, keepdims=True)
-    exp_scores = jnp.exp(scores - top_score)
-    exp_total = jnp.sum(exp_scores, axis=-1, keepdims=True)
-    log_total = top_score + jnp.log(exp_total)
-    attn_probs = (exp_scores / exp_total).astype(jnp.bfloat16)
-    mixed = jnp.einsum(
-        "ihqk,ikhd->iqhd", attn_probs, qkv_proj[:, :, 2], preferred_element_type=jnp.float32
-    )
-    mixed = mixed.astype(jnp.bfloat16).reshape(images * row_count, width)
-    middle = flat + matmul(mixed, w_proj)
-    normed_two, inv_two = norm_rows(middle)
-    ln_two = (normed_two * gain_two.astype(jnp.float32)).astype(jnp.bfloat16)
-    up_proj = matmul(ln_two, w_up)
-    up_act = jax.nn.gelu(up_proj, approximate=False).astype(jnp.bfloat16)
-    result = middle + matmul(up_act, w_down)
-    kept = (
-        normed_one,
-        inv_one,
-        ln_one,
-        qkv_proj,
-        log_total,
-        mixed,
-        normed_two,
-        inv_two,
-        ln_two,
-        up_proj,
-        up_act,
-    )
-    return (result.reshape(images, row_count, width), kept)
-
-
-def block_backward(grad_out, key_valid, weights, kept):
-    gain_one, w_qkv, w_proj, gain_two, w_up, w_down = weights
-    (
-        normed_one,
-        inv_one,
-        ln_one,
-        qkv_proj,
-        log_total,
-        mixed,
-        normed_two,
-        inv_two,
-        ln_two,
-        up_proj,
-        up_act,
-    ) = kept
-    images, row_count, width = grad_out.shape
-    head_size = width // HEADS
-    grad_flat = grad_out.reshape(images * row_count, width)
-    grad_low = grad_flat.astype(jnp.bfloat16)
-    grad_w_down = left_trans(up_act, grad_low)
-    grad_act = right_trans(grad_low, w_down)
-    grad_up = (grad_act * gelu_slope(up_proj)).astype(jnp.bfloat16)
-    grad_w_up = left_trans(ln_two, grad_up)
-    grad_ln_two = right_trans(grad_up, w_up)
-    grad_gain_two = jnp.sum(grad_ln_two * normed_two, axis=0)
-    grad_mid = grad_flat + norm_back(
-        grad_ln_two * gain_two.astype(jnp.float32), normed_two, inv_two
-    )
-    grad_mid_low = grad_mid.astype(jnp.bfloat16)
-    grad_w_proj = left_trans(mixed, grad_mid_low)
-    grad_mixed = (
-        right_trans(grad_mid_low, w_proj)
-        .astype(jnp.bfloat16)
-        .reshape(images, row_count, HEADS, head_size)
-    )
-    scores = attention_scores(qkv_proj, key_valid, head_size)
-    attn_probs = jnp.exp(scores - log_total)
-    grad_probs = jnp.einsum(
-        "iqhd,ikhd->ihqk", grad_mixed, qkv_proj[:, :, 2], preferred_element_type=jnp.float32
-    )
-    row_dot = jnp.sum(grad_probs * attn_probs, axis=-1, keepdims=True)
-    grad_scores = (attn_probs * (grad_probs - row_dot) * head_size ** (-0.5)).astype(jnp.bfloat16)
-    grad_query = jnp.einsum(
-        "ihqk,ikhd->iqhd", grad_scores, qkv_proj[:, :, 1], preferred_element_type=jnp.float32
-    )
-    grad_key = jnp.einsum(
-        "ihqk,iqhd->ikhd", grad_scores, qkv_proj[:, :, 0], preferred_element_type=jnp.float32
-    )
-    grad_value = jnp.einsum(
-        "ihqk,iqhd->ikhd",
-        attn_probs.astype(jnp.bfloat16),
-        grad_mixed,
-        preferred_element_type=jnp.float32,
-    )
-    grad_qkv = jnp.stack([grad_query, grad_key, grad_value], axis=2)
-    grad_qkv = grad_qkv.reshape(images * row_count, 3 * width).astype(jnp.bfloat16)
-    grad_w_qkv = left_trans(ln_one, grad_qkv)
-    grad_ln_one = right_trans(grad_qkv, w_qkv)
-    grad_gain_one = jnp.sum(grad_ln_one * normed_one, axis=0)
-    grad_in = grad_mid + norm_back(grad_ln_one * gain_one.astype(jnp.float32), normed_one, inv_one)
-    grads = (grad_gain_one, grad_w_qkv, grad_w_proj, grad_gain_two, grad_w_up, grad_w_down)
-    return (grad_in.reshape(images, row_count, width), grads)
-
-
-def head_step(cond_rows, live, noisy, noise_vals, steps, weights):
-    w_in, w_cond, w_ada, w_inner, w_outer, w_out = weights
-    row_count = cond_rows.shape[0]
-    flat_count = row_count * COPIES
-    cond = matmul(cond_rows, w_cond)
-    cond_full = (cond[:, None, :] + time_embed(steps)).reshape(flat_count, HW)
-    cond_act = jax.nn.silu(cond_full).astype(jnp.bfloat16)
-    modulate = matmul(cond_act, w_ada)
-    shift_part = modulate[:, :HW]
-    scale_part = modulate[:, HW : 2 * HW]
-    gate_part = modulate[:, 2 * HW :]
-    hidden = matmul(noisy, w_in)
-    normed_in, inv_in = norm_rows(hidden)
-    mlp_in = (normed_in * (1.0 + scale_part) + shift_part).astype(jnp.bfloat16)
-    inner = matmul(mlp_in, w_inner)
-    inner_act = jax.nn.silu(inner).astype(jnp.bfloat16)
-    branch = matmul(inner_act, w_outer)
-    hidden_two = hidden + gate_part * branch
-    normed_out, inv_out = norm_rows(hidden_two)
-    final_in = normed_out.astype(jnp.bfloat16)
-    error = matmul(final_in, w_out) - noise_vals
-    row_loss = jnp.sum((error * error).reshape(row_count, COPIES * CH), axis=1).astype(jnp.bfloat16)
-    live_flat = jnp.broadcast_to(live[:, None], (row_count, COPIES)).reshape(flat_count, 1)
-    grad_pred = jnp.where(live_flat, error * (2.0 / COPIES), 0.0).astype(jnp.bfloat16)
-    grad_w_out = left_trans(final_in, grad_pred)
-    grad_two = norm_back(right_trans(grad_pred, w_out), normed_out, inv_out)
-    grad_branch = (grad_two * gate_part).astype(jnp.bfloat16)
-    grad_gate = grad_two * branch
-    grad_w_outer = left_trans(inner_act, grad_branch)
-    grad_inner = (right_trans(grad_branch, w_outer) * silu_slope(inner)).astype(jnp.bfloat16)
-    grad_w_inner = left_trans(mlp_in, grad_inner)
-    grad_mlp_in = right_trans(grad_inner, w_inner)
-    grad_hidden = (
-        grad_two + norm_back(grad_mlp_in * (1.0 + scale_part), normed_in, inv_in)
-    ).astype(jnp.bfloat16)
-    grad_w_in = left_trans(noisy, grad_hidden)
-    grad_mod = jnp.concatenate([grad_mlp_in, grad_mlp_in * normed_in, grad_gate], axis=1).astype(
-        jnp.bfloat16
-    )
-    grad_w_ada = left_trans(cond_act, grad_mod)
-    grad_cond_full = right_trans(grad_mod, w_ada) * silu_slope(cond_full)
-    grad_cond = jnp.sum(grad_cond_full.reshape(row_count, COPIES, HW), axis=1).astype(jnp.bfloat16)
-    grad_w_cond = left_trans(cond_rows, grad_cond)
-    grad_rows = right_trans(grad_cond, w_cond).astype(jnp.bfloat16)
-    grads = (grad_w_in, grad_w_cond, grad_w_ada, grad_w_inner, grad_w_outer, grad_w_out)
-    return (grads, grad_rows, row_loss)
+ROOT_HALF = 1.0 / math.sqrt(2.0)
+TILE = 512
+STEP = 16
+
+
+def rows_dot(left, right):
+    return lax.dot_general(left, right, (((0,), (0,)), ((), ())), preferred_element_type=jnp.float32)
+
+
+def loop(count, body):
+    def turn(i, carry):
+        body(i)
+        return carry
+
+    lax.fori_loop(0, count, turn, 0)
+
+
+def at_step(i, size=STEP):
+    return pl.ds(pl.multiple_of(i * size, size), size)
+
+
+def at_col(i, size):
+    return pl.ds(pl.multiple_of(i * size, 128), size)
+
+
+def exact_dot(ones, values):
+    high = values.astype(jnp.bfloat16)
+    rest = values - high.astype(jnp.float32)
+    middle = rest.astype(jnp.bfloat16)
+    low = (rest - middle.astype(jnp.float32)).astype(jnp.bfloat16)
+    return matmul(ones, high) + matmul(ones, middle) + matmul(ones, low)
+
+
+def scale_norm(source, gain, target):
+    normed, _ = norm_rows(source[...])
+    target[...] = (normed * gain).astype(jnp.bfloat16)
+
+
+def head_mask(half):
+    lane = lax.broadcasted_iota(jnp.int32, (1, 128), 1)
+    return (lane < 64) if half == 0 else (lane >= 64)
+
+
+def keep_half(values, half):
+    return jnp.where(head_mask(half), values, jnp.zeros((), values.dtype))
+
+
+def probabilities(query, key, half, bias):
+    scores = right_trans(keep_half(query, half), key) * 0.125
+    if bias is not None:
+        scores = jnp.where(bias, scores, NEG_FILL)
+    grown = jnp.exp(scores - jnp.max(scores, axis=-1, keepdims=True))
+    return grown / jnp.sum(grown, axis=-1, keepdims=True)
+
+
+def forward_steps(width, stream, gain_one, gain_two, w_a, w_up, w_down, qkv, mixed, middle, up, out, low, live=None):
+    def project(j):
+        cols = pl.ds(j * width, width)
+        qkv[:, cols] = matmul(low[...], w_a[:, cols]).astype(jnp.bfloat16)
+
+    def attend(pair):
+        query, key, value = (qkv[:, pl.ds(pair * 128 + part * width, 128)] for part in range(3))
+        parts = [
+            matmul(probabilities(query, key, half, live).astype(jnp.bfloat16), value) for half in range(2)
+        ]
+        mixed[:, pl.ds(pair * 128, 128)] = jnp.where(head_mask(0), parts[0], parts[1]).astype(jnp.bfloat16)
+
+    def mix():
+        middle[...] = stream[...] + matmul(mixed[...], w_a[:, 3 * width :])
+        scale_norm(middle, gain_two, low)
+
+    def feed(j):
+        cols = pl.ds(j * TILE, TILE)
+        raised = matmul(low[...], w_up[:, cols])
+        up[:, cols] = raised
+        act = (raised * (0.5 + 0.5 * lax.erf(raised * ROOT_HALF))).astype(jnp.bfloat16)
+        out[...] = (middle[...] if j == 0 else out[...]) + matmul(act, w_down[cols, :])
+
+    yield lambda: scale_norm(stream, gain_one, low)
+    for j in range(3):
+        yield functools.partial(project, j)
+    for pair in range(width // 128):
+        yield functools.partial(attend, pair)
+    yield mix
+    for j in range(w_up.shape[1] // TILE):
+        yield functools.partial(feed, j)
+
+
+def forward_block(*args):
+    for step in forward_steps(*args):
+        step()
+
+
+def forward_kernel(*refs):
+    (embedded, vis_col, vis_row, vec, e_a_hbm, e_u_hbm, e_d_hbm, d_a_hbm, d_u_hbm, d_d_hbm,
+     e_in, e_qkv, e_mixed, e_mid, e_up, d_in, d_qkv, d_mixed, d_mid, d_up, acts,
+     e_a, e_u, e_d, d_a, d_u, d_d, e_out, d_out, e_low, d_low, sems) = refs
+    width = embedded.shape[1]
+    loads = [
+        pltpu.make_async_copy(a, b, sems.at[i])
+        for i, (a, b) in enumerate(
+            [(e_a_hbm, e_a), (e_u_hbm, e_u), (e_d_hbm, e_d), (d_a_hbm, d_a), (d_u_hbm, d_u), (d_d_hbm, d_d)]
+        )
+    ]
+    for load in loads:
+        load.start()
+    encode(embedded, vis_col, vec, e_in)
+    for load in loads[:3]:
+        load.wait()
+    live = live_keys(vis_row)
+    forward_block(width, e_in, vec[0:1, :], vec[1:2, :], e_a, e_u, e_d, e_qkv, e_mixed, e_mid, e_up, e_out, e_low, live)
+    spread_rows(vis_row, e_out, vec, d_in)
+    for load in loads[3:]:
+        load.wait()
+    forward_block(width, d_in, vec[2:3, :], vec[3:4, :], d_a, d_u, d_d, d_qkv, d_mixed, d_mid, d_up, d_out, d_low)
+    acts[...] = d_out[...].astype(jnp.bfloat16)
+
+
+def token_hot(vis_col, count):
+    return (lax.broadcasted_iota(jnp.int32, (vis_col.shape[0], count), 1) == vis_col[...]).astype(jnp.bfloat16)
+
+
+def spot_hot(vis_row, count):
+    return (lax.broadcasted_iota(jnp.int32, (count, vis_row.shape[1]), 0) == vis_row[...]).astype(jnp.bfloat16)
+
+
+def live_keys(vis_row):
+    ones = jnp.ones((1, BUFFER), jnp.int32)
+    return jnp.concatenate([ones, (vis_row[...] >= 0).astype(jnp.int32)], axis=1) > 0
+
+
+def encode(embedded, vis_col, vec, target):
+    tokens = embedded.shape[0] - BUFFER
+    target[:BUFFER, :] = embedded[:BUFFER, :].astype(jnp.float32)
+    target[BUFFER:, :] = matmul(token_hot(vis_col, tokens), embedded[BUFFER:, :])
+
+
+def spread_rows(vis_row, enc_out, vec, target):
+    tokens = target.shape[0] - BUFFER
+    hot = spot_hot(vis_row, tokens)
+    masked = 1.0 - jnp.sum(hot.astype(jnp.float32), axis=1, keepdims=True)
+    target[:BUFFER, :] = enc_out[:BUFFER, :]
+    target[BUFFER:, :] = exact_dot(hot, enc_out[BUFFER:, :]) + masked * vec[4:5, :]
+
+
+def forward_blocks(embedded, vis_col, vis_row, vec, weights):
+    tokens, width = embedded.shape
+    inner = weights[1].shape[1]
+    rows = BUFFER + vis_col.shape[0]
+    f32, half = jnp.float32, jnp.bfloat16
+
+    def kept(count):
+        return [
+            jax.ShapeDtypeStruct((count, width), f32),
+            jax.ShapeDtypeStruct((count, 3 * width), half),
+            jax.ShapeDtypeStruct((count, width), half),
+            jax.ShapeDtypeStruct((count, width), f32),
+            jax.ShapeDtypeStruct((count, inner), f32),
+        ]
+
+    outs = kept(rows) + kept(tokens) + [jax.ShapeDtypeStruct((tokens, width), half)]
+    whole = pl.BlockSpec(memory_space=pltpu.VMEM)
+    found = pl.pallas_call(
+        forward_kernel,
+        out_shape=outs,
+        in_specs=[whole] * 4 + [pl.BlockSpec(memory_space=pl.ANY)] * 6,
+        out_specs=[whole] * len(outs),
+        scratch_shapes=[pltpu.VMEM(w.shape, half) for w in weights]
+        + [
+            pltpu.VMEM((rows, width), f32),
+            pltpu.VMEM((tokens, width), f32),
+            pltpu.VMEM((rows, width), half),
+            pltpu.VMEM((tokens, width), half),
+            pltpu.SemaphoreType.DMA((6,)),
+        ],
+        compiler_params=pltpu.CompilerParams(vmem_limit_bytes=SUM_VMEM),
+        name="forward_blocks",
+    )(embedded, vis_col, vis_row, vec, *weights)
+    return found[:5], found[5:10], found[10]
+
+
+def norm_back_into(grads, source, gain, add, target, gain_grad):
+    normed, inv_std = norm_rows(source[...])
+    grad = grads[...]
+    gain_grad[...] = jnp.sum(grad * normed, axis=0, keepdims=True)
+    target[...] = add[...] + norm_back(grad * gain, normed, inv_std)
+
+
+class Tiles:
+    def __init__(self, slots, sems):
+        self.slots, self.sems = slots, sems
+
+    def put(self, i, value, target):
+        slot = i % 2 if isinstance(i, int) else lax.rem(i, 2)
+        copy = pltpu.make_async_copy(self.slots.at[slot], target, self.sems.at[slot])
+
+        @pl.when(i >= 2)
+        def _():
+            copy.wait()
+
+        self.slots[slot] = value.astype(jnp.bfloat16)
+        copy.start()
+
+    def flush(self, like):
+        for slot in range(2):
+            pltpu.make_async_copy(self.slots.at[slot], like, self.sems.at[slot]).wait()
+
+
+def backward_block(width, grad, stream, gain_one, gain_two, w_a, w_up, w_down, qkv, mixed, middle, up,
+                   d_a, d_up, d_down, d_one, d_two, grad_low, low, grad_qkv, acc, grad_mid, out, tiles, live=None):
+    rows = grad.shape[0]
+    wide, narrow, square = tiles
+    grad_low[...] = grad[...].astype(jnp.bfloat16)
+    scale_norm(middle, gain_two, low)
+    acc[...] = jnp.zeros_like(acc)
+    count = w_up.shape[1] // TILE
+
+    def feed(j):
+        raised = up[:, at_col(j, TILE)]
+        cumul = 0.5 + 0.5 * lax.erf(raised * ROOT_HALF)
+        slope = cumul + raised * (jnp.exp(-0.5 * raised * raised) * (1.0 / math.sqrt(2.0 * math.pi)))
+        act = (raised * cumul).astype(jnp.bfloat16)
+        down = w_down[at_step(j, TILE), :]
+        narrow.put(j, rows_dot(act, grad_low[...]), d_down.at[at_step(j, TILE), :])
+        grad_up = (right_trans(grad_low[...], down) * slope).astype(jnp.bfloat16)
+        wide.put(j, rows_dot(low[...], grad_up), d_up.at[:, at_col(j, TILE)])
+        acc[...] += right_trans(grad_up, w_up[:, at_col(j, TILE)])
+
+    loop(count, feed)
+    narrow.flush(d_down.at[pl.ds(0, TILE), :])
+    wide.flush(d_up.at[:, pl.ds(0, TILE)])
+    norm_back_into(acc, middle, gain_two, grad, grad_mid, d_two)
+    grad_low[...] = grad_mid[...].astype(jnp.bfloat16)
+    for j in range(width // 256):
+        square.put(j, rows_dot(mixed[...], grad_low[:, pl.ds(j * 256, 256)]), d_a.at[:, pl.ds(3 * width + j * 256, 256)])
+    for j in range(width // 256):
+        low[:, pl.ds(j * 256, 256)] = right_trans(grad_low[...], w_a[pl.ds(j * 256, 256), pl.ds(3 * width, width)]).astype(jnp.bfloat16)
+
+    def attend(pair):
+        where = [pl.ds(pl.multiple_of(pair * 128 + part * width, 128), 128) for part in range(3)]
+        query, key, value = (qkv[:, at] for at in where)
+        grad_mixed = low[:, at_col(pair, 128)]
+        found = []
+        for half in range(2):
+            probs = probabilities(query, key, half, live)
+            grad_half = keep_half(grad_mixed, half)
+            grad_probs = right_trans(grad_half, value)
+            dots = jnp.sum(grad_probs * probs, axis=-1, keepdims=True)
+            grad_scores = (probs * (grad_probs - dots) * 0.125).astype(jnp.bfloat16)
+            found.append(
+                (matmul(grad_scores, key), rows_dot(grad_scores, query), rows_dot(probs.astype(jnp.bfloat16), grad_half))
+            )
+        for part in range(3):
+            both = jnp.where(head_mask(0), found[0][part], found[1][part])
+            grad_qkv[:, where[part]] = both.astype(jnp.bfloat16)
+
+    loop(width // 128, attend)
+    scale_norm(stream, gain_one, low)
+    acc[...] = jnp.zeros_like(acc)
+    first = width // 256
+
+    def project(j):
+        piece = grad_qkv[:, at_col(j, 256)]
+        square.put(j + first, rows_dot(low[...], piece), d_a.at[:, at_col(j, 256)])
+        acc[...] += right_trans(piece, w_a[:, at_col(j, 256)])
+
+    loop(3 * width // 256, project)
+    square.flush(d_a.at[:, pl.ds(0, 256)])
+    norm_back_into(acc, stream, gain_one, grad_mid, out, d_one)
+
+
+def backward_kernel(*refs):
+    (grad_rows, vis_col, vis_row, vec, e_in, e_qkv, e_mixed, e_mid, e_up, d_in, d_qkv, d_mixed, d_mid, d_up,
+     e_a_hbm, e_u_hbm, e_d_hbm, d_a_hbm, d_u_hbm, d_d_hbm,
+     embed_grad, small, de_a, de_u, de_d, dd_a, dd_u, dd_d,
+     e_a, e_u, e_d, d_a, d_u, d_d, d_grad, e_grad, low_a, low_b, grad_qkv, acc, grad_mid,
+     wide, narrow, square, load_sems, tile_sems) = refs
+    tokens, width = d_in.shape
+    rows = e_in.shape[0]
+    loads = [
+        pltpu.make_async_copy(a, b, load_sems.at[i])
+        for i, (a, b) in enumerate(
+            [(d_d_hbm, d_d), (d_u_hbm, d_u), (d_a_hbm, d_a), (e_d_hbm, e_d), (e_u_hbm, e_u), (e_a_hbm, e_a)]
+        )
+    ]
+    for load in loads:
+        load.start()
+    tiles = (Tiles(wide, tile_sems.at[0]), Tiles(narrow, tile_sems.at[1]), Tiles(square, tile_sems.at[2]))
+    d_grad[:BUFFER, :] = jnp.zeros((BUFFER, width), jnp.float32)
+    d_grad[BUFFER:, :] = grad_rows[...].astype(jnp.float32)
+    for load in loads[:3]:
+        load.wait()
+    backward_block(width, d_grad, d_in, vec[2:3, :], vec[3:4, :], d_a, d_u, d_d, d_qkv, d_mixed, d_mid, d_up,
+                   dd_a, dd_u, dd_d, small.at[2:3, :], small.at[3:4, :], low_a, low_b, grad_qkv, acc, grad_mid, d_grad, tiles)
+    hot = spot_hot(vis_row, tokens - BUFFER)
+    masked = 1.0 - jnp.sum(hot.astype(jnp.float32), axis=1, keepdims=True)
+    small[4:5, :] = jnp.sum(d_grad[BUFFER:, :] * masked, axis=0, keepdims=True)
+    e_grad[:BUFFER, :] = d_grad[:BUFFER, :]
+    e_grad[BUFFER:, :] = exact_dot(token_hot(vis_col, tokens - BUFFER), d_grad[BUFFER:, :])
+    for load in loads[3:]:
+        load.wait()
+    part = pl.ds(0, rows)
+    backward_block(width, e_grad, e_in, vec[0:1, :], vec[1:2, :], e_a, e_u, e_d, e_qkv, e_mixed, e_mid, e_up,
+                   de_a, de_u, de_d, small.at[0:1, :], small.at[1:2, :], low_a.at[part], low_b.at[part],
+                   grad_qkv.at[part], acc.at[part], grad_mid.at[part], e_grad, tiles, live_keys(vis_row))
+    embed_grad[:BUFFER, :] = e_grad[:BUFFER, :]
+    embed_grad[BUFFER:, :] = exact_dot(hot, e_grad[BUFFER:, :])
+
+
+def backward_blocks(grad_rows, vis_col, vis_row, vec, enc_kept, dec_kept, weights):
+    tokens, width = dec_kept[0].shape
+    rows = enc_kept[0].shape[0]
+    f32, half = jnp.float32, jnp.bfloat16
+    whole, anywhere = pl.BlockSpec(memory_space=pltpu.VMEM), pl.BlockSpec(memory_space=pl.ANY)
+    outs = [jax.ShapeDtypeStruct((tokens, width), f32), jax.ShapeDtypeStruct((8, width), f32)]
+    outs += [jax.ShapeDtypeStruct(w.shape, half) for w in weights]
+    found = pl.pallas_call(
+        backward_kernel,
+        out_shape=outs,
+        in_specs=[whole] * 14 + [anywhere] * 6,
+        out_specs=[whole] * 2 + [anywhere] * 6,
+        scratch_shapes=[pltpu.VMEM(w.shape, half) for w in weights]
+        + [
+            pltpu.VMEM((tokens, width), f32),
+            pltpu.VMEM((rows, width), f32),
+            pltpu.VMEM((tokens, width), half),
+            pltpu.VMEM((tokens, width), half),
+            pltpu.VMEM((tokens, 3 * width), half),
+            pltpu.VMEM((tokens, width), f32),
+            pltpu.VMEM((tokens, width), f32),
+            pltpu.VMEM((2, width, TILE), half),
+            pltpu.VMEM((2, TILE, width), half),
+            pltpu.VMEM((2, width, 256), half),
+            pltpu.SemaphoreType.DMA((6,)),
+            pltpu.SemaphoreType.DMA((3, 2)),
+        ],
+        compiler_params=pltpu.CompilerParams(vmem_limit_bytes=SUM_VMEM),
+        name="backward_blocks",
+    )(grad_rows, vis_col, vis_row, vec, *enc_kept, *dec_kept, *weights)
+    return found[0], found[1], found[2:]
+
+
+def embed_steps(steps, freqs, target):
+    half = freqs.shape[1]
+
+    def body(i):
+        phase = steps[at_step(i), :].astype(jnp.float32) * freqs[...]
+        target[at_step(i), :half] = jnp.cos(phase)
+        target[at_step(i), half:] = jnp.sin(phase)
+
+    loop(steps.shape[0] // STEP, body)
+
+
+ROWS = 128
+
+
+def at_rows(i):
+    return pl.ds(pl.multiple_of(i * ROWS, 16), ROWS)
+
+
+def head_kernel(*refs):
+    (acts, vis_row, targets, noise, steps, embeds, w_cond_hbm, w_ada_hbm, w_io_hbm, w_in, w_out,
+     grad_rows, losses, d_in, d_out, d_cond, d_ada, d_io,
+     w_cond, w_ada, w_io, cond, cond_full, mod, hidden, normed_in, inv_in, inner, branch, normed_out, inv_out,
+     work, grad_two, grad_sum, noisy, cond_act, mlp_in, inner_act, final_in, grad_pred, grad_branch, grad_inner,
+     grad_hidden, grad_mod, wide, load_sems, tile_sems) = refs
+    tokens, wide_cols = targets.shape[0], w_in.shape[1]
+    loads = [
+        pltpu.make_async_copy(a, b, load_sems.at[i])
+        for i, (a, b) in enumerate([(w_cond_hbm, w_cond), (w_ada_hbm, w_ada), (w_io_hbm, w_io)])
+    ]
+    for load in loads:
+        load.start()
+    hot = spot_hot(vis_row, tokens)
+    masked = jnp.sum(hot.astype(jnp.float32), axis=1, keepdims=True) < 0.5
+    loads[0].wait()
+    cond[...] = matmul(acts[BUFFER:, :], w_cond[...])
+    loads[1].wait()
+    loads[2].wait()
+    grad_sum[...] = jnp.zeros_like(grad_sum)
+    columns = wide_cols // 256
+
+    def copy_pass(c, loss):
+        rows = pl.ds(pl.multiple_of(c * tokens, 16), tokens)
+
+        def at(i):
+            return pl.ds(pl.multiple_of(c * tokens + i * ROWS, 16), ROWS)
+
+        angle = noise_angle(steps[rows, :])
+        noise_vals = noise[rows, :].astype(jnp.float32)
+        noisy[rows, :] = (jnp.cos(angle) * targets[...] + jnp.sin(angle) * noise_vals).astype(jnp.bfloat16)
+
+        def condition(i):
+            full = cond[at_rows(i), :] + embeds[at(i), :]
+            cond_full[at_rows(i), :] = full
+            cond_act[at(i), :] = (full * jax.nn.sigmoid(full)).astype(jnp.bfloat16)
+
+        loop(tokens // ROWS, condition)
+
+        def modulate(j):
+            mod[:, at_col(j, wide_cols)] = matmul(cond_act[rows, :], w_ada[:, at_col(j, wide_cols)])
+
+        loop(3, modulate)
+        hidden[...] = matmul(noisy[rows, :], w_in[...])
+
+        def enter(i):
+            normed, inv_std = norm_rows(hidden[at_rows(i), :])
+            normed_in[at_rows(i), :] = normed
+            inv_in[at_rows(i), :] = inv_std
+            shift, scale = mod[at_rows(i), :wide_cols], mod[at_rows(i), wide_cols : 2 * wide_cols]
+            mlp_in[at(i), :] = (normed * (1.0 + scale) + shift).astype(jnp.bfloat16)
+
+        loop(tokens // ROWS, enter)
+
+        inner[...] = matmul(mlp_in[rows, :], w_io[:, :wide_cols])
+
+        def activate(i):
+            values = inner[at_rows(i), :]
+            inner_act[at(i), :] = (values * jax.nn.sigmoid(values)).astype(jnp.bfloat16)
+
+        loop(tokens // ROWS, activate)
+
+        branch[...] = matmul(inner_act[rows, :], w_io[:, wide_cols:])
+
+        def leave(i):
+            gate = mod[at_rows(i), 2 * wide_cols :]
+            normed, inv_std = norm_rows(hidden[at_rows(i), :] + gate * branch[at_rows(i), :])
+            normed_out[at_rows(i), :] = normed
+            inv_out[at_rows(i), :] = inv_std
+            final_in[at(i), :] = normed.astype(jnp.bfloat16)
+
+        loop(tokens // ROWS, leave)
+        error = right_trans(final_in[rows, :], w_out[...]) - noise_vals
+        loss = loss + jnp.sum(error * error, axis=1, keepdims=True)
+        low_error = jnp.where(masked, error * (2.0 / COPIES), 0.0).astype(jnp.bfloat16)
+        grad_pred[rows, :] = low_error
+        work[...] = matmul(low_error, w_out[...])
+
+        def back_out(i):
+            gate = mod[at_rows(i), 2 * wide_cols :]
+            grad = norm_back(work[at_rows(i), :], normed_out[at_rows(i), :], inv_out[at_rows(i), :])
+            grad_two[at_rows(i), :] = grad
+            grad_branch[at(i), :] = (grad * gate).astype(jnp.bfloat16)
+            grad_mod[at(i), 2 * wide_cols :] = (grad * branch[at_rows(i), :]).astype(jnp.bfloat16)
+
+        loop(tokens // ROWS, back_out)
+
+        work[...] = right_trans(grad_branch[rows, :], w_io[:, wide_cols:])
+
+        def back_act(i):
+            grad_inner[at(i), :] = (work[at_rows(i), :] * silu_slope(inner[at_rows(i), :])).astype(jnp.bfloat16)
+
+        loop(tokens // ROWS, back_act)
+
+        work[...] = right_trans(grad_inner[rows, :], w_io[:, :wide_cols])
+
+        def back_in(i):
+            grad, normed = work[at_rows(i), :], normed_in[at_rows(i), :]
+            scale = mod[at_rows(i), wide_cols : 2 * wide_cols]
+            grad_mod[at(i), :wide_cols] = grad.astype(jnp.bfloat16)
+            grad_mod[at(i), wide_cols : 2 * wide_cols] = (grad * normed).astype(jnp.bfloat16)
+            total = grad_two[at_rows(i), :] + norm_back(grad * (1.0 + scale), normed, inv_in[at_rows(i), :])
+            grad_hidden[at(i), :] = total.astype(jnp.bfloat16)
+
+        loop(tokens // ROWS, back_in)
+
+        def back_mod(j):
+            work[:, at_col(j, 256)] = right_trans(grad_mod[rows, :], w_ada[at_step(j, 256), :])
+
+        loop(columns, back_mod)
+
+        def back_cond(i):
+            grad_sum[at_rows(i), :] += work[at_rows(i), :] * silu_slope(cond_full[at_rows(i), :])
+
+        loop(tokens // ROWS, back_cond)
+        return loss
+
+    loss = lax.fori_loop(0, COPIES, copy_pass, jnp.zeros((tokens, 1), jnp.float32))
+    loss = jnp.where(masked, loss.astype(jnp.bfloat16).astype(jnp.float32), 0.0)
+    losses[...] = jnp.broadcast_to(jnp.sum(loss, axis=0, keepdims=True), losses.shape)
+    grad_cond = grad_sum[...].astype(jnp.bfloat16)
+    grad_rows[...] = right_trans(grad_cond, w_cond[...]).astype(jnp.bfloat16)
+    tiles = Tiles(wide, tile_sems)
+
+    def out_ada(j):
+        tiles.put(j, rows_dot(cond_act[...], grad_mod[:, at_col(j, TILE)]), d_ada.at[:, at_col(j, TILE)])
+
+    count = 3 * wide_cols // TILE
+    loop(count, out_ada)
+    half = wide_cols // TILE
+
+    def out_inner(j):
+        tiles.put(j + count, rows_dot(mlp_in[...], grad_inner[:, at_col(j, TILE)]), d_io.at[:, at_col(j, TILE)])
+
+    def out_outer(j):
+        tiles.put(j + count + half, rows_dot(inner_act[...], grad_branch[:, at_col(j, TILE)]), d_io.at[:, at_col(j + half, TILE)])
+
+    loop(half, out_inner)
+    loop(half, out_outer)
+    d_cond[...] = rows_dot(acts[BUFFER:, :], grad_cond).astype(jnp.bfloat16)
+    d_in[...] = rows_dot(noisy[...], grad_hidden[...])
+    d_out[...] = rows_dot(grad_pred[...], final_in[...])
+    tiles.flush(d_ada.at[:, pl.ds(0, TILE)])
+
+
+def head_pass(acts, vis_row, targets, noise, steps, embeds, w_cond, w_ada, w_io, w_in, w_out):
+    tokens, width = targets.shape[0], acts.shape[1]
+    wide, flat = w_in.shape[1], noise.shape[0]
+    f32, half = jnp.float32, jnp.bfloat16
+    whole, anywhere = pl.BlockSpec(memory_space=pltpu.VMEM), pl.BlockSpec(memory_space=pl.ANY)
+    shape = jax.ShapeDtypeStruct
+    outs = [
+        shape((tokens, width), half), shape((8, 128), f32), shape((CH, wide), f32), shape((CH, wide), f32),
+        shape(w_cond.shape, half), shape(w_ada.shape, half), shape(w_io.shape, half),
+    ]
+    tile = lambda cols, kind=f32: pltpu.VMEM((tokens, cols), kind)
+    long = lambda cols: pltpu.VMEM((flat, cols), half)
+    return pl.pallas_call(
+        head_kernel,
+        out_shape=outs,
+        in_specs=[whole] * 6 + [anywhere] * 3 + [whole] * 2,
+        out_specs=[whole] * 5 + [anywhere] * 2,
+        scratch_shapes=[pltpu.VMEM(w.shape, half) for w in (w_cond, w_ada, w_io)]
+        + [
+            tile(wide), tile(wide), tile(3 * wide), tile(wide), tile(wide), tile(1), tile(wide), tile(wide), tile(wide), tile(1),
+            tile(wide), tile(wide), tile(wide),
+            long(CH), long(wide), long(wide), long(wide), long(wide), long(CH), long(wide), long(wide), long(wide), long(3 * wide),
+            pltpu.VMEM((2, wide, TILE), half),
+            pltpu.SemaphoreType.DMA((3,)),
+            pltpu.SemaphoreType.DMA((2,)),
+        ],
+        compiler_params=pltpu.CompilerParams(vmem_limit_bytes=SUM_VMEM),
+        name="head_pass",
+    )(acts, vis_row, targets, noise, steps, embeds, w_cond, w_ada, w_io, w_in, w_out)
 
 
 class Slab:
@@ -680,30 +1019,269 @@
     )(*grads)
 
 
+class Gathering:
+    def __init__(self, slabs, depth, mine, whole, sems):
+        self.slabs, self.depth, self.mine, self.whole = slabs, depth, mine, whole
+        self.sent, self.got, self.own_sent, self.own_got, self.own_copy = sems
+        self.group, self.level, self.core, self.flip = place(depth)
+        me = 2 * self.level + self.core
+        self.peers = ((self.flip(0), me), (self.flip(1), me), (self.group, 2 * self.level + 1 - self.core))
+        self.items = [(k, step) for k in range(len(slabs)) for step in range(1, depth)]
+        self.turn = 0
+        self.turns = len(self.items) + 2
+
+    def level_at(self, step):
+        return lax.rem(self.level + step + self.depth, self.depth)
+
+    def move(self, kind, item, source, target, device):
+        return pltpu.make_async_remote_copy(
+            src_ref=source,
+            dst_ref=target,
+            send_sem=self.sent.at[kind, item],
+            recv_sem=self.got.at[kind, item],
+            device_id=device,
+            device_id_type=MESH,
+        )
+
+    def z_peer(self, step):
+        return (self.group, 2 * self.level_at(step) + self.core)
+
+    def along_z(self, item):
+        k, step = self.items[item]
+        slab = self.slabs[k]
+        target = self.whole[k].at[slab.spot(2 * self.level + self.core, self.group)]
+        return self.move(0, item, self.mine[k].at[slab.within(self.group)], target, self.z_peer(step))
+
+    def onward(self, kind, item, quarter, half, device):
+        k, step = self.items[item]
+        shard = 2 * self.level_at(-step) + self.core
+        here = self.whole[k].at[self.slabs[k].spot(shard, quarter, half)]
+        return self.move(kind, item, here, here, device)
+
+    def to_core(self, item, core):
+        k, step = self.items[item]
+        here = self.whole[k].at[self.slabs[k].shard(2 * self.level_at(-step) + core)]
+        return self.move(5, item, here, here, self.peers[2])
+
+    def own(self, k):
+        target = self.whole[k].at[self.slabs[k].shard(2 * self.level + self.core)]
+        share = pltpu.make_async_remote_copy(
+            src_ref=self.mine[k],
+            dst_ref=target,
+            send_sem=self.own_sent.at[k],
+            recv_sem=self.own_got.at[k],
+            device_id=self.peers[2],
+            device_id_type=MESH,
+        )
+        return pltpu.make_async_copy(self.mine[k], target, self.own_copy.at[k]), share
+
+    def start(self):
+        greet([*self.peers, *(self.z_peer(step) for step in range(1, self.depth))])
+        for item in range(len(self.items)):
+            self.along_z(item).start()
+            if self.items[item][1] == 1:
+                for copy in self.own(self.items[item][0]):
+                    copy.start()
+
+    def pump(self, until):
+        group, flip = self.group, self.flip
+        x_peer, y_peer, _ = self.peers
+        total = len(self.items)
+        while self.turn < min(until, self.turns):
+            item = self.turn
+            if item < total:
+                self.onward(0, item, group, None, x_peer).wait_recv()
+                self.onward(1, item, group, None, x_peer).start()
+                self.onward(2, item, group, None, y_peer).start()
+            item = self.turn - 1
+            if 0 <= item < total:
+                self.onward(1, item, flip(0), None, x_peer).wait_recv()
+                self.onward(4, item, flip(0), 0, y_peer).start()
+                self.onward(2, item, flip(1), None, y_peer).wait_recv()
+                self.onward(3, item, flip(1), 1, x_peer).start()
+            item = self.turn - 2
+            if 0 <= item < total:
+                self.onward(4, item, 3 - group, 0, y_peer).wait_recv()
+                self.onward(3, item, 3 - group, 1, x_peer).wait_recv()
+                self.to_core(item, self.core).start()
+            self.turn += 1
+
+    def ready_at(self, k):
+        return (k + 1) * (self.depth - 1) + 2
+
+    def take(self, k):
+        self.pump(self.ready_at(k))
+        for item, (slab, _) in enumerate(self.items):
+            if slab == k:
+                self.to_core(item, 1 - self.core).wait_recv()
+        keep, share = self.own(k)
+        keep.wait()
+        share.wait_recv()
+
+    def finish(self):
+        group, flip = self.group, self.flip
+        x_peer, y_peer, _ = self.peers
+        for item in range(len(self.items)):
+            self.along_z(item).wait_send()
+            self.onward(1, item, group, None, x_peer).wait_send()
+            self.onward(2, item, group, None, y_peer).wait_send()
+            self.onward(4, item, flip(0), 0, y_peer).wait_send()
+            self.onward(3, item, flip(1), 1, x_peer).wait_send()
+            self.to_core(item, self.core).wait_send()
+        for k in range(len(self.slabs)):
+            self.own(k)[1].wait_send()
+
+
+def unpack_vectors(small, parts, width, vec):
+    piece = width // parts
+    vec[...] = jnp.zeros_like(vec)
+    lane = lax.broadcasted_iota(jnp.int32, (128, width), 0)
+    col = lax.broadcasted_iota(jnp.int32, (128, width), 1)
+    for part in range(parts):
+        spread = ((col == lane + part * piece) & (lane < piece)).astype(jnp.bfloat16)
+        vec[...] += matmul(small[pl.ds(part * SMALL_ROWS, CH), :128], spread)
+
+
+def first_kernel(slabs, depth, *refs):
+    count = len(slabs)
+    mine, refs = refs[:count], refs[count:]
+    embedded, vis_col, vis_row, steps, freqs = refs[:5]
+    whole, refs = refs[5 : 5 + count], refs[5 + count :]
+    kept_hbm, (acts, vec, w_in, w_out, embeds_hbm), refs = refs[:10], refs[10:15], refs[15:]
+    sems, refs = refs[:5], refs[5:]
+    small, (e_a, e_u, e_d, d_a, d_u, d_d) = refs[0], refs[1:7]
+    e_kept, d_kept = refs[7:12], refs[12:17]
+    embeds, e_out, d_out, e_low, d_low, load_sems, kept_sems = refs[17:]
+    width = embedded.shape[1]
+    parts = 2 * depth
+    gathering = Gathering(slabs, depth, mine, whole, sems)
+    gathering.start()
+    half, height = freqs.shape[1], 64
+    pieces = steps.shape[0] // height
+    enc_turn, dec_turn = gathering.ready_at(3), gathering.ready_at(6)
+    encode(embedded, vis_col, None, e_kept[0])
+    for piece in range(pieces):
+        gathering.pump(piece * enc_turn // pieces)
+        rows = pl.ds(piece * height, height)
+        phase = steps[rows, :].astype(jnp.float32) * freqs[...]
+        embeds[rows, :half] = jnp.cos(phase)
+        embeds[rows, half:] = jnp.sin(phase)
+    copies = [pltpu.make_async_copy(embeds, embeds_hbm, kept_sems.at[10])]
+    copies[0].start()
+
+    def fetch(slots):
+        loads = []
+        for slab, target in slots:
+            gathering.take(slab)
+            load = pltpu.make_async_copy(whole[slab], target, load_sems.at[slab])
+            load.start()
+            loads.append(load)
+        return loads
+
+    def run(steps_of, turn, last):
+        steps_of = list(steps_of)
+        for i, step in enumerate(steps_of):
+            step()
+            gathering.pump(turn + (last - turn) * (i + 1) // len(steps_of))
+
+    def keep(kept, at):
+        for i, buffer in enumerate(kept):
+            copy = pltpu.make_async_copy(buffer, kept_hbm[at + i], kept_sems.at[at + i])
+            copy.start()
+            copies.append(copy)
+
+    for load in fetch([(0, small), (1, e_a), (2, e_u), (3, e_d)]):
+        load.wait()
+    unpack_vectors(small, parts, width, vec)
+    for part in range(parts):
+        block = pl.ds(part * SMALL_ROWS, CH)
+        w_in[:, pl.ds(part * 128, 128)] = small[block, pl.ds(128, 128)]
+        w_out[:, pl.ds(part * 128, 128)] = small[block, pl.ds(256, 128)]
+    live = live_keys(vis_row)
+    run(forward_steps(width, e_kept[0], vec[0:1, :], vec[1:2, :], e_a, e_u, e_d, *e_kept[1:], e_out, e_low, live), enc_turn, dec_turn)
+    keep(e_kept, 0)
+    spread_rows(vis_row, e_out, vec, d_kept[0])
+    for load in fetch([(4, d_a), (5, d_u), (6, d_d)]):
+        load.wait()
+    run(forward_steps(width, d_kept[0], vec[2:3, :], vec[3:4, :], d_a, d_u, d_d, *d_kept[1:], d_out, d_low), dec_turn, gathering.turns)
+    keep(d_kept, 5)
+    acts[...] = d_out[...].astype(jnp.bfloat16)
+    for slab in range(7, count):
+        gathering.take(slab)
+    gathering.finish()
+    for copy in copies:
+        copy.wait()
+
+
+def first_part(shards, slabs, depth, embedded, vis_col, vis_row, steps, freqs):
+    tokens, width = embedded.shape
+    count, items = len(slabs), len(slabs) * (depth - 1)
+    inner = slabs[2].cols
+    rows = BUFFER + vis_col.shape[0]
+    flat, wide = steps.shape[0], 2 * freqs.shape[1]
+    f32, half = jnp.float32, jnp.bfloat16
+    whole, anywhere = pl.BlockSpec(memory_space=pltpu.VMEM), pl.BlockSpec(memory_space=pl.ANY)
+    shape, dma = jax.ShapeDtypeStruct, pltpu.SemaphoreType.DMA
+    gathered = [shape((2 * depth * s.rows, s.cols), half) for s in slabs]
+
+    def kept(height):
+        return [
+            shape((height, width), f32),
+            shape((height, 3 * width), half),
+            shape((height, width), half),
+            shape((height, width), f32),
+            shape((height, inner), f32),
+        ]
+
+    saved = kept(rows) + kept(tokens)
+    outs = gathered + saved
+    outs += [shape((tokens, width), half), shape((CH, width), f32), shape((CH, wide), half), shape((CH, wide), half), shape((flat, wide), f32)]
+    found = pl.pallas_call(
+        functools.partial(first_kernel, slabs, depth),
+        out_shape=outs,
+        in_specs=[anywhere] * count + [whole] * 5,
+        out_specs=[anywhere] * (count + 10) + [whole] * 4 + [anywhere],
+        scratch_shapes=[dma((6, items)), dma((6, items)), dma((count,)), dma((count,)), dma((count,))]
+        + [pltpu.VMEM(s.shape, s.dtype) for s in (*gathered[:7], *saved)]
+        + [
+            pltpu.VMEM((flat, wide), f32),
+            pltpu.VMEM((rows, width), f32),
+            pltpu.VMEM((tokens, width), f32),
+            pltpu.VMEM((rows, width), half),
+            pltpu.VMEM((tokens, width), half),
+            dma((count,)),
+            dma((11,)),
+        ],
+        compiler_params=pltpu.CompilerParams(collective_id=0, has_side_effects=True, vmem_limit_bytes=SUM_VMEM),
+        name="gather_and_forward",
+    )(*shards, embedded, vis_col, vis_row, steps, freqs)
+    slabs_found, found = found[:count], found[count:]
+    return slabs_found, found[:5], found[5:10], *found[10:]
+
+
 SMALL_ROWS, SMALL_COLS = 32, 512
 
 
 def pack_small(vectors, first, last):
     parts = vectors[0].shape[0] // 96
     lanes = jnp.stack([v.reshape(parts, 96) for v in vectors], axis=1)
-    lanes = jnp.pad(lanes, ((0, 0), (0, 16 - len(vectors)), (0, 128 - 96)))
-    first = first.reshape(CH, parts, 128).transpose(1, 0, 2)
-    last = last.reshape(parts, 128, CH).transpose(0, 2, 1)
-    packed = jnp.concatenate([lanes, first, last], axis=2)
-    packed = jnp.pad(packed, ((0, 0), (0, SMALL_ROWS - 16), (0, SMALL_COLS - 384)))
+    lanes = jnp.pad(lanes, ((0, 0), (0, CH - len(vectors)), (0, 128 - 96)))
+    wide = [w.reshape(CH, parts, 128).transpose(1, 0, 2) for w in (first, last)]
+    packed = jnp.concatenate([lanes, *wide], axis=2)
+    packed = jnp.pad(packed, ((0, 0), (0, SMALL_ROWS - CH), (0, SMALL_COLS - 384)))
     return packed.reshape(parts * SMALL_ROWS, SMALL_COLS)
 
 
 def unpack_small(packed):
     parts = packed.shape[0] // SMALL_ROWS
     packed = packed.reshape(parts, SMALL_ROWS, SMALL_COLS)
-    vectors = [packed[:, i, :96].reshape(parts * 96) for i in range(5)]
-    first = packed[:, :CH, 128:256].transpose(1, 0, 2).reshape(CH, parts * 128)
-    last = packed[:, :CH, 256:384].transpose(0, 2, 1).reshape(parts * 128, CH)
-    return vectors, first, last
+    vectors = packed[:, :5, :96].transpose(1, 0, 2).reshape(5, parts * 96)
+    wide = [packed[:, :CH, 128 * i : 128 * i + 128].transpose(1, 0, 2).reshape(CH, parts * 128) for i in (1, 2)]
+    return vectors, wide[0], wide[1]
 
 
 SLABS = (
+    Slab(SMALL_ROWS, SMALL_COLS, False),
     Slab(96, 3072, False),
     Slab(96, 3072, False),
     Slab(384, 768, True),
@@ -713,148 +1291,90 @@
     Slab(96, 1024, False),
     Slab(128, 3072, False),
     Slab(128, 2048, False),
-    Slab(32, 512, False),
 )
 
 
-def gather_weights(shards):
+def by_links():
+    return lax.axis_size("dev") == 8 and lax.axis_size("grp") == 4
+
+
+def packed_shards(shards):
     (e_one, e_qkv, e_proj, e_two, e_up, e_down, d_one, d_qkv, d_proj, d_two, d_up, d_down, fill, h_in, h_cond, h_ada, h_inner, h_outer, h_out) = shards
-    if lax.axis_size("dev") != 8 or lax.axis_size("grp") != 4:
-        whole = [lax.all_gather(w, "dev", axis=0, tiled=True) for w in shards]
-        whole[13] = lax.all_gather(h_in, "dev", axis=1, tiled=True)
-        return whole
-    depth = lax.axis_size("dev") // 2
-    packed = (
+    large = (
         jnp.concatenate([e_qkv, e_proj], axis=1), e_up, e_down,
         jnp.concatenate([d_qkv, d_proj], axis=1), d_up, d_down,
         h_cond, h_ada, jnp.concatenate([h_inner, h_outer], axis=1),
-        pack_small([e_one, e_two, d_one, d_two, fill], h_in, h_out),
     )
-    ea, eu, ed, da, du, dd, hc, ha, hio, small = gather_slabs(packed, SLABS, depth)
-    (e_one, e_two, d_one, d_two, fill), h_in, h_out = unpack_small(small)
-    split = e_qkv.shape[1]
-    return [e_one, ea[:, :split], ea[:, split:], e_two, eu, ed, d_one, da[:, :split], da[:, split:], d_two, du, dd, fill,
-            h_in, hc, ha, hio[:, :HW], hio[:, HW:], h_out]
-
-
-def sum_gradients(grads):
-    low = [g.astype(jnp.bfloat16) for g in grads]
-    (e_one, e_qkv, e_proj, e_two, e_up, e_down, d_one, d_qkv, d_proj, d_two, d_up, d_down, fill, h_in, h_cond, h_ada, h_inner, h_outer, h_out) = low
-    if lax.axis_size("dev") != 8 or lax.axis_size("grp") != 4:
-        sums = [lax.psum_scatter(g, "dev", scatter_dimension=int(i == 13), tiled=True) for i, g in enumerate(grads)]
-        return [lax.psum(g.astype(jnp.bfloat16), "grp").astype(jnp.float32) for g in sums]
-    depth = lax.axis_size("dev") // 2
-    packed = (
-        jnp.concatenate([e_qkv, e_proj], axis=1), e_up, e_down,
-        jnp.concatenate([d_qkv, d_proj], axis=1), d_up, d_down,
-        h_cond, h_ada, jnp.concatenate([h_inner, h_outer], axis=1),
-        pack_small([e_one, e_two, d_one, d_two, fill], h_in, h_out),
-    )
-    turn = (7, 8, 6, 3, 4, 5, 0, 1, 2, 9)
-    orders = ("xy", "yx", "zx", "xy", "yx", "zx", "yx", "xy", "yx", "xy")
-    sums = sum_slabs([packed[t] for t in turn], [SLABS[t] for t in turn], [orders[t] for t in turn], depth)
-    back = [None] * len(turn)
-    for t, s in zip(turn, sums, strict=True):
-        back[t] = s.astype(jnp.float32)
-    ea, eu, ed, da, du, dd, hc, ha, hio, small = back
-    (e_one, e_two, d_one, d_two, fill), h_in, h_out = unpack_small(small)
-    split = e_qkv.shape[1]
-    return [e_one, ea[:, :split], ea[:, split:], e_two, eu, ed, d_one, da[:, :split], da[:, split:], d_two, du, dd, fill,
-            h_in, hc, ha, hio[:, :HW], hio[:, HW:], h_out]
-
-
-def per_device(
-    embedded,
-    mask_order,
-    counts,
-    targets,
-    noise_copies,
-    timesteps,
-    enc_gain_one,
-    enc_qkv,
-    enc_proj,
-    enc_gain_two,
-    enc_up,
-    enc_down,
-    dec_gain_one,
-    dec_qkv,
-    dec_proj,
-    dec_gain_two,
-    dec_up,
-    dec_down,
-    mask_token,
-    head_in,
-    head_cond,
-    head_ada,
-    head_inner,
-    head_outer,
-    head_out,
-):
+    return large, [e_one, e_two, d_one, d_two, fill], h_in, h_out
+
+
+def gather_weights(shards):
+    packed, vectors, h_in, h_out = packed_shards(shards)
+    whole = lambda w, axis=0: lax.all_gather(w, "dev", axis=axis, tiled=True)
+    return [whole(w) for w in packed], whole(jnp.stack(vectors), 1), whole(h_in, 1), whole(h_out).T
+
+
+def sum_gradients(slabs, vectors, d_in, d_out):
+    if by_links():
+        packed = (pack_small(list(vectors), d_in, d_out).astype(jnp.bfloat16), *slabs)
+        turn = (8, 9, 7, 4, 5, 6, 1, 2, 3, 0)
+        orders = ("xy", "yx", "zx", "xy", "yx", "zx", "yx", "xy", "yx", "xy")
+        sums = sum_slabs([packed[t] for t in turn], [SLABS[t] for t in turn], [orders[t] for t in turn], lax.axis_size("dev") // 2)
+        back = [None] * len(turn)
+        for t, s in zip(turn, sums, strict=True):
+            back[t] = s
+        small, *slabs = back
+        vectors, d_in, d_out = unpack_small(small)
+    else:
+
+        def scatter(grad, axis=0):
+            part = lax.psum_scatter(grad.astype(jnp.float32), "dev", scatter_dimension=axis, tiled=True)
+            return lax.psum(part.astype(jnp.bfloat16), "grp")
+
+        slabs = [scatter(g) for g in slabs]
+        vectors, d_in, d_out = scatter(vectors, 1), scatter(d_in, 1), scatter(d_out, 1)
+    ea, eu, ed, da, du, dd, hc, ha, hio = (s.astype(jnp.float32) for s in slabs)
+    vectors, d_in, d_out = (s.astype(jnp.float32) for s in (vectors, d_in, d_out))
+    split = 3 * ed.shape[1]
+    return (vectors[0], ea[:, :split], ea[:, split:], vectors[1], eu, ed, vectors[2], da[:, :split], da[:, split:], vectors[3], du, dd,
+            vectors[4], d_in, hc, ha, hio[:, :HW], hio[:, HW:], d_out.T)
+
+
+def per_device(embedded, mask_order, counts, targets, noise_copies, timesteps, *shards):
     images, tokens, width = embedded.shape
     seq_len = mask_order.shape[1]
-    buffer = tokens - seq_len
-    visible_max = ENC - buffer
-    seen = gather_weights(
-        (enc_gain_one, enc_qkv, enc_proj, enc_gain_two, enc_up, enc_down,
-         dec_gain_one, dec_qkv, dec_proj, dec_gain_two, dec_up, dec_down, mask_token,
-         head_in, head_cond, head_ada, head_inner, head_outer, head_out)
-    )
-    enc_weights, dec_weights, token_fill = seen[:6], seen[6:12], seen[12].astype(jnp.float32)
-    head_weights = seen[13:]
-    spots = jnp.arange(visible_max, dtype=jnp.int32)
-    spot_src = jnp.minimum(counts[:, None] + spots[None, :], seq_len - 1)
-    vis_tokens = jnp.take_along_axis(mask_order, spot_src, axis=1)
-    spot_live = spots[None, :] < (seq_len - counts)[:, None]
-    buffer_rows = jnp.arange(buffer, dtype=jnp.int32)[None, :]
-    enc_rows = jnp.concatenate([buffer_rows, buffer + vis_tokens], axis=1)
-    enc_in = jax.vmap(pick_rows)(embedded, enc_rows).astype(jnp.float32)
-    enc_valid = jnp.concatenate([jnp.ones((images, buffer), bool), spot_live], axis=1)
-    enc_out, enc_kept = block_forward(enc_in, enc_valid, enc_weights)
-    rank = jax.vmap(inverse_order)(mask_order)
-    visible = rank >= counts[:, None]
-    enc_source = buffer + jnp.clip(rank - counts[:, None], 0, visible_max - 1)
-    tok_rows = jnp.where(
-        visible[..., None], jax.vmap(pick_rows)(enc_out, enc_source), token_fill[None, None, :]
-    )
-    dec_in = jnp.concatenate([enc_out[:, :buffer], tok_rows], axis=1)
-    dec_valid = jnp.ones((images, tokens), bool)
-    dec_out, dec_kept = block_forward(dec_in, dec_valid, dec_weights)
-    activations = dec_out.astype(jnp.bfloat16)
-    masked = ~visible.reshape(images * seq_len)
-    angle = noise_angle(timesteps)
-    noise_vals = noise_copies.astype(jnp.float32)
-    noisy = jnp.cos(angle)[..., None] * targets[:, :, None, :] + jnp.sin(angle)[..., None] * noise_vals
-    flat_count = images * seq_len * COPIES
-    head_grads, grad_rows, row_loss = head_step(
-        activations[:, buffer:].reshape(images * seq_len, width),
-        masked,
-        noisy.astype(jnp.bfloat16).reshape(flat_count, CH),
-        noise_vals.reshape(flat_count, CH),
-        timesteps.reshape(images * seq_len, COPIES),
-        head_weights,
-    )
-    image_loss = jnp.sum(jnp.where(masked, row_loss.astype(jnp.float32), 0.0).reshape(images, seq_len), axis=1)
-    image_loss = image_loss / (counts.astype(jnp.float32) * (COPIES * CH))
-    grad_dec = jnp.concatenate(
-        [jnp.zeros((images, buffer, width), jnp.float32), grad_rows.astype(jnp.float32).reshape(images, seq_len, width)],
-        axis=1,
-    )
-    grad_dec_in, dec_grads = block_backward(
-        grad_dec, dec_valid, dec_weights, dec_kept
-    )
-    grad_tok = grad_dec_in[:, buffer:]
-    fill_grad = jnp.sum(jnp.where(visible[..., None], 0.0, grad_tok), axis=(0, 1))
-    grad_vis = jnp.where(spot_live[..., None], jax.vmap(pick_rows)(grad_tok, vis_tokens), 0.0)
-    grad_enc_out = jnp.concatenate([grad_dec_in[:, :buffer], grad_vis], axis=1)
-    grad_enc_in, enc_grads = block_backward(grad_enc_out, enc_valid, enc_weights, enc_kept)
-    token_grad = jax.vmap(place_rows)(
-        jnp.zeros((images, seq_len, width), jnp.float32),
-        jnp.where(spot_live, vis_tokens, seq_len),
-        grad_enc_in[:, buffer:],
-    )
-    embed_grad = jnp.concatenate([grad_enc_in[:, :buffer], token_grad], axis=1)
-    final_grads = sum_gradients([*enc_grads, *dec_grads, fill_grad, *head_grads])
-    return (image_loss, activations, embed_grad, *final_grads)
+    linked = by_links() and images == 1
+    if not linked:
+        slabs, vectors, w_in, w_out = gather_weights(shards)
+        vec = jnp.pad(vectors.astype(jnp.float32), ((0, CH - 5), (0, 0)))
+    freqs = jnp.exp(-math.log(10000.0) * jnp.arange(HW // 2, dtype=jnp.float32) / (HW // 2)).reshape(1, HW // 2)
+    losses, acts_of, embed_grads, totals = [], [], [], None
+    for image in range(images):
+        padded = jnp.concatenate([mask_order[image], jnp.full((SPOTS,), -1, jnp.int32)])
+        seen = lax.dynamic_slice(padded, (counts[image],), (SPOTS,))
+        vis_col, vis_row = seen.reshape(SPOTS, 1), seen.reshape(1, SPOTS)
+        steps = timesteps[image].T.reshape(COPIES * seq_len, 1)
+        noise = noise_copies[image].transpose(1, 0, 2).reshape(COPIES * seq_len, CH)
+        if linked:
+            packed, vectors, h_in, h_out = packed_shards(shards)
+            (_, *slabs), enc_kept, dec_kept, acts, vec, w_in, w_out, embeds = first_part(
+                (pack_small(vectors, h_in, h_out.T), *packed), SLABS, lax.axis_size("dev") // 2,
+                embedded[image], vis_col, vis_row, steps, freqs,
+            )
+        else:
+            phase = steps.astype(jnp.float32) * freqs
+            embeds = jnp.concatenate([jnp.cos(phase), jnp.sin(phase)], axis=1)
+            enc_kept, dec_kept, acts = forward_blocks(embedded[image], vis_col, vis_row, vec, slabs[:6])
+        grad_rows, loss, d_in, d_out, *head_grads = head_pass(
+            acts, vis_row, targets[image], noise, steps, embeds, *slabs[6:], w_in, w_out
+        )
+        embed_grad, small, block_grads = backward_blocks(grad_rows, vis_col, vis_row, vec, enc_kept, dec_kept, slabs[:6])
+        found = ([*block_grads, *head_grads], small[:5], d_in, d_out)
+        totals = found if totals is None else jax.tree.map(jnp.add, totals, found)
+        losses.append(loss[0, 0] / (counts[image].astype(jnp.float32) * (COPIES * CH)))
+        acts_of.append(acts)
+        embed_grads.append(embed_grad)
+    return (jnp.stack(losses), jnp.stack(acts_of), jnp.stack(embed_grads), *sum_gradients(*totals))
 
 
 def solution(mesh):

time: 831 us -> 671 us (0.81)
  matrix products: 231 us -> 0 us
  Pallas kernels: 444 us -> 625 us
  other arithmetic: 74.1 us -> 16 us
  local copies, waits for them, and re-layouts: 70.4 us -> 17 us
    dot_general x53 -> x0, matrix products: 231 us -> none  [the longest x14 62.1 us: matmul(): return jnp.dot(left, right, preferred_element_type=jnp.float32)]
    pallas_call x1 -> x3, Pallas kernels: 167 us -> 337 us  [the longest x1 183 us: first_part(): pl.pallas_call(functools.partial(first_kernel, slabs, depth), out_shape=o...]
    convert_element_type x13 -> x7, other arithmetic: 22.2 us -> 8.35 us  [the longest x6 7.55 us: sum_gradients(): ea, eu, ed, da, du, dd, hc, ha, hio = (s.astype(jnp.float32) for s in slabs)]
    add x3 -> x0, local copies, waits for them, and re-layouts: 13.8 us -> none  [head_step(): cond_full = (cond[:, None, :] + time_embed(steps)).reshape(flat_count, HW)]
    pallas_call x1, Pallas kernels: 278 us -> 288 us  [sum_slabs(): pl.pallas_call(functools.partial(sum_kernel, slabs, orders, depth), out_s...]
    reduce_sum x14 -> x0, other arithmetic: 10.2 us -> none  [the longest x1 4.9 us: head_step(): jnp.sum(grad_cond_full.reshape(row_count, COPIES, HW), axis=1)]
    convert_element_type x18 -> x0, local copies, waits for them, and re-layouts: 9.46 us -> none  [the longest x2 5.96 us: block_forward(): matmul(ln_one, w_qkv).astype(jnp.bfloat16)]
    cos x1 -> x0, other arithmetic: 8.87 us -> none  [time_embed(): return jnp.concatenate([jnp.cos(phase), jnp.sin(phase)], axis=-1)]
where the time goes in v2:
time: 671 us; the launch traced here: 662 us
  Pallas kernels  625 us (93%)
  local copies, waits for them, and re-layouts  17 us (3%)
  other arithmetic  16 us (2%)
    pallas_call x1, Pallas kernels, sum_slabs(): pl.pallas_call(functools.partial(sum_kernel, slabs, orders, depth), out_s...  288 us
    pallas_call x1, Pallas kernels, first_part(): pl.pallas_call(functools.partial(first_kernel, slabs, depth), out_shape=o...  183 us
    pallas_call x1, Pallas kernels, backward_blocks(): pl.pallas_call(backward_kernel, out_shape=outs, in_specs=[whole] * 14 + [...  81.1 us
    pallas_call x1, Pallas kernels, head_pass(): pl.pallas_call(head_kernel, out_shape=outs, in_specs=[whole] * 6 + [anywh...  73.2 us

profile of v2, /device:TPU:24, one launch (start us, length us, event | category | flops | bytes accessed | tf_op | source)
XLA Modules:
  0.0 661.8 jit_solution(2902553937430409371)
XLA Ops:
  0.7 0.7 stack.16
  1.4 0.7 fusion.5
  2.1 0.6 pad_bitcast_fusion.refs_0_
  2.7 2.4 pad_maximum_fusion
  5.1 1.9 pad_maximum_fusion.2.refs_9_
  7.7 1.3 fusion.7
  9.0 0.7 copy.58.refs_11_.refs_1_
  9.7 0.7 copy.73
  10.4 1.0 copy.74
  12.1 182.8 %gather_and_forward.1 = (bf16[256,512]{1,0:T(8,128)(2,1)}, bf16[768,3072]{1,0:T(8,128)(2,1)}, bf16[768,3072]{1,0:T(8,128)(2,1)}, bf16[3072,768]{1,0:T(8,128)(2,1...) custom-call(bf16[32,512]{1,0:T(8,128)(2,1)} %pad_bitcast_fusion.refs, ...), custom_call_target="tpu_custom_call" | custom-call | tf_op jit(solution)/shard_map/gather_and_forward/pallas_call | solution.py:1239
  194.9 0.8 copy.60
  195.6 0.8 copy.61
  196.5 73.2 %head_pass.1 = (bf16[256,768]{1,0:T(8,128)(2,1)}, f32[8,128]{1,0:T(8,128)}, f32[16,1024]{1,0:T(8,128)}, f32[16,1024]{1,0:T(8,128)}, bf16[768,1024]{1,0:T(8,128)(...) custom-call(bf16[320,768]{1,0:T(8,128)(2,1)} %get-tuple-element.71.refs_0_, ...), custom_call_target="tpu_custom_call" | custom-call | tf_op jit(solution)/shard_map/head_pass/pallas_call | solution.py:571
  269.6 1.2 slice.56
  271.5 81.1 %backward_blocks.1 = (f32[320,768]{1,0:T(8,128)}, f32[8,768]{1,0:T(8,128)}, bf16[768,3072]{1,0:T(8,128)(2,1)}, bf16[768,3072]{1,0:T(8,128)(2,1)}, bf16[3072,768]...) custom-call(bf16[256,768]{1,0:T(8,128)(2,1)} %get-tuple-element.79.refs_0_, ...), custom_call_target="tpu_custom_call" | custom-call | tf_op jit(solution)/shard_map/backward_blocks/pallas_call | solution.py:370
  352.6 0.7 convert.35
  353.9 0.7 pad.22
  354.7 288.1 %sum_gradients.1 = (bf16[128,3072]{1,0:T(8,128)(2,1)}, bf16[128,2048]{1,0:T(8,128)(2,1)}, bf16[96,1024]{1,0:T(8,128)(2,1)}, bf16[96,3072]{1,0:T(8,128)(2,1)}, bf...) custom-call(bf16[1024,3072]{1,0:T(8,128)(2,1)} %get-tuple-element.98, ...), custom_call_target="tpu_custom_call" | custom-call | tf_op jit(solution)/shard_map/sum_gradients/pallas_call | solution.py:994
  642.8 0.8 slice_convert_fusion
  644.1 2.0 slice.72
  646.1 1.7 slice.73
  647.8 2.2 convert_element_type.59
  650.0 1.1 convert_element_type.60
  651.1 1.0 slice.74
  652.1 0.7 slice.75
  652.8 1.1 convert_element_type.62
  653.9 1.1 convert_element_type.63
  655.0 1.3 convert_bitcast_fusion.2
  656.3 0.8 convert_element_type.66
  657.1 1.3 convert_element_type.67
  658.4 1.1 fusion.9
  659.5 0.8 copy.79
  (36 shorter events, 1.7 us)
Async XLA Ops:
  5.1 189.7 %copy-start.11 = (f32[1,256,16]{1,2,0:T(8,128)S(1)}, f32[1,256,16]{1,2,0:T(8,128)}, u32[]{:S(2)}) copy-start(f32[1,256,16]{1,2,0:T(8,128)} %param.28) | copy-start | bytes 49156
  5.1 190.5 %copy-start.10 = (bf16[1,256,4,16]{1,3,2,0:T(8,128)(2,1)S(1)}, bf16[1,256,4,16]{1,3,2,0:T(8,128)(2,1)}, u32[]{:S(2)}) copy-start(bf16[1,256,4,16]{1,3,2,0:T(8,128)(2,1)} %param.29) | copy-start | bytes 98308
  271.5 82.4 %copy-start.9 = (f32[16,1024]{1,0:T(8,128)S(1)}, f32[16,1024]{1,0:T(8,128)}, u32[]{:S(2)}) copy-start(f32[16,1024]{1,0:T(8,128)} %get-tuple-element.109) | copy-start | bytes 196612
  271.5 82.4 %copy-start.8 = (f32[16,1024]{1,0:T(8,128)S(1)}, f32[16,1024]{1,0:T(8,128)}, u32[]{:S(2)}) copy-start(f32[16,1024]{1,0:T(8,128)} %get-tuple-element.108) | copy-start | bytes 196612
  642.8 7.2 %copy-start.6 = (bf16[384,768]{1,0:T(8,128)(2,1)S(1)}, bf16[384,768]{1,0:T(8,128)(2,1)}, u32[]{:S(2)}) copy-start(bf16[384,768]{1,0:T(8,128)(2,1)} %get-tuple-element.113) | copy-start | bytes 1769476
  642.8 8.3 %copy-start = (bf16[96,3072]{1,0:T(8,128)(2,1)S(1)}, bf16[96,3072]{1,0:T(8,128)(2,1)}, u32[]{:S(2)}) copy-start(bf16[96,3072]{1,0:T(8,128)(2,1)} %get-tuple-element.114) | copy-start | bytes 1769476
  642.8 10.0 %copy-start.5 = (bf16[96,3072]{1,0:T(8,128)(2,1)S(1)}, bf16[96,3072]{1,0:T(8,128)(2,1)}, u32[]{:S(2)}) copy-start(bf16[96,3072]{1,0:T(8,128)(2,1)} %get-tuple-element.115) | copy-start | bytes 1769476
  646.1 7.8 %copy-start.4 = (bf16[384,768]{1,0:T(8,128)(2,1)S(1)}, bf16[384,768]{1,0:T(8,128)(2,1)}, u32[]{:S(2)}) copy-start(bf16[384,768]{1,0:T(8,128)(2,1)} %get-tuple-element.116) | copy-start | bytes 1769476
  650.0 6.3 copy-start.7
  650.0 7.1 %copy-start.3 = (bf16[128,3072]{1,0:T(8,128)(2,1)S(1)}, bf16[128,3072]{1,0:T(8,128)(2,1)}, u32[]{:S(2)}) copy-start(bf16[128,3072]{1,0:T(8,128)(2,1)} %get-tuple-element.118) | copy-start | bytes 2359300
  651.1 7.3 %copy-start.1 = (bf16[128,2048]{1,0:T(8,128)(2,1)S(1)}, bf16[128,2048]{1,0:T(8,128)(2,1)}, u32[]{:S(2)}) copy-start(bf16[128,2048]{1,0:T(8,128)(2,1)} %get-tuple-element.119) | copy-start | bytes 1572868
  652.8 6.7 %copy-start.2 = (bf16[320,768]{1,0:T(8,128)(2,1)S(1)}, bf16[320,768]{1,0:T(8,128)(2,1)}, u32[]{:S(2)}) copy-start(bf16[320,768]{1,0:T(8,128)(2,1)} %get-tuple-element.71.refs_0_) | copy-start | bytes 1474564

commit v3 on v2

--- a/solution.py
+++ b/solution.py
@@ -10,6 +10,7 @@
 
 MESH = pl.DeviceIdType.MESH
 SUM_VMEM = 60 * 1024 * 1024
+LAST_VMEM = 62 * 1024 * 1024
 HW = 1024
 CH = 16
 COPIES = 4
@@ -233,10 +234,17 @@
 
 
 def norm_back_into(grads, source, gain, add, target, gain_grad):
-    normed, inv_std = norm_rows(source[...])
-    grad = grads[...]
-    gain_grad[...] = jnp.sum(grad * normed, axis=0, keepdims=True)
-    target[...] = add[...] + norm_back(grad * gain, normed, inv_std)
+    gain_grad[...] = jnp.zeros_like(gain_grad)
+    height = 64 if source.shape[0] % 64 == 0 else 48
+
+    def body(i):
+        rows = at_step(i, height)
+        normed, inv_std = norm_rows(source[rows, :])
+        grad = grads[rows, :]
+        gain_grad[...] += jnp.broadcast_to(jnp.sum(grad * normed, axis=0, keepdims=True), gain_grad.shape)
+        target[rows, :] = add[rows, :] + norm_back(grad * gain, normed, inv_std)
+
+    loop(source.shape[0] // height, body)
 
 
 class Tiles:
@@ -1259,6 +1267,619 @@
     return slabs_found, found[:5], found[5:10], *found[10:]
 
 
+SIDE = 256
+BACK_TILE = 256
+
+
+class Chunk:
+    def __init__(self, parent, height, row, rows, col, cols, by_rows):
+        self.parent, self.height = parent, height
+        self.row, self.rows, self.col, self.cols, self.by_rows = row, rows, col, cols, by_rows
+        self.piece = (rows // 4, cols) if by_rows else (rows, cols // 4)
+        self.set_order(False, 0)
+
+    def set_order(self, z_first, first_bit):
+        self.z_first, self.first_bit = z_first, first_bit
+
+    def shard(self, shard):
+        return (pl.ds(aligned(shard * self.height + self.row, 16), self.rows), pl.ds(self.col, self.cols))
+
+    def out(self):
+        return (pl.ds(self.row, self.rows), pl.ds(self.col, self.cols))
+
+    def within(self, quarter):
+        rows, cols = self.piece
+        if self.by_rows:
+            return (pl.ds(aligned(quarter * rows, 16), rows), pl.ds(0, cols))
+        return (pl.ds(0, rows), pl.ds(aligned(quarter * cols, 128), cols))
+
+
+def cut(parent, slab, pieces):
+    for i in range(pieces):
+        if slab.by_rows:
+            cols = slab.cols // pieces
+            yield Chunk(parent, slab.rows, 0, slab.rows, i * cols, cols, True)
+        else:
+            rows = slab.rows // pieces
+            yield Chunk(parent, slab.rows, i * rows, rows, 0, slab.cols, False)
+
+
+class Summing:
+    STAGES, LAG, AHEAD = 6, 4, 2
+
+    def __init__(self, chunks, depth, grads, outs, buffers, sems):
+        self.chunks, self.depth, self.grads, self.outs = chunks, depth, grads, outs
+        self.held, self.from_first, self.from_second, self.from_level, self.result, self.stage = buffers
+        self.stage_sem, self.out_sem, self.core_pair, self.pair, self.z_pair = sems
+        self.group, self.level, self.core, self.flip = place(depth)
+        self.me = 2 * self.level + self.core
+        self.partner = (self.group, 2 * self.level + 1 - self.core)
+        self.z_peers = [(self.group, 2 * self.level_at(step) + self.core) for step in range(1, depth)]
+        self.peers = [(self.flip(0), self.me), (self.flip(1), self.me), self.partner, *self.z_peers]
+
+    def level_at(self, step):
+        return lax.rem(self.level + step + self.depth, self.depth)
+
+    def bit(self, b):
+        return (self.group // (1 << b)) % 2
+
+    def move(self, pair, k, kind, source, target, device):
+        return pltpu.make_async_remote_copy(
+            src_ref=source,
+            dst_ref=target,
+            send_sem=pair[0].at[kind, k],
+            recv_sem=pair[1].at[kind, k],
+            device_id=device,
+            device_id_type=MESH,
+        )
+
+    def quarter(self, k, first, second):
+        b = self.chunks[k].first_bit
+        return first * (1 << b) + second * (1 << (1 - b))
+
+    def core_move(self, k, lev):
+        chunk = self.chunks[k]
+        source = self.grads[chunk.parent].at[chunk.shard(2 * lev + 1 - self.core)]
+        return self.move(self.core_pair, k, lev, source, self.held[k].at[lev], self.partner)
+
+    def part(self, k, quarter):
+        chunk, held = self.chunks[k], self.held[k]
+        where = chunk.within(quarter)
+        return held.at[(self.level,) + where] if chunk.z_first else held.at[(slice(None),) + where]
+
+    def first_move(self, k, j):
+        b = self.chunks[k].first_bit
+        source = self.part(k, self.quarter(k, 1 - self.bit(b), j))
+        return self.move(self.pair, k, j, source, self.from_first[k].at[j], (self.flip(b), self.me))
+
+    def second_move(self, k):
+        b = self.chunks[k].first_bit
+        source = self.part(k, self.quarter(k, self.bit(b), 1 - self.bit(1 - b)))
+        return self.move(self.pair, k, 2, source, self.from_second[k], (self.flip(1 - b), self.me))
+
+    def level_move(self, k, step):
+        chunk, held = self.chunks[k], self.held[k]
+        lev = self.level_at(step)
+        source = held.at[lev] if chunk.z_first else held.at[(lev,) + chunk.within(self.group)]
+        target = self.from_level[k].at[step - 1]
+        return self.move(self.z_pair, k, step - 1, source, target, self.z_peers[step - 1])
+
+    def spread(self, k, kind, whose, b):
+        here = self.result[k].at[self.chunks[k].within(whose)]
+        return self.move(self.pair, k, kind, here, here, (self.flip(b), self.me))
+
+    def spread_second(self, k, whose):
+        return self.spread(k, 3, whose, 1 - self.chunks[k].first_bit)
+
+    def spread_first(self, k, j, whose):
+        return self.spread(k, 4 + j, whose, self.chunks[k].first_bit)
+
+    def out_copy(self, k):
+        chunk = self.chunks[k]
+        target = self.outs[chunk.parent].at[chunk.out()]
+        return pltpu.make_async_copy(self.result[k], target, self.out_sem.at[k])
+
+    def stage_copy(self, k, lev):
+        chunk = self.chunks[k]
+        source = self.grads[chunk.parent].at[chunk.shard(2 * lev + self.core)]
+        slot = self.stage[(chunk.rows, chunk.cols)].at[lev % 2]
+        return pltpu.make_async_copy(source, slot, self.stage_sem.at[k, lev % 2])
+
+    def rows_loop(self, height, body):
+        step = 32 if height % 32 == 0 else 16
+        loop(height // step + self.level // self.depth, lambda i: body(at_step(i, step)))
+
+    def add_core(self, k):
+        chunk, held = self.chunks[k], self.held[k]
+        stage = self.stage[(chunk.rows, chunk.cols)]
+        self.stage_copy(k, 0).start()
+        for lev in range(self.depth):
+            if lev + 1 < self.depth:
+                self.stage_copy(k, lev + 1).start()
+            self.core_move(k, lev).wait_recv()
+            self.stage_copy(k, lev).wait()
+
+            def body(rows):
+                total = held[lev, rows, :].astype(jnp.float32) + stage[lev % 2, rows, :].astype(jnp.float32)
+                held[lev, rows, :] = total.astype(jnp.bfloat16)
+
+            self.rows_loop(chunk.rows, body)
+
+    def levels_of(self, k):
+        return [self.level] if self.chunks[k].z_first else list(range(self.depth))
+
+    def shifted(self, rows, by):
+        return pl.ds(aligned(rows.start + by, 16), rows.size)
+
+    def add_first(self, k):
+        chunk, slot = self.chunks[k], k
+        held, arrived = self.held[slot], self.from_first[slot]
+        for j in range(2):
+            self.first_move(k, j).wait_recv()
+            top, cols = chunk.within(self.quarter(k, self.bit(chunk.first_bit), j))
+            for lev in self.levels_of(k):
+
+                def body(rows):
+                    at = (lev, self.shifted(rows, top.start), cols)
+                    extra = arrived[j, rows, :] if chunk.z_first else arrived[j, lev, rows, :]
+                    held[at] = (held[at].astype(jnp.float32) + extra.astype(jnp.float32)).astype(jnp.bfloat16)
+
+                self.rows_loop(chunk.piece[0], body)
+
+    def add_second(self, k):
+        chunk, slot = self.chunks[k], k
+        held, arrived, result = self.held[slot], self.from_second[slot], self.result[slot]
+        self.second_move(k).wait_recv()
+        top, cols = chunk.within(self.group)
+        for lev in self.levels_of(k):
+
+            def body(rows):
+                at = (lev, self.shifted(rows, top.start), cols)
+                extra = arrived[rows, :] if chunk.z_first else arrived[lev, rows, :]
+                total = (held[at].astype(jnp.float32) + extra.astype(jnp.float32)).astype(jnp.bfloat16)
+                if chunk.z_first:
+                    result[at[1:]] = total
+                else:
+                    held[at] = total
+
+            self.rows_loop(chunk.piece[0], body)
+
+    def add_level(self, k):
+        chunk, slot = self.chunks[k], k
+        held, arrived, result = self.held[slot], self.from_level[slot], self.result[slot]
+        for step in range(1, self.depth):
+            self.level_move(k, step).wait_recv()
+        top, cols = (pl.ds(0, chunk.rows), pl.ds(0, chunk.cols)) if chunk.z_first else chunk.within(self.group)
+
+        def body(rows):
+            at = (self.shifted(rows, top.start), cols)
+            total = held[(self.level,) + at].astype(jnp.float32)
+            for step in range(self.depth - 1):
+                total = total + arrived[step, rows, :].astype(jnp.float32)
+            if chunk.z_first:
+                held[(self.level,) + at] = total.astype(jnp.bfloat16)
+            else:
+                result[at] = total.astype(jnp.bfloat16)
+
+        self.rows_loop(top.size, body)
+
+    def begin_core(self, k):
+        for lev in range(self.depth):
+            self.core_move(k, lev).start()
+
+    def begin_first(self, k):
+        self.first_move(k, 0).start()
+        self.first_move(k, 1).start()
+
+    def begin_level(self, k):
+        for step in range(1, self.depth):
+            self.level_move(k, step).start()
+
+    def begin_spread(self, k):
+        self.spread_second(k, self.group).start()
+
+    def end_spread_second(self, k):
+        other = self.flip(1 - self.chunks[k].first_bit)
+        self.spread_second(k, other).wait_recv()
+        self.spread_first(k, 0, self.group).start()
+        self.spread_first(k, 1, other).start()
+
+    def end_spread_first(self, k):
+        self.spread_first(k, 0, self.flip(self.chunks[k].first_bit)).wait_recv()
+        self.spread_first(k, 1, 3 - self.group).wait_recv()
+        self.out_copy(k).start()
+
+    def stages(self, k):
+        if self.chunks[k].z_first:
+            return [
+                lambda: (self.add_core(k), self.begin_level(k)),
+                lambda: (self.add_level(k), self.begin_first(k)),
+                lambda: (self.add_first(k), self.second_move(k).start()),
+                lambda: (self.add_second(k), self.begin_spread(k)),
+                lambda: self.end_spread_second(k),
+                lambda: self.end_spread_first(k),
+            ]
+        return [
+            lambda: (self.add_core(k), self.begin_first(k)),
+            lambda: (self.add_first(k), self.second_move(k).start()),
+            lambda: (self.add_second(k), self.begin_level(k)),
+            lambda: (self.add_level(k), self.begin_spread(k)),
+            lambda: self.end_spread_second(k),
+            lambda: self.end_spread_first(k),
+        ]
+
+    def settle(self, k):
+        for lev in range(self.depth):
+            self.core_move(k, lev).wait_send()
+        self.first_move(k, 0).wait_send()
+        self.first_move(k, 1).wait_send()
+        self.second_move(k).wait_send()
+        for step in range(1, self.depth):
+            self.level_move(k, step).wait_send()
+        self.spread_second(k, self.group).wait_send()
+        self.spread_first(k, 0, self.group).wait_send()
+        self.spread_first(k, 1, self.flip(1 - self.chunks[k].first_bit)).wait_send()
+        self.out_copy(k).wait()
+
+    def run(self, ready, beside):
+        count = len(self.chunks)
+        greet(self.peers)
+        plans = [self.stages(k) for k in range(count)]
+        for turn in range(-self.AHEAD, count + self.LAG * (self.STAGES - 1)):
+            if turn + self.AHEAD < count:
+                ready(turn + self.AHEAD)
+                self.begin_core(turn + self.AHEAD)
+            for stage in range(self.STAGES):
+                if 0 <= turn - self.LAG * stage < count:
+                    plans[turn - self.LAG * stage][stage]()
+                beside()
+        for k in range(count):
+            self.settle(k)
+
+
+class Saved:
+    def __init__(self, kept, buffers, sems):
+        rows = kept[0].shape[0]
+        part = pl.ds(0, rows)
+        self.wide, self.qkv, self.mixed = (b if b.shape[0] == rows else b.at[part] for b in buffers)
+        places = (self.wide, self.qkv, self.mixed, self.wide)
+        self.copies = [pltpu.make_async_copy(a, b, sems.at[i]) for i, (a, b) in enumerate(zip(kept, places, strict=True))]
+
+    def start(self, which):
+        self.copies[("x", "qkv", "mixed", "middle").index(which)].start()
+
+    def wait(self, which):
+        self.copies[("x", "qkv", "mixed", "middle").index(which)].wait()
+
+
+class Stream:
+    def __init__(self, sources, slots, sems):
+        self.sources, self.slots, self.sems, self.used = sources, slots, sems, 0
+        self.copy(0).start()
+
+    def slot(self, i):
+        height, slot = self.sources[i].shape[0], self.slots.at[i % 2]
+        return slot if height == slot.shape[0] else slot.at[pl.ds(0, height)]
+
+    def copy(self, i):
+        return pltpu.make_async_copy(self.sources[i], self.slot(i), self.sems.at[i % 2])
+
+    def next(self):
+        i = self.used
+        self.copy(i).wait()
+        if i + 1 < len(self.sources):
+            self.copy(i + 1).start()
+        self.used += 1
+        return self.slot(i)
+
+
+def backward_steps(width, grad, gain_one, gain_two, saved, following, streams, d_a, d_up, d_down, d_one, d_two,
+                   grad_low, low, grad_qkv, acc, grad_mid, out, tiles, live, reach, names):
+    wide, narrow, square = tiles
+    downs, ups, raiseds, heads = streams
+    inner, side = d_up.shape[1], SIDE
+    qkv, mixed, middle, stream = saved.qkv, saved.mixed, saved.wide, saved.wide
+
+    def begin():
+        saved.wait("middle")
+        grad_low[...] = grad[...].astype(jnp.bfloat16)
+        scale_norm(middle, gain_two, low)
+        acc[...] = jnp.zeros_like(acc)
+
+    yield begin
+    def feed_down(j):
+        raised, down = raiseds.next()[...], downs.next()
+        cumul = 0.5 + 0.5 * lax.erf(raised * ROOT_HALF)
+        slope = cumul + raised * (jnp.exp(-0.5 * raised * raised) * (1.0 / math.sqrt(2.0 * math.pi)))
+        grad_qkv[:, :BACK_TILE] = (raised * cumul).astype(jnp.bfloat16)
+        narrow.put(j, rows_dot(grad_qkv[:, :BACK_TILE], grad_low[...]), d_down.at[pl.ds(j * BACK_TILE, BACK_TILE), :])
+        grad_qkv[:, BACK_TILE : 2 * BACK_TILE] = (right_trans(grad_low[...], down[...]) * slope).astype(jnp.bfloat16)
+
+    def feed_up(j):
+        wide.put(j, rows_dot(low[...], grad_qkv[:, BACK_TILE : 2 * BACK_TILE]), d_up.at[:, pl.ds(j * BACK_TILE, BACK_TILE)])
+        acc[...] += right_trans(grad_qkv[:, BACK_TILE : 2 * BACK_TILE], ups.next()[...])
+
+    for j in range(inner // BACK_TILE):
+        yield functools.partial(feed_down, j)
+        yield functools.partial(feed_up, j)
+
+    def middle_back():
+        narrow.flush(d_down.at[pl.ds(0, BACK_TILE), :])
+        wide.flush(d_up.at[:, pl.ds(0, BACK_TILE)])
+        reach(names[0])
+        norm_back_into(acc, middle, gain_two, grad, grad_mid, d_two)
+        saved.start("x")
+        grad_low[...] = grad_mid[...].astype(jnp.bfloat16)
+        saved.wait("mixed")
+
+    yield middle_back
+
+    def project_back(j):
+        cols = pl.ds(j * side, side)
+        square.put(j, rows_dot(mixed[...], grad_low[:, cols]), d_a.at[:, pl.ds(3 * width + j * side, side)])
+        added = right_trans(grad_low[:, cols], heads.next()[...])
+        acc[...] = added if j == 0 else acc[...] + added
+
+    for j in range(width // side):
+        yield functools.partial(project_back, j)
+
+    def mixed_back():
+        if following:
+            following.start("mixed")
+        low[...] = acc[...].astype(jnp.bfloat16)
+        saved.wait("qkv")
+
+    yield mixed_back
+
+    def attend(pair):
+        where = [pl.ds(pair * 128 + part * width, 128) for part in range(3)]
+        query, key, value = (qkv[:, at] for at in where)
+        grad_mixed = low[:, pl.ds(pair * 128, 128)]
+        found = []
+        for half in range(2):
+            probs = probabilities(query, key, half, live)
+            grad_half = keep_half(grad_mixed, half)
+            grad_probs = right_trans(grad_half, value)
+            dots = jnp.sum(grad_probs * probs, axis=-1, keepdims=True)
+            grad_scores = (probs * (grad_probs - dots) * 0.125).astype(jnp.bfloat16)
+            found.append(
+                (matmul(grad_scores, key), rows_dot(grad_scores, query), rows_dot(probs.astype(jnp.bfloat16), grad_half))
+            )
+        for part in range(3):
+            both = jnp.where(head_mask(0), found[0][part], found[1][part])
+            grad_qkv[:, where[part]] = both.astype(jnp.bfloat16)
+
+    for pair in range(width // 128):
+        yield functools.partial(attend, pair)
+
+    def normed():
+        if following:
+            following.start("qkv")
+        saved.wait("x")
+        scale_norm(stream, gain_one, low)
+
+    yield normed
+
+    def project(j):
+        piece = grad_qkv[:, pl.ds(j * side, side)]
+        square.put(j + width // side, rows_dot(low[...], piece), d_a.at[:, pl.ds(j * side, side)])
+        added = right_trans(piece, heads.next()[...])
+        acc[...] = added if j == 0 else acc[...] + added
+
+    for j in range(3 * width // side):
+        yield functools.partial(project, j)
+
+    def end():
+        square.flush(d_a.at[:, pl.ds(0, side)])
+        reach(names[1])
+        norm_back_into(acc, stream, gain_one, grad_mid, out, d_one)
+        if following:
+            following.start("middle")
+
+    yield end
+
+
+def last_kernel(chunks, stage_keys, depth, *refs):
+    head_grads, refs = refs[:3], refs[3:]
+    head_small, refs = refs[:2], refs[2:]
+    (grad_rows, vis_col, vis_row, vec), e_kept, d_kept, refs = refs[:4], refs[4:8], refs[8:12], refs[12:]
+    (e_up, d_up, e_a, e_u, e_d, d_a, d_u, d_d), refs = refs[:8], refs[8:]
+    outs, refs = refs[:10], refs[10:]
+    embed_grad, small_grad, refs = refs[0], refs[1], refs[2:]
+    block_grads, refs = refs[:6], refs[6:]
+    (small, small_pack, d_grad, e_grad, low_a, low_b, grad_qkv, acc, grad_mid), refs = refs[:9], refs[9:]
+    saved_buffers, saved_sems, refs = refs[:3], refs[3], refs[4:]
+    (wide, narrow, square, down_slots, up_slots, raised_slots, head_slots, tile_sems, load_sems, pack_sem), refs = refs[:10], refs[10:]
+    count = len(chunks)
+    buffers = [refs[i * count : (i + 1) * count] for i in range(5)]
+    refs = refs[5 * count :]
+    stage, refs = dict(zip(stage_keys, refs[: len(stage_keys)], strict=True)), refs[len(stage_keys) :]
+    stage_sem, out_sem, core_sent, core_got, sent, got, z_sent, z_got = refs
+    sems = (stage_sem, out_sem, (core_sent, core_got), (sent, got), (z_sent, z_got))
+    tokens, width = d_kept[0].shape
+    rows = e_kept[0].shape[0]
+    parts = 2 * depth
+    d_saved = Saved(d_kept, saved_buffers, saved_sems.at[0])
+    e_saved = Saved(e_kept, saved_buffers, saved_sems.at[1])
+    de_a, de_u, de_d, dd_a, dd_u, dd_d = block_grads
+    grads = (small_grad, *block_grads, *head_grads)
+    summing = Summing(chunks, depth, grads, outs, (*buffers, stage), sems)
+    tiles = (Tiles(wide, tile_sems.at[0]), Tiles(narrow, tile_sems.at[1]), Tiles(square, tile_sems.at[2]))
+    reached = {"head"}
+    embed_copy = pltpu.make_async_copy(d_grad, embed_grad, pack_sem.at[1])
+
+    def streams(inner, w_a, w_u, w_d, up):
+        tile = [pl.ds(j * BACK_TILE, BACK_TILE) for j in range(inner // BACK_TILE)]
+        past = width // SIDE
+        sides = [pl.ds((j + 3 * past) % (4 * past) * SIDE, SIDE) for j in range(4 * past)]
+        return (
+            Stream([w_d.at[t, :] for t in tile], down_slots, load_sems.at[0]),
+            Stream([w_u.at[:, t] for t in tile], up_slots, load_sems.at[1]),
+            Stream([up.at[:, t] for t in tile], raised_slots, load_sems.at[2]),
+            Stream([w_a.at[:, t] for t in sides], head_slots, load_sems.at[3]),
+        )
+
+    def work():
+        inner = d_u.shape[1]
+        ready_streams = []
+
+        def begin():
+            for which in ("middle", "mixed", "qkv"):
+                d_saved.start(which)
+            ready_streams.append(streams(inner, d_a, d_u, d_d, d_up))
+            d_grad[:BUFFER, :] = jnp.zeros((BUFFER, width), jnp.float32)
+            d_grad[BUFFER:, :] = grad_rows[...].astype(jnp.float32)
+
+        yield begin
+        yield from lazy_steps(lambda: backward_steps(
+            width, d_grad, vec[2:3, :], vec[3:4, :], d_saved, e_saved, ready_streams[0], dd_a, dd_u, dd_d,
+            small.at[2], small.at[3], low_a, low_b, grad_qkv, acc, grad_mid, d_grad, tiles, None, reached.add, ("dec feed", "dec")))
+
+        def between():
+            ready_streams.append(streams(inner, e_a, e_u, e_d, e_up))
+            hot = spot_hot(vis_row, tokens - BUFFER)
+            masked = 1.0 - jnp.sum(hot.astype(jnp.float32), axis=1, keepdims=True)
+            small[4] = jnp.broadcast_to(jnp.sum(d_grad[BUFFER:, :] * masked, axis=0, keepdims=True), (8, width))
+            e_grad[:BUFFER, :] = d_grad[:BUFFER, :]
+            e_grad[BUFFER:, :] = exact_dot(token_hot(vis_col, tokens - BUFFER), d_grad[BUFFER:, :])
+
+        yield between
+        part = pl.ds(0, rows)
+        yield from lazy_steps(lambda: backward_steps(
+            width, e_grad, vec[0:1, :], vec[1:2, :], e_saved, None, ready_streams[1], de_a, de_u, de_d,
+            small.at[0], small.at[1], low_a.at[part], low_b.at[part], grad_qkv.at[part], acc.at[part],
+            grad_mid.at[part], e_grad, tiles, live_keys(vis_row), reached.add, ("enc feed", "enc")))
+
+        def end():
+            d_grad[:BUFFER, :] = e_grad[:BUFFER, :]
+            d_grad[BUFFER:, :] = exact_dot(spot_hot(vis_row, tokens - BUFFER), e_grad[BUFFER:, :])
+            embed_copy.start()
+            pack_gradients(small, head_small, parts, small_pack)
+            copy = pltpu.make_async_copy(small_pack, small_grad, pack_sem.at[0])
+            copy.start()
+            copy.wait()
+            reached.add("all")
+
+        yield end
+
+    steps = work()
+    needs = ["all", "enc", "enc feed", "enc feed", "dec", "dec feed", "dec feed", "head", "head", "head"]
+
+    def beside():
+        step = next(steps, None)
+        if step is not None:
+            step()
+
+    def ready(k):
+        while needs[chunks[k].parent] not in reached:
+            beside()
+
+    summing.run(ready, beside)
+    embed_copy.wait()
+
+
+def lazy_steps(make):
+    yield from make()
+
+
+def pack_gradients(small, head_small, parts, target):
+    count, _, width = small.shape
+    piece = width // parts
+    target[...] = jnp.zeros_like(target)
+    lane = lax.broadcasted_iota(jnp.int32, (width, 128), 1)
+    row = lax.broadcasted_iota(jnp.int32, (width, 128), 0)
+    which = lax.broadcasted_iota(jnp.int32, (CH, width), 0)
+    rows = jnp.zeros((CH, width), jnp.float32)
+    for i in range(count):
+        rows = jnp.where(which == i, jnp.concatenate([small[i], small[i]], axis=0), rows)
+    low = rows.astype(jnp.bfloat16)
+    for part in range(parts):
+        block = pl.ds(part * SMALL_ROWS, CH)
+        pick = ((row == lane + part * piece) & (lane < piece)).astype(jnp.bfloat16)
+        target[block, :128] = matmul(low, pick).astype(jnp.bfloat16)
+        for i in range(2):
+            target[block, pl.ds(128 * (i + 1), 128)] = head_small[i][:, pl.ds(part * 128, 128)].astype(jnp.bfloat16)
+
+
+def last_part(slabs, chunks, depth, head_grads, head_small, grad_rows, vis_col, vis_row, vec, enc_kept, dec_kept, weights):
+    tokens, width = dec_kept[0].shape
+    rows = enc_kept[0].shape[0]
+    parts = 2 * depth
+    f32, half = jnp.float32, jnp.bfloat16
+    whole, anywhere = pl.BlockSpec(memory_space=pltpu.VMEM), pl.BlockSpec(memory_space=pl.ANY)
+    shape, dma = jax.ShapeDtypeStruct, pltpu.SemaphoreType.DMA
+    stage_keys = sorted({(c.rows, c.cols) for c in chunks})
+    held, first, second, lev, result = [], [], [], [], []
+    for chunk in chunks:
+        part = (chunk.rows, chunk.cols)
+        held.append(pltpu.VMEM((depth,) + part, half))
+        result.append(pltpu.VMEM(part, half))
+        if chunk.z_first:
+            first.append(pltpu.VMEM((2,) + chunk.piece, half))
+            second.append(pltpu.VMEM(chunk.piece, half))
+            lev.append(pltpu.VMEM((depth - 1,) + part, half))
+        else:
+            first.append(pltpu.VMEM((2, depth) + chunk.piece, half))
+            second.append(pltpu.VMEM((depth,) + chunk.piece, half))
+            lev.append(pltpu.VMEM((depth - 1,) + chunk.piece, half))
+    count = len(chunks)
+    outs = [shape((s.rows, s.cols), half) for s in slabs]
+    outs += [shape((tokens, width), f32), shape((parts * SMALL_ROWS, SMALL_COLS), half)]
+    outs += [shape(w.shape, half) for w in weights]
+    e_up, d_up = enc_kept[4], dec_kept[4]
+    vmem = pltpu.VMEM
+    found = pl.pallas_call(
+        functools.partial(last_kernel, chunks, stage_keys, depth),
+        out_shape=outs,
+        in_specs=[anywhere] * 3 + [whole] * 6 + [anywhere] * 16,
+        out_specs=[anywhere] * (len(slabs) + 8),
+        scratch_shapes=[
+            vmem((5, 8, width), f32),
+            vmem((parts * SMALL_ROWS, SMALL_COLS), half),
+            vmem((tokens, width), f32),
+            vmem((rows, width), f32),
+            vmem((tokens, width), half),
+            vmem((tokens, width), half),
+            vmem((tokens, 3 * width), half),
+            vmem((tokens, width), f32),
+            vmem((tokens, width), f32),
+            vmem((tokens, width), f32),
+            vmem((tokens, 3 * width), half),
+            vmem((tokens, width), half),
+            dma((2, 4)),
+            vmem((2, width, BACK_TILE), half),
+            vmem((2, BACK_TILE, width), half),
+            vmem((2, width, SIDE), half),
+            vmem((2, BACK_TILE, width), half),
+            vmem((2, width, BACK_TILE), half),
+            vmem((2, tokens, BACK_TILE), f32),
+            vmem((2, width, SIDE), half),
+            dma((3, 2)),
+            dma((4, 2)),
+            dma((2,)),
+        ]
+        + held
+        + first
+        + second
+        + lev
+        + result
+        + [vmem((2,) + key, half) for key in stage_keys]
+        + [
+            dma((count, 2)),
+            dma((count,)),
+            dma((depth, count)),
+            dma((depth, count)),
+            dma((6, count)),
+            dma((6, count)),
+            dma((depth - 1, count)),
+            dma((depth - 1, count)),
+        ],
+        compiler_params=pltpu.CompilerParams(collective_id=1, has_side_effects=True, vmem_limit_bytes=LAST_VMEM),
+        name="backward_and_sum",
+    )(*head_grads, *head_small, grad_rows, vis_col, vis_row, vec, *enc_kept[:4], *dec_kept[:4], e_up, d_up, *weights)
+    return found[len(slabs)], found[: len(slabs)]
+
+
 SMALL_ROWS, SMALL_COLS = 32, 512
 
 
@@ -1294,6 +1915,16 @@
 )
 
 
+def chunks_of():
+    plan = [(8, 4, ()), (9, 2, ()), (7, 1, ()), (6, 3, (0, 2)), (5, 3, ()), (4, 3, ()), (3, 3, (0, 2)), (2, 3, ()), (1, 3, ()), (0, 1, ())]
+    found = []
+    for parent, pieces, z_first in plan:
+        for i, chunk in enumerate(cut(parent, SLABS[parent], pieces)):
+            chunk.set_order(i in z_first, len(found) % 2)
+            found.append(chunk)
+    return found
+
+
 def by_links():
     return lax.axis_size("dev") == 8 and lax.axis_size("grp") == 4
 
@@ -1315,24 +1946,14 @@
 
 
 def sum_gradients(slabs, vectors, d_in, d_out):
-    if by_links():
-        packed = (pack_small(list(vectors), d_in, d_out).astype(jnp.bfloat16), *slabs)
-        turn = (8, 9, 7, 4, 5, 6, 1, 2, 3, 0)
-        orders = ("xy", "yx", "zx", "xy", "yx", "zx", "yx", "xy", "yx", "xy")
-        sums = sum_slabs([packed[t] for t in turn], [SLABS[t] for t in turn], [orders[t] for t in turn], lax.axis_size("dev") // 2)
-        back = [None] * len(turn)
-        for t, s in zip(turn, sums, strict=True):
-            back[t] = s
-        small, *slabs = back
-        vectors, d_in, d_out = unpack_small(small)
-    else:
-
-        def scatter(grad, axis=0):
-            part = lax.psum_scatter(grad.astype(jnp.float32), "dev", scatter_dimension=axis, tiled=True)
-            return lax.psum(part.astype(jnp.bfloat16), "grp")
-
-        slabs = [scatter(g) for g in slabs]
-        vectors, d_in, d_out = scatter(vectors, 1), scatter(d_in, 1), scatter(d_out, 1)
+    def scatter(grad, axis=0):
+        part = lax.psum_scatter(grad.astype(jnp.float32), "dev", scatter_dimension=axis, tiled=True)
+        return lax.psum(part.astype(jnp.bfloat16), "grp")
+
+    return unpack_gradients([scatter(g) for g in slabs], scatter(vectors, 1), scatter(d_in, 1), scatter(d_out, 1))
+
+
+def unpack_gradients(slabs, vectors, d_in, d_out):
     ea, eu, ed, da, du, dd, hc, ha, hio = (s.astype(jnp.float32) for s in slabs)
     vectors, d_in, d_out = (s.astype(jnp.float32) for s in (vectors, d_in, d_out))
     split = 3 * ed.shape[1]
@@ -1368,13 +1989,24 @@
         grad_rows, loss, d_in, d_out, *head_grads = head_pass(
             acts, vis_row, targets[image], noise, steps, embeds, *slabs[6:], w_in, w_out
         )
-        embed_grad, small, block_grads = backward_blocks(grad_rows, vis_col, vis_row, vec, enc_kept, dec_kept, slabs[:6])
-        found = ([*block_grads, *head_grads], small[:5], d_in, d_out)
-        totals = found if totals is None else jax.tree.map(jnp.add, totals, found)
+        if linked:
+            embed_grad, sums = last_part(
+                SLABS, chunks_of(), lax.axis_size("dev") // 2, head_grads, (d_in, d_out), grad_rows, vis_col, vis_row, vec,
+                enc_kept, dec_kept, slabs[:6],
+            )
+        else:
+            embed_grad, small, block_grads = backward_blocks(grad_rows, vis_col, vis_row, vec, enc_kept, dec_kept, slabs[:6])
+            found = ([*block_grads, *head_grads], small[:5], d_in, d_out)
+            totals = found if totals is None else jax.tree.map(jnp.add, totals, found)
         losses.append(loss[0, 0] / (counts[image].astype(jnp.float32) * (COPIES * CH)))
         acts_of.append(acts)
         embed_grads.append(embed_grad)
-    return (jnp.stack(losses), jnp.stack(acts_of), jnp.stack(embed_grads), *sum_gradients(*totals))
+    if linked:
+        small, *large = sums
+        shares = unpack_gradients(large, *unpack_small(small))
+    else:
+        shares = sum_gradients(*totals)
+    return (jnp.stack(losses), jnp.stack(acts_of), jnp.stack(embed_grads), *shares)
 
 
 def solution(mesh):

time: 671 us -> 554 us (0.83)
  Pallas kernels: 625 us -> 507 us
    pallas_call x2 -> x1, Pallas kernels: 369 us -> 259 us  [last_part(): pl.pallas_call(functools.partial(last_kernel, chunks, stage_keys, depth),...]
    pallas_call x1, Pallas kernels: 183 us -> 175 us  [first_part(): pl.pallas_call(functools.partial(first_kernel, slabs, depth), out_shape=o...]
where the time goes in v3:
time: 554 us; the launch traced here: 543 us
  Pallas kernels  507 us (92%)
  local copies, waits for them, and re-layouts  16.7 us (3%)
  other arithmetic  15.2 us (3%)
    pallas_call x1, Pallas kernels, last_part(): pl.pallas_call(functools.partial(last_kernel, chunks, stage_keys, depth),...  259 us
    pallas_call x1, Pallas kernels, first_part(): pl.pallas_call(functools.partial(first_kernel, slabs, depth), out_shape=o...  175 us
    pallas_call x1, Pallas kernels, head_pass(): pl.pallas_call(head_kernel, out_shape=outs, in_specs=[whole] * 6 + [anywh...  73.3 us

profile of v3, /device:TPU:24, one launch (start us, length us, event | category | flops | bytes accessed | tf_op | source)
XLA Modules:
  0.0 542.9 jit_solution(4329113838667879340)
XLA Ops:
  0.7 0.7 stack.12
  1.4 0.7 fusion.2
  2.1 0.6 pad_bitcast_fusion.refs_0_
  2.7 2.4 pad_maximum_fusion
  5.1 1.9 pad_maximum_fusion.2.refs_9_
  7.7 1.3 fusion.4
  9.0 0.7 copy.51.refs_11_.refs_6_
  9.7 0.7 copy.57
  10.4 1.0 copy.58
  11.5 0.6 multiply_exponential_fusion.refs_14_
  12.1 175.2 %gather_and_forward.1 = (bf16[256,512]{1,0:T(8,128)(2,1)}, bf16[768,3072]{1,0:T(8,128)(2,1)}, bf16[768,3072]{1,0:T(8,128)(2,1)}, bf16[3072,768]{1,0:T(8,128)(2,1...) custom-call(bf16[32,512]{1,0:T(8,128)(2,1)} %pad_bitcast_fusion.refs, ...), custom_call_target="tpu_custom_call" | custom-call | tf_op jit(solution)/shard_map/gather_and_forward/pallas_call | solution.py:1247
  187.3 0.8 copy.53
  188.1 0.8 copy.54
  188.9 73.3 %head_pass.1 = (bf16[256,768]{1,0:T(8,128)(2,1)}, f32[8,128]{1,0:T(8,128)}, f32[16,1024]{1,0:T(8,128)}, f32[16,1024]{1,0:T(8,128)}, bf16[768,1024]{1,0:T(8,128)(...) custom-call(bf16[320,768]{1,0:T(8,128)(2,1)} %get-tuple-element.64.refs_0_, ...), custom_call_target="tpu_custom_call" | custom-call | tf_op jit(solution)/shard_map/head_pass/pallas_call | solution.py:579
  262.2 1.2 slice.50
  264.1 258.7 %backward_and_sum.1 = (bf16[32,512]{1,0:T(8,128)(2,1)}, bf16[96,3072]{1,0:T(8,128)(2,1)}, bf16[96,3072]{1,0:T(8,128)(2,1)}, bf16[384,768]{1,0:T(8,128)(2,1)}, bf...) custom-call(bf16[768,1024]{1,0:T(8,128)(2,1)} %get-tuple-element.72., ...), custom_call_target="tpu_custom_call" | custom-call | tf_op jit(solution)/shard_map/backward_and_sum/pallas_call | solution.py:1831
  522.9 0.8 slice_convert_fusion
  523.7 0.5 slice_bitcast_fusion.2
  524.2 2.0 slice.66
  526.2 1.7 slice.67
  527.9 2.2 convert_element_type.51
  530.1 1.1 convert_element_type.52
  531.2 1.0 slice.68
  532.1 0.7 slice.69
  532.9 1.1 convert_element_type.54
  534.0 1.1 convert_element_type.55
  535.1 1.3 convert_bitcast_fusion
  536.4 0.8 convert_element_type.58
  537.2 1.3 convert_element_type.59
  538.5 1.1 fusion.6
  539.6 0.8 copy.62
  540.3 0.9 copy.63
  (22 shorter events, 0.0 us)
Async XLA Ops:
  5.1 182.2 %copy-start.10 = (f32[1,256,16]{1,2,0:T(8,128)S(1)}, f32[1,256,16]{1,2,0:T(8,128)}, u32[]{:S(2)}) copy-start(f32[1,256,16]{1,2,0:T(8,128)} %param.28) | copy-start | bytes 49156
  5.1 182.9 %copy-start.9 = (bf16[1,256,4,16]{1,3,2,0:T(8,128)(2,1)S(1)}, bf16[1,256,4,16]{1,3,2,0:T(8,128)(2,1)}, u32[]{:S(2)}) copy-start(bf16[1,256,4,16]{1,3,2,0:T(8,128)(2,1)} %param.29) | copy-start | bytes 98308
  522.8 7.2 %copy-start.7 = (bf16[384,768]{1,0:T(8,128)(2,1)S(1)}, bf16[384,768]{1,0:T(8,128)(2,1)}, u32[]{:S(2)}) copy-start(bf16[384,768]{1,0:T(8,128)(2,1)} %get-tuple-element.99) | copy-start | bytes 1769476
  522.9 8.3 %copy-start = (bf16[96,3072]{1,0:T(8,128)(2,1)S(1)}, bf16[96,3072]{1,0:T(8,128)(2,1)}, u32[]{:S(2)}) copy-start(bf16[96,3072]{1,0:T(8,128)(2,1)} %get-tuple-element.100) | copy-start | bytes 1769476
  522.9 10.0 %copy-start.6 = (bf16[96,3072]{1,0:T(8,128)(2,1)S(1)}, bf16[96,3072]{1,0:T(8,128)(2,1)}, u32[]{:S(2)}) copy-start(bf16[96,3072]{1,0:T(8,128)(2,1)} %get-tuple-element.101) | copy-start | bytes 1769476
  526.2 7.8 %copy-start.5 = (bf16[384,768]{1,0:T(8,128)(2,1)S(1)}, bf16[384,768]{1,0:T(8,128)(2,1)}, u32[]{:S(2)}) copy-start(bf16[384,768]{1,0:T(8,128)(2,1)} %get-tuple-element.102) | copy-start | bytes 1769476
  530.1 6.3 %copy-start.8 = (bf16[96,1024]{1,0:T(8,128)(2,1)S(1)}, bf16[96,1024]{1,0:T(8,128)(2,1)}, u32[]{:S(2)}) copy-start(bf16[96,1024]{1,0:T(8,128)(2,1)} %get-tuple-element.103) | copy-start | bytes 589828
  530.1 7.1 %copy-start.4 = (bf16[128,3072]{1,0:T(8,128)(2,1)S(1)}, bf16[128,3072]{1,0:T(8,128)(2,1)}, u32[]{:S(2)}) copy-start(bf16[128,3072]{1,0:T(8,128)(2,1)} %get-tuple-element.104) | copy-start | bytes 2359300
  531.2 7.3 %copy-start.1 = (bf16[128,2048]{1,0:T(8,128)(2,1)S(1)}, bf16[128,2048]{1,0:T(8,128)(2,1)}, u32[]{:S(2)}) copy-start(bf16[128,2048]{1,0:T(8,128)(2,1)} %get-tuple-element.105) | copy-start | bytes 1572868
  532.9 6.7 %copy-start.2 = (bf16[320,768]{1,0:T(8,128)(2,1)S(1)}, bf16[320,768]{1,0:T(8,128)(2,1)}, u32[]{:S(2)}) copy-start(bf16[320,768]{1,0:T(8,128)(2,1)} %get-tuple-element.64.refs_0_) | copy-start | bytes 1474564
  534.0 6.3 %copy-start.3 = (f32[320,768]{1,0:T(8,128)S(1)}, f32[320,768]{1,0:T(8,128)}, u32[]{:S(2)}) copy-start(f32[320,768]{1,0:T(8,128)} %get-tuple-element.95) | copy-start | bytes 2949124
